TPU v7x, 128 devices: a whole 4x4x4 slice. The times are simulated.
128 devices in a mesh: seq: 4 (over z), tensor: 2 (over y_lo), fsdp: 16 (over x, y_hi, core).
Axes of the slice: x: 4, y: 4 (y_hi: 2, y_lo: 2; y = y_hi * 2 + y_lo), z: 4, core: 2. Of those that a mesh axis runs over, the one named last changes fastest.
Arguments:
- tokens: bfloat16 [16, 2048, 1536], P('fsdp', 'seq'), may hold values from -6 to 6
- output_gradient: bfloat16 [16, 2048, 1536], P('fsdp', 'seq'), may hold values from -6 to 6
- document_length_table: int32 [16, 4], P('fsdp'), may hold values from 1 to 1792, 2048 in all within a row
- sequence_adapter_index: int32 [16], P('fsdp'), may hold values from 0 to 7
- sequence_window_length: int32 [16], P('fsdp'), may hold values from 512 to 1024, as said below
- attention_norm_gain: float32 [1536], replicated, may hold values from 0.25 to 1.75
- feedforward_norm_gain: float32 [1536], replicated, may hold values from 0.25 to 1.75
- query_projection_weight: bfloat16 [1536, 1536], P('fsdp', 'tensor'), may hold values from -0.15625 to 0.15625
- key_projection_weight: bfloat16 [1536, 512], P('fsdp', 'tensor'), may hold values from -0.15625 to 0.15625
- value_projection_weight: bfloat16 [1536, 512], P('fsdp', 'tensor'), may hold values from -0.15625 to 0.15625
- output_projection_weight: bfloat16 [1536, 1536], P('fsdp', 'tensor'), may hold values from -2.5 to 2.5
- gate_projection_weight: bfloat16 [1536, 3840], P('fsdp', 'tensor'), may hold values from -0.15625 to 0.15625
- up_projection_weight: bfloat16 [1536, 3840], P('fsdp', 'tensor'), may hold values from -0.15625 to 0.15625
- down_projection_weight: bfloat16 [1536, 3840], P('fsdp', 'tensor'), may hold values from -0.75 to 0.75
- query_adapter_first: bfloat16 [8, 1536, 16], replicated, may hold values from -0.15625 to 0.15625
- query_adapter_second: bfloat16 [8, 16, 1536], P(None, None, 'tensor'), may hold values from -0.75 to 0.75
- key_adapter_first: bfloat16 [8, 1536, 16], replicated, may hold values from -0.15625 to 0.15625
- key_adapter_second: bfloat16 [8, 16, 512], P(None, None, 'tensor'), may hold values from -0.75 to 0.75
- value_adapter_first: bfloat16 [8, 1536, 16], replicated, may hold values from -0.15625 to 0.15625
- value_adapter_second: bfloat16 [8, 16, 512], P(None, None, 'tensor'), may hold values from -0.75 to 0.75
- output_adapter_first: bfloat16 [8, 16, 1536], P(None, None, 'tensor'), may hold values from -0.15625 to 0.15625
- output_adapter_second: bfloat16 [8, 16, 1536], replicated, may hold values from -3 to 3
- gate_adapter_first: bfloat16 [8, 1536, 16], replicated, may hold values from -0.15625 to 0.15625
- gate_adapter_second: bfloat16 [8, 16, 3840], P(None, None, 'tensor'), may hold values from -0.75 to 0.75
- up_adapter_first: bfloat16 [8, 1536, 16], replicated, may hold values from -0.15625 to 0.15625
- up_adapter_second: bfloat16 [8, 16, 3840], P(None, None, 'tensor'), may hold values from -0.75 to 0.75
- down_adapter_first: bfloat16 [8, 16, 3840], P(None, None, 'tensor'), may hold values from -0.09375 to 0.09375
- down_adapter_second: bfloat16 [8, 16, 1536], replicated, may hold values from -3 to 3
Outputs:
- output: bfloat16 [16, 2048, 1536], P('fsdp', 'seq')
- token_grad: bfloat16 [16, 2048, 1536], P('fsdp', 'seq')
- query_lora_in_grad: float32 [8, 1536, 16], replicated
- query_lora_out_grad: float32 [8, 16, 1536], replicated
- key_lora_in_grad: float32 [8, 1536, 16], replicated
- key_lora_out_grad: float32 [8, 16, 512], replicated
- value_lora_in_grad: float32 [8, 1536, 16], replicated
- value_lora_out_grad: float32 [8, 16, 512], replicated
- output_lora_in_grad: float32 [8, 16, 1536], replicated
- output_lora_out_grad: float32 [8, 16, 1536], replicated
- gate_lora_in_grad: float32 [8, 1536, 16], replicated
- gate_lora_out_grad: float32 [8, 16, 3840], replicated
- up_lora_in_grad: float32 [8, 1536, 16], replicated
- up_lora_out_grad: float32 [8, 16, 3840], replicated
- down_lora_in_grad: float32 [8, 16, 3840], replicated
- down_lora_out_grad: float32 [8, 16, 1536], replicated
Inputs may be any that keep to these rules, and one draw needn't show every extreme that they name: `document_length_table`: each row lists the lengths of the 4 documents of one sequence in order, each 1 or more, summing to 2048; the longest is exactly 1792. `sequence_window_length`: one sequence has a window of exactly 1024.
All inputs are finite; a program needn't handle non-finite values.
Results may differ from a plain program's by a relative error of at most 0.023.
Values may be sent and summed in bfloat16 or wider, within the bound.
No kernel may reach another device: no remote copies, remote signals or barrier semaphores. Data moves between devices by JAX's collectives and lax.ppermute only.
A program may use at most 192 MiB of HBM per device.

v0:
```python
import jax
import jax.numpy as jnp
from jax import lax
from jax.sharding import PartitionSpec as P

HDIM = 64
WINDOW = 1024
GROUP = 3


highest = lax.Precision.HIGHEST
eps_norm = 1e-05
adapter_scale = 2.0
rope_base = 10000.0
residual_scale = 1.4 / 52.0**0.5
masked_score = -1e30
contract_row_axis = ((1,), (0,))
contract_trailing = ((1,), (1,))
contract_leading = ((0,), (0,))


def default_product(left_side, right_side, contract):
    return lax.dot_general(
        left_side, right_side, (contract, ((), ())), preferred_element_type=jnp.float32
    )


def precise_product(left_side, right_side, contract):
    return lax.dot_general(
        left_side,
        right_side,
        (contract, ((), ())),
        precision=highest,
        preferred_element_type=jnp.float32,
    )


def rms_norm(values, gain_vector):
    return (
        values
        * lax.rsqrt(jnp.mean(values * values, axis=-1, keepdims=True) + eps_norm)
        * gain_vector
    )


def rms_back(values, gain_vector, normed_grad):
    inverse = lax.rsqrt(jnp.mean(values * values, axis=-1, keepdims=True) + eps_norm)
    scaled = normed_grad * gain_vector
    return inverse * scaled - values * inverse**3 * jnp.mean(
        scaled * values, axis=-1, keepdims=True
    )


def doc_tables(lengths_row, length_total):
    doc_ends = jnp.cumsum(lengths_row, dtype=jnp.int32)
    places = jnp.arange(length_total, dtype=jnp.int32)
    doc_ids = jnp.sum(
        (places[:, None] >= doc_ends[None, :]).astype(jnp.int32), axis=1, dtype=jnp.int32
    )
    starts = doc_ends - lengths_row
    member = doc_ids[:, None] == jnp.arange(lengths_row.shape[0], dtype=jnp.int32)[None, :]
    begins = jnp.sum(jnp.where(member, starts[None, :], 0), axis=1, dtype=jnp.int32)
    return (doc_ids, places - begins)


def rotary_tables(positions):
    frequency = rope_base ** (-(jnp.arange(HDIM // 2, dtype=jnp.float32) * (2.0 / HDIM)))
    angles = positions.astype(jnp.float32)[:, None] * frequency[None, :]
    return (jnp.cos(angles), jnp.sin(angles))


def rotary(values, cosine_table, sine_table):
    half_dim = values.shape[-1] // 2
    first_half = values[..., :half_dim]
    second_half = values[..., half_dim:]
    return jnp.concatenate(
        [
            first_half * cosine_table - second_half * sine_table,
            second_half * cosine_table + first_half * sine_table,
        ],
        axis=-1,
    )


def rotary_back(gradient, cosine_table, sine_table):
    half_dim = gradient.shape[-1] // 2
    first_half = gradient[..., :half_dim]
    second_half = gradient[..., half_dim:]
    return jnp.concatenate(
        [
            first_half * cosine_table + second_half * sine_table,
            second_half * cosine_table - first_half * sine_table,
        ],
        axis=-1,
    )


def adapter_pick(adapter_selector, factor_stack):
    return jnp.einsum(
        "a,aij->ij", adapter_selector, factor_stack.astype(jnp.float32), precision=highest
    )


def block_mask(doc_ids, row_start, row_count, key_start, key_count, window):
    row_places = row_start + jnp.arange(row_count, dtype=jnp.int32)
    key_places = key_start + jnp.arange(key_count, dtype=jnp.int32)
    row_docs = lax.dynamic_slice_in_dim(doc_ids, row_start, row_count, 0)
    key_docs = lax.dynamic_slice_in_dim(doc_ids, key_start, key_count, 0)
    return (
        (row_docs[:, None] == key_docs[None, :])
        & (key_places[None, :] <= row_places[:, None])
        & (row_places[:, None] - key_places[None, :] < window)
    )


def apply_projection(
    input_tokens_reduced, base_weight, adapter_first_reduced, adapter_second_float
):
    inner_product = default_product(input_tokens_reduced, adapter_first_reduced, contract_row_axis)
    return (
        default_product(input_tokens_reduced, base_weight, contract_row_axis)
        + adapter_scale * precise_product(inner_product, adapter_second_float, contract_row_axis),
        inner_product,
    )


def apply_row_projection(
    input_tokens_reduced, base_weight, adapter_first_reduced, adapter_second_float
):
    inner_product = default_product(input_tokens_reduced, adapter_first_reduced, contract_trailing)
    return (
        default_product(input_tokens_reduced, base_weight, contract_trailing)
        + adapter_scale * precise_product(inner_product, adapter_second_float, contract_row_axis),
        inner_product,
    )


def input_factor_side(
    gradient_reduced,
    base_weight,
    adapter_first_float,
    adapter_second_reduced,
    inner_product,
    input_tokens_float,
):
    inner_gradient = adapter_scale * default_product(
        gradient_reduced, adapter_second_reduced, contract_trailing
    )
    input_gradient = default_product(
        gradient_reduced, base_weight, contract_trailing
    ) + precise_product(inner_gradient, adapter_first_float, contract_trailing)
    in_grad = precise_product(input_tokens_float, inner_gradient, contract_leading)
    second_factor_gradient = adapter_scale * precise_product(
        inner_product, gradient_reduced.astype(jnp.float32), contract_leading
    )
    return (input_gradient, in_grad, second_factor_gradient)


def output_factor_side(
    gradient_reduced,
    base_weight,
    adapter_first_float,
    adapter_second_reduced,
    inner_product,
    input_tokens_reduced,
):
    inner_gradient = adapter_scale * default_product(
        gradient_reduced, adapter_second_reduced, contract_trailing
    )
    input_gradient = default_product(
        gradient_reduced, base_weight, contract_row_axis
    ) + precise_product(inner_gradient, adapter_first_float, contract_row_axis)
    in_grad = precise_product(
        inner_gradient, input_tokens_reduced.astype(jnp.float32), contract_leading
    )
    second_factor_gradient = adapter_scale * precise_product(
        inner_product, gradient_reduced.astype(jnp.float32), contract_leading
    )
    return (input_gradient, in_grad, second_factor_gradient)


def shards(
    tokens,
    output_gradient,
    document_length_table,
    sequence_adapter_index,
    sequence_window_length,
    attention_norm_gain,
    feedforward_norm_gain,
    query_projection_weight,
    key_projection_weight,
    value_projection_weight,
    output_projection_weight,
    gate_projection_weight,
    up_projection_weight,
    down_projection_weight,
    query_adapter_first,
    query_adapter_second,
    key_adapter_first,
    key_adapter_second,
    value_adapter_first,
    value_adapter_second,
    output_adapter_first,
    output_adapter_second,
    gate_adapter_first,
    gate_adapter_second,
    up_adapter_first,
    up_adapter_second,
    down_adapter_first,
    down_adapter_second,
):
    seq_parts = lax.axis_size("seq")
    seq_rank = lax.axis_index("seq")
    local_len = tokens.shape[1]
    full_len = local_len * seq_parts
    gathered = (
        lax.all_gather(query_projection_weight, "fsdp", axis=0, tiled=True),
        lax.all_gather(key_projection_weight, "fsdp", axis=0, tiled=True),
        lax.all_gather(value_projection_weight, "fsdp", axis=0, tiled=True),
        lax.all_gather(output_projection_weight, "fsdp", axis=0, tiled=True),
        lax.all_gather(gate_projection_weight, "fsdp", axis=0, tiled=True),
        lax.all_gather(up_projection_weight, "fsdp", axis=0, tiled=True),
        lax.all_gather(down_projection_weight, "fsdp", axis=0, tiled=True),
    )
    full_query, full_key, full_value, full_output, full_gate, full_up, full_down = gathered
    adapter_factor_list = (
        query_adapter_first,
        query_adapter_second,
        key_adapter_first,
        key_adapter_second,
        value_adapter_first,
        value_adapter_second,
        output_adapter_first,
        output_adapter_second,
        gate_adapter_first,
        gate_adapter_second,
        up_adapter_first,
        up_adapter_second,
        down_adapter_first,
        down_adapter_second,
    )
    adapter_selector = (
        jnp.arange(query_adapter_first.shape[0], dtype=jnp.int32) == sequence_adapter_index[0]
    ).astype(jnp.float32)
    picked = [
        adapter_pick(adapter_selector, adapter_factor) for adapter_factor in adapter_factor_list
    ]
    picked_low = [adapter_factor.astype(jnp.bfloat16) for adapter_factor in picked]
    doc_ids, doc_pos = doc_tables(document_length_table[0], full_len)
    cosine_table, sine_table = rotary_tables(doc_pos)
    local_cos = lax.dynamic_slice_in_dim(cosine_table, seq_rank * local_len, local_len, 0)
    local_sin = lax.dynamic_slice_in_dim(sine_table, seq_rank * local_len, local_len, 0)
    window = sequence_window_length[0]
    tokens_f = tokens[0].astype(jnp.float32)
    normed_attn = rms_norm(tokens_f, attention_norm_gain).astype(jnp.bfloat16)
    query_raw, query_mid = apply_projection(normed_attn, full_query, picked_low[0], picked[1])
    key_raw, key_mid = apply_projection(normed_attn, full_key, picked_low[2], picked[3])
    value_raw, value_mid = apply_projection(normed_attn, full_value, picked_low[4], picked[5])
    query_tokens = rotary(
        query_raw.reshape(local_len, -1, HDIM), local_cos[:, None, :], local_sin[:, None, :]
    ).astype(jnp.bfloat16)
    key_tokens = rotary(
        key_raw.reshape(local_len, -1, HDIM), local_cos[:, None, :], local_sin[:, None, :]
    ).astype(jnp.bfloat16)
    value_tokens = value_raw.astype(jnp.bfloat16)
    head_query, head_key, head_value = (
        lax.all_to_all(
            query_tokens.reshape(local_len, seq_parts, -1),
            "seq",
            split_axis=1,
            concat_axis=0,
            tiled=True,
        ),
        lax.all_to_all(key_tokens, "seq", split_axis=1, concat_axis=0, tiled=True),
        lax.all_to_all(
            value_tokens.reshape(local_len, seq_parts, -1),
            "seq",
            split_axis=1,
            concat_axis=0,
            tiled=True,
        ),
    )
    kv_local = head_key.shape[2] // HDIM
    head_query = head_query.reshape(full_len, kv_local, GROUP, HDIM)
    query_block = min(512, full_len)
    key_span = min(full_len, query_block + WINDOW)
    score_scale = HDIM ** (-0.5)
    block_starts = jnp.arange(full_len // query_block, dtype=jnp.int32) * query_block

    def key_anchor(start):
        return jnp.clip(start + query_block - key_span, 0, full_len - key_span)

    def block_scores(start, key_start):
        query_rows = lax.dynamic_slice_in_dim(head_query, start, query_block, 0)
        key_rows = lax.dynamic_slice_in_dim(head_key, key_start, key_span, 0)
        scores = (
            jnp.einsum("ikgd,jkd->kgij", query_rows, key_rows, preferred_element_type=jnp.float32)
            * score_scale
        )
        allowed = block_mask(doc_ids, start, query_block, key_start, key_span, window)
        return (jnp.where(allowed, scores, masked_score), query_rows, key_rows)

    def attend_block(start):
        key_start = key_anchor(start)
        scores, query_rows, key_rows = block_scores(start, key_start)
        value_rows = lax.dynamic_slice_in_dim(head_value, key_start, key_span, 0)
        top_score = jnp.max(scores, axis=-1, keepdims=True)
        exp_scores = jnp.exp(scores - top_score)
        row_total = jnp.sum(exp_scores, axis=-1, keepdims=True)
        probabilities = (exp_scores / row_total).astype(jnp.bfloat16)
        block_out = jnp.einsum(
            "kgij,jkd->ikgd", probabilities, value_rows, preferred_element_type=jnp.float32
        )
        return (block_out.astype(jnp.bfloat16), (top_score + jnp.log(row_total))[..., 0])

    attended_heads, log_totals = lax.map(attend_block, block_starts)
    attended = lax.all_to_all(
        attended_heads.reshape(full_len, 1, -1), "seq", split_axis=0, concat_axis=1, tiled=True
    ).reshape(local_len, -1)
    attn_partial, output_mid = apply_row_projection(attended, full_output, picked_low[6], picked[7])
    attn_branch = lax.psum(attn_partial.astype(jnp.bfloat16), "tensor").astype(jnp.float32)
    residual = tokens_f + residual_scale * attn_branch
    normed_ffn = rms_norm(residual, feedforward_norm_gain).astype(jnp.bfloat16)
    gate_value, gate_mid = apply_projection(normed_ffn, full_gate, picked_low[8], picked[9])
    up_value, up_mid = apply_projection(normed_ffn, full_up, picked_low[10], picked[11])
    hidden = (jax.nn.silu(gate_value) * up_value).astype(jnp.bfloat16)
    ffn_partial, down_mid = apply_row_projection(hidden, full_down, picked_low[12], picked[13])
    ffn_branch = lax.psum(ffn_partial.astype(jnp.bfloat16), "tensor").astype(jnp.float32)
    output = (residual + residual_scale * ffn_branch).astype(jnp.bfloat16)
    again = (
        lax.all_gather(query_projection_weight, "fsdp", axis=0, tiled=True),
        lax.all_gather(key_projection_weight, "fsdp", axis=0, tiled=True),
        lax.all_gather(value_projection_weight, "fsdp", axis=0, tiled=True),
        lax.all_gather(output_projection_weight, "fsdp", axis=0, tiled=True),
        lax.all_gather(gate_projection_weight, "fsdp", axis=0, tiled=True),
        lax.all_gather(up_projection_weight, "fsdp", axis=0, tiled=True),
        lax.all_gather(down_projection_weight, "fsdp", axis=0, tiled=True),
    )
    back_query, back_key, back_value, back_output, back_gate, back_up, back_down = again
    cotangent = output_gradient[0].astype(jnp.float32)
    ffn_out_grad = (residual_scale * cotangent).astype(jnp.bfloat16)
    hidden_grad, grad_down_in, grad_down_out = output_factor_side(
        ffn_out_grad, back_down, picked[12], picked_low[13], down_mid, hidden
    )
    sigmoid_gate = jax.nn.sigmoid(gate_value)
    gate_grad = (
        hidden_grad * up_value * sigmoid_gate * (1.0 + gate_value * (1.0 - sigmoid_gate))
    ).astype(jnp.bfloat16)
    up_grad = (hidden_grad * (gate_value * sigmoid_gate)).astype(jnp.bfloat16)
    normed_ffn_f = normed_ffn.astype(jnp.float32)
    gate_input_grad, grad_gate_in, grad_gate_out = input_factor_side(
        gate_grad, back_gate, picked[8], picked_low[9], gate_mid, normed_ffn_f
    )
    up_input_grad, grad_up_in, grad_up_out = input_factor_side(
        up_grad, back_up, picked[10], picked_low[11], up_mid, normed_ffn_f
    )
    normed_ffn_grad = lax.psum(
        (gate_input_grad + up_input_grad).astype(jnp.bfloat16), "tensor"
    ).astype(jnp.float32)
    residual_grad = cotangent + rms_back(residual, feedforward_norm_gain, normed_ffn_grad)
    attn_out_grad = (residual_scale * residual_grad).astype(jnp.bfloat16)
    attended_grad, grad_output_in, grad_output_out = output_factor_side(
        attn_out_grad, back_output, picked[6], picked_low[7], output_mid, attended
    )
    head_grad = lax.all_to_all(
        attended_grad.astype(jnp.bfloat16).reshape(local_len, seq_parts, -1),
        "seq",
        split_axis=1,
        concat_axis=0,
        tiled=True,
    )
    head_grad = head_grad.reshape(full_len, kv_local, GROUP, HDIM)

    def back_block(carry, input_tokens):
        key_grads, value_grads = carry
        start, log_total = input_tokens
        key_start = key_anchor(start)
        scores, query_rows, key_rows = block_scores(start, key_start)
        value_rows = lax.dynamic_slice_in_dim(head_value, key_start, key_span, 0)
        grad_rows = lax.dynamic_slice_in_dim(head_grad, start, query_block, 0)
        probabilities = jnp.exp(scores - log_total[..., None])
        prob_grad = jnp.einsum(
            "ikgd,jkd->kgij", grad_rows, value_rows, preferred_element_type=jnp.float32
        )
        spread = jnp.sum(prob_grad * probabilities, axis=-1, keepdims=True)
        score_grad = (probabilities * (prob_grad - spread)).astype(jnp.bfloat16)
        query_part = (
            jnp.einsum("kgij,jkd->ikgd", score_grad, key_rows, preferred_element_type=jnp.float32)
            * score_scale
        )
        key_part = (
            jnp.einsum("kgij,ikgd->jkd", score_grad, query_rows, preferred_element_type=jnp.float32)
            * score_scale
        )
        value_part = jnp.einsum(
            "kgij,ikgd->jkd",
            probabilities.astype(jnp.bfloat16),
            grad_rows,
            preferred_element_type=jnp.float32,
        )
        key_grads = lax.dynamic_update_slice_in_dim(
            key_grads,
            lax.dynamic_slice_in_dim(key_grads, key_start, key_span, 0) + key_part,
            key_start,
            0,
        )
        value_grads = lax.dynamic_update_slice_in_dim(
            value_grads,
            lax.dynamic_slice_in_dim(value_grads, key_start, key_span, 0) + value_part,
            key_start,
            0,
        )
        return ((key_grads, value_grads), query_part)

    empty_keys = jnp.zeros((full_len, kv_local, HDIM), jnp.float32)
    (key_grads, value_grads), query_grads = lax.scan(
        back_block, (empty_keys, empty_keys), (block_starts, log_totals)
    )
    query_send = rotary_back(
        query_grads.reshape(full_len, kv_local, GROUP, HDIM),
        cosine_table[:, None, None, :],
        sine_table[:, None, None, :],
    )
    key_send = rotary_back(key_grads, cosine_table[:, None, :], sine_table[:, None, :])
    query_back, key_back, value_back = (
        lax.all_to_all(
            query_send.astype(jnp.bfloat16).reshape(full_len, 1, -1),
            "seq",
            split_axis=0,
            concat_axis=1,
            tiled=True,
        ),
        lax.all_to_all(
            key_send.astype(jnp.bfloat16), "seq", split_axis=0, concat_axis=1, tiled=True
        ),
        lax.all_to_all(
            value_grads.astype(jnp.bfloat16), "seq", split_axis=0, concat_axis=1, tiled=True
        ),
    )
    normed_attn_f = normed_attn.astype(jnp.float32)
    query_input_grad, grad_query_in, grad_query_out = input_factor_side(
        query_back.reshape(local_len, -1),
        back_query,
        picked[0],
        picked_low[1],
        query_mid,
        normed_attn_f,
    )
    key_input_grad, grad_key_in, grad_key_out = input_factor_side(
        key_back.reshape(local_len, -1), back_key, picked[2], picked_low[3], key_mid, normed_attn_f
    )
    value_input_grad, grad_value_in, grad_value_out = input_factor_side(
        value_back.reshape(local_len, -1),
        back_value,
        picked[4],
        picked_low[5],
        value_mid,
        normed_attn_f,
    )
    normed_attn_grad = lax.psum(
        (query_input_grad + key_input_grad + value_input_grad).astype(jnp.bfloat16), "tensor"
    ).astype(jnp.float32)
    token_grad = (residual_grad + rms_back(tokens_f, attention_norm_gain, normed_attn_grad)).astype(
        jnp.bfloat16
    )
    local_grads = (
        grad_query_in,
        grad_query_out,
        grad_key_in,
        grad_key_out,
        grad_value_in,
        grad_value_out,
        grad_output_in,
        grad_output_out,
        grad_gate_in,
        grad_gate_out,
        grad_up_in,
        grad_up_out,
        grad_down_in,
        grad_down_out,
    )
    stacks = [adapter_selector[:, None, None] * term[None] for term in local_grads]
    tensor_rank = lax.axis_index("tensor")
    tensor_parts = lax.axis_size("tensor")
    padded = list(stacks)
    for place in (1, 3, 5, 6, 9, 11, 12):
        piece_grad = stacks[place]
        local_width = piece_grad.shape[2]
        whole_grad = jnp.zeros(piece_grad.shape[:2] + (local_width * tensor_parts,), jnp.float32)
        padded[place] = lax.dynamic_update_slice_in_dim(
            whole_grad, piece_grad, tensor_rank * local_width, 2
        )
    summed = lax.psum(
        (
            padded[0],
            padded[1],
            padded[2],
            padded[3],
            padded[4],
            padded[5],
            padded[6],
            padded[7],
            padded[8],
            padded[9],
            padded[10],
            padded[11],
            padded[12],
            padded[13],
        ),
        ("seq", "tensor", "fsdp"),
    )
    return (output.reshape(1, local_len, -1), token_grad.reshape(1, local_len, -1)) + tuple(summed)


def solution(mesh):
    return jax.shard_map(
        shards,
        mesh=mesh,
        in_specs=(
            P("fsdp", "seq", None),
            P("fsdp", "seq", None),
            P("fsdp", None),
            P("fsdp"),
            P("fsdp"),
            P(),
            P(),
            P("fsdp", "tensor"),
            P("fsdp", "tensor"),
            P("fsdp", "tensor"),
            P("fsdp", "tensor"),
            P("fsdp", "tensor"),
            P("fsdp", "tensor"),
            P("fsdp", "tensor"),
            P(),
            P(None, None, "tensor"),
            P(),
            P(None, None, "tensor"),
            P(),
            P(None, None, "tensor"),
            P(None, None, "tensor"),
            P(),
            P(),
            P(None, None, "tensor"),
            P(),
            P(None, None, "tensor"),
            P(None, None, "tensor"),
            P(),
        ),
        out_specs=(
            P("fsdp", "seq", None),
            P("fsdp", "seq", None),
            P(),
            P(),
            P(),
            P(),
            P(),
            P(),
            P(),
            P(),
            P(),
            P(),
            P(),
            P(),
            P(),
            P(),
        ),
        check_vma=False,
    )
```

profile of v0, /device:TPU:1, one launch (start us, length us, event | category | flops | bytes accessed | tf_op | source)
XLA Modules:
  0.0 1168.6 jit_solution(7014231282631117192)
XLA Ops:
  10.3 29.8 %all_gather.28 = bf16[1536,256]{1,0:T(8,128)(2,1)} all-gather(bf16[96,256]{1,0:T(8,128)(2,1)} %param.41), channel_id=1, replica_groups=mesh['seq'=4,'tensor'=2,'fsdp'=16] {'fsdp'}, dimensions={0}, use_global_device_ids=true | all-gather | bytes 835584 | tf_op jit(solution)/shard_map/all_gather | solution.py:219
  58.5 22.3 %all_gather.29 = bf16[1536,256]{1,0:T(8,128)(2,1)S(1)} all-gather(bf16[96,256]{1,0:T(8,128)(2,1)} %param.40), channel_id=1, replica_groups=mesh['seq'=4,'tensor'=2,'fsdp'=16] {'fsdp'}, dimensions={0}, use_global_device_ids=true | all-gather | bytes 835584 | tf_op jit(solution)/shard_map/all_gather | solution.py:218
  108.7 8.0 all-to-all-done.2
  117.9 61.4 %while.34 = (s32[]{:T(128)}, bf16[4,512,1,3,64]{1,4,3,2,0:T(8,128)(2,1)S(1)}, f32[4,1,3,512]{3,2,1,0:T(4,128)}, s32[4]{0:T(128)S(1)}, bf16[2048,1,64]{0,2,1:T(8,...) while((s32[]{:T(128)}, ...), condition=%wide.region_7.8_spmd, body=%wide.region_4.7_spmd.sunk | while | flops 637108736 | bytes 32340232 | solution.py:316
  194.2 7.6 all-to-all-done.3
  229.7 46.2 %all-reduce.7.cloned.1.call-done = bf16[512,1536]{1,0:T(8,128)(2,1)} async-done(((bf16[512,1536]{1,0:T(8,128)(2,1)}), bf16[512,1536]{1,0:T(8,128)(2,1)}) %all-reduce.7.cloned.1.call-update) | async-done | bytes 1572880 | tf_op jit(solution)/shard_map/psum | solution.py:321
  280.8 61.5 %all-gather.10.cloned.1.call-done = bf16[1536,1920]{1,0:T(8,128)(2,1)} async-done(((bf16[96,1920]{1,0:T(8,128)(2,1)}), bf16[1536,1920]{1,0:T(8,128)(2,1)}) %all-gather.10.cloned.1.call-update) | async-done | bytes 5898256 | tf_op jit(solution)/shard_map/all_gather | solution.py:221
  342.3 6.2 fusion.221
  353.9 52.2 %all-gather.12.cloned.1.call-done = bf16[1536,1920]{1,0:T(8,128)(2,1)} async-done(((bf16[96,1920]{1,0:T(8,128)(2,1)}), bf16[1536,1920]{1,0:T(8,128)(2,1)}) %all-gather.12.cloned.1.call-update) | async-done | bytes 5898256 | tf_op jit(solution)/shard_map/all_gather | solution.py:222
  406.1 6.0 fusion.222
  417.5 52.3 %all-gather.14.cloned.1.call-done = bf16[1536,1920]{1,0:T(8,128)(2,1)} async-done(((bf16[96,1920]{1,0:T(8,128)(2,1)}), bf16[1536,1920]{1,0:T(8,128)(2,1)}) %all-gather.14.cloned.1.call-update) | async-done | bytes 5898256 | tf_op jit(solution)/shard_map/all_gather | solution.py:223
  469.8 6.4 fusion.92
  503.1 6.2 fusion.223
  521.6 37.9 %all-reduce.9.cloned.1.call-done = bf16[512,1536]{1,0:T(8,128)(2,1)} async-done(((bf16[512,1536]{1,0:T(8,128)(2,1)}), bf16[512,1536]{1,0:T(8,128)(2,1)}) %all-reduce.9.cloned.1.call-update) | async-done | bytes 1572880 | tf_op jit(solution)/shard_map/psum | solution.py:357
  580.3 7.3 all-to-all-done.4
  589.8 207.6 %while.35 = (s32[]{:T(128)}, f32[2048,1,64]{0,2,1:T(8,128)S(1)}, f32[2048,1,64]{0,2,1:T(8,128)S(1)}, f32[4,512,1,3,64]{1,0,4,3,2:T(4,128)}, s32[4]{0:T(128)S(1)}...) while((s32[]{:T(128)}, f32[2048,1,64]{0,2,1:T(8,128)S(1)}, ...), condition=%wide.region_15.16_spmd, body=%wide.region_13.15_spmd.sunk | while | flops 1536295424 | bytes 116662608 | solution.py:416
  601.1 5.7 fusion.363
  606.8 11.1 fusion.364
  623.2 5.4 fusion.366
  633.7 8.6 dynamic_update_slice.94
  653.2 5.7 fusion.363
  658.9 11.1 fusion.364
  675.3 5.4 fusion.366
  685.8 8.6 dynamic_update_slice.94
  705.2 5.7 fusion.363
  711.0 11.1 fusion.364
  737.9 8.6 dynamic_update_slice.94
  757.3 5.7 fusion.363
  763.0 11.1 fusion.364
  788.8 8.6 dynamic_update_slice.94
  867.0 87.6 %all-reduce.13.cloned.1.call-done = (bf16[512,1536]{1,0:T(8,128)(2,1)}, bf16[512,1536]{1,0:T(8,128)(2,1)}) async-done(((bf16[512,1536]{1,0:T(8,128)(2,1)}, bf16[512,1536]{1,0:T(8,128)(2,1)}), (bf16[512,1536]{1,0:T(8,128)(2,1)}, bf16[512,1536]{1,0:T(8,128)(2,1)})) %all-reduce.13.cloned.1.call-update) | async-done | bytes 3145744 | tf_op jit(solution)/shard_map/psum | solution.py:328
  961.6 184.3 %all-reduce.11.cloned.1.call-done = (f32[8,1536,16]{1,2,0:T(8,128)}, f32[8,16,1536]{2,1,0:T(8,128)}, f32[8,1536,16]{1,2,0:T(8,128)}, f32[8,16,512]{2,1,0:T(8,128...) async-done(((f32[8,1536,16]{1,2,0:T(8,128)}, ...) | async-done | bytes 13500432 | tf_op jit(solution)/shard_map/psum | solution.py:493
  (526 shorter events, 396.4 us)
Async XLA Ops:
  7.2 217.5 %copy-start = (bf16[8,16,1920]{2,1,0:T(8,128)(2,1)S(1)}, bf16[8,16,1920]{2,1,0:T(8,128)(2,1)}, u32[]{:S(2)}) copy-start(bf16[8,16,1920]{2,1,0:T(8,128)(2,1)} %param.55) | copy-start | bytes 1474564
  7.2 35.3 %copy-start.89 = (f32[1536]{0:T(1024)S(1)}, f32[1536]{0:T(1024)}, u32[]{:S(2)}) copy-start(f32[1536]{0:T(1024)} %param.37) | copy-start | bytes 18436
  7.2 76.4 %all-gather.6.cloned.1.call-start = ((), (), s32[]{:S(2)}) async-start(), calls=%async_computation.8 | async-start | bytes 2506752 | tf_op jit(solution)/shard_map/all_gather | solution.py:217
  10.3 32.1 %copy-start.94 = (f32[512]{0:T(512)}, f32[512]{0:T(512)S(1)}, u32[]{:S(2)}) copy-start(f32[512]{0:T(512)S(1)} %get-tuple-element.517) | copy-start | bytes 6148
  44.6 39.1 %copy-start.3 = (bf16[512,1536]{1,0:T(8,128)(2,1)}, bf16[512,1536]{1,0:T(8,128)(2,1)S(1)}, u32[]{:S(2)}) copy-start(bf16[512,1536]{1,0:T(8,128)(2,1)S(1)} %fusion.74) | copy-start | bytes 4718596
  47.3 44.0 %all-to-all-start = ((bf16[512,4,64]{0,2,1:T(8,128)(2,1)}), bf16[512,4,64]{0,2,1:T(8,128)(2,1)}, u32[]{:S(2)}, u32[]{:S(2)}) async-start(bf16[512,4,64]{0,2,1:T(8,128)(2,1)} %bitcast.44), calls=%async_computation | async-start | bytes 524288 | tf_op jit(solution)/shard_map/all_to_all | solution.py:275
  52.8 28.6 %copy-start.17 = (f32[1,1536,16]{2,1,0:T(8,128)}, f32[1,1536,16]{2,1,0:T(8,128)S(1)}, u32[]{:S(2)}) copy-start(f32[1,1536,16]{2,1,0:T(8,128)S(1)} %copy.193) | copy-start | bytes 294916
  56.8 24.6 %copy-start.43 = (f32[2048,32]{0,1:T(8,128)}, f32[2048,32]{0,1:T(8,128)S(1)}, u32[]{:S(2)}) copy-start(f32[2048,32]{0,1:T(8,128)S(1)} %get-tuple-element.514) | copy-start | bytes 786436
  58.5 24.6 %copy-start.75 = (f32[512,16]{0,1:T(8,128)}, f32[512,16]{0,1:T(8,128)S(1)}, u32[]{:S(2)}) copy-start(f32[512,16]{0,1:T(8,128)S(1)} %fusion.208) | copy-start | bytes 98308
  58.5 24.6 %copy-start.21 = (f32[1,1536,16]{2,1,0:T(8,128)S(1)}, f32[1,1536,16]{2,1,0:T(8,128)}, u32[]{:S(2)}) copy-start(f32[1,1536,16]{2,1,0:T(8,128)} %copy.197) | copy-start | bytes 294916
  91.3 10.5 all-to-all-start.1
  102.5 14.2 %all-to-all-start.2 = ((bf16[512,4,192]{0,2,1:T(8,128)(2,1)}), bf16[512,4,192]{0,2,1:T(8,128)(2,1)S(1)}, u32[]{:S(2)}, u32[]{:S(2)}) async-start(bf16[512,4,192]{0,2,1:T(8,128)(2,1)} %bitcast.64), calls=%async_computation.2 | async-start | bytes 1572864 | tf_op jit(solution)/shard_map/all_to_all | solution.py:267
  106.0 103.9 %all-gather.8.cloned.1.call-start = ((), (), s32[]{:S(2)}) async-start(), calls=%async_computation.9 | async-start | bytes 2506752 | tf_op jit(solution)/shard_map/all_gather | solution.py:220
  188.8 13.0 %all-to-all-start.3 = ((bf16[4,2,49152]{2,1,0:T(2,128)(2,1)}), bf16[4,2,49152]{2,1,0:T(2,128)(2,1)S(1)}, u32[]{:S(2)}, u32[]{:S(2)}) async-start(bf16[4,2,49152]{2,1,0:T(2,128)(2,1)} %reshape.639), calls=%async_computation.3 | async-start | bytes 1572864 | tf_op jit(solution)/shard_map/all_to_all | solution.py:317
  192.3 83.5 %all-reduce.7.cloned.1.call-start = ((), (), s32[]{:S(2)}) async-start(), calls=%async_computation.10 | async-start | bytes 3145728 | tf_op jit(solution)/shard_map/psum | solution.py:321
  217.0 125.3 %all-gather.10.cloned.1.call-start = ((), (), s32[]{:S(2)}) async-start(), calls=%async_computation.11 | async-start | bytes 6266880 | tf_op jit(solution)/shard_map/all_gather | solution.py:221
  217.6 188.5 %all-gather.12.cloned.1.call-start = ((), (), s32[]{:S(2)}) async-start(), calls=%async_computation.12 | async-start | bytes 6266880 | tf_op jit(solution)/shard_map/all_gather | solution.py:222
  218.2 251.6 %all-gather.14.cloned.1.call-start = ((), (), s32[]{:S(2)}) async-start(), calls=%async_computation.13 | async-start | bytes 6266880 | tf_op jit(solution)/shard_map/all_gather | solution.py:223
  218.7 340.8 %all-reduce.9.cloned.1.call-start = ((), (), s32[]{:S(2)}) async-start(), calls=%async_computation.14 | async-start | bytes 3145728 | tf_op jit(solution)/shard_map/psum | solution.py:357
  219.1 56.7 %copy-start.5 = (bf16[1,512,1536]{2,1,0:T(8,128)(2,1)S(1)}, bf16[1,512,1536]{2,1,0:T(8,128)(2,1)}, u32[]{:S(2)}) copy-start(bf16[1,512,1536]{2,1,0:T(8,128)(2,1)} %param.32) | copy-start | bytes 4718596
  224.9 53.2 %copy-start.88 = (f32[1536]{0:T(1024)S(1)}, f32[1536]{0:T(1024)}, u32[]{:S(2)}) copy-start(f32[1536]{0:T(1024)} %param.38) | copy-start | bytes 18436
  227.7 248.5 %copy-start.77 = (f32[1,16,1920]{2,0,1:T(1,128)}, f32[1,16,1920]{2,0,1:T(1,128)S(1)}, u32[]{:S(2)}) copy-start(f32[1,16,1920]{2,0,1:T(1,128)S(1)} %fusion.102) | copy-start | bytes 368644
  572.1 15.5 %all-to-all-start.4 = ((bf16[512,4,192]{0,2,1:T(8,128)(2,1)}), bf16[512,4,192]{0,2,1:T(8,128)(2,1)S(1)}, u32[]{:S(2)}, u32[]{:S(2)}) async-start(bf16[512,4,192]{0,2,1:T(8,128)(2,1)} %bitcast.88), calls=%async_computation.4 | async-start | bytes 1572864 | tf_op jit(solution)/shard_map/all_to_all | solution.py:365
  804.5 9.8 all-to-all-start.6
  814.4 9.7 all-to-all-start.7
  824.1 12.7 %all-to-all-start.5 = ((bf16[4,2,49152]{2,1,0:T(2,128)(2,1)}), bf16[4,2,49152]{2,1,0:T(2,128)(2,1)}, u32[]{:S(2)}, u32[]{:S(2)}) async-start(bf16[4,2,49152]{2,1,0:T(2,128)(2,1)} %reshape.641), calls=%async_computation.5 | async-start | bytes 1572864 | tf_op jit(solution)/shard_map/all_to_all | solution.py:426
  828.3 126.3 %all-reduce.13.cloned.1.call-start = ((), (), s32[]{:S(2)}) async-start(), calls=%async_computation.16 | async-start | bytes 6291456 | tf_op jit(solution)/shard_map/psum | solution.py:328
  858.8 287.1 %all-reduce.11.cloned.1.call-start = ((), (), s32[]{:S(2)}) async-start(), calls=%async_computation.15 | async-start | bytes 27000832 | tf_op jit(solution)/shard_map/psum | solution.py:493
  866.9 87.7 %copy-start.6 = (bf16[1,512,1536]{2,1,0:T(8,128)(2,1)S(1)}, bf16[1,512,1536]{2,1,0:T(8,128)(2,1)}, u32[]{:S(2)}) copy-start(bf16[1,512,1536]{2,1,0:T(8,128)(2,1)} %param.32) | copy-start | bytes 4718596
  866.9 87.7 %copy-start.90 = (f32[1536]{0:T(1024)S(1)}, f32[1536]{0:T(1024)}, u32[]{:S(2)}) copy-start(f32[1536]{0:T(1024)} %param.37) | copy-start | bytes 18436
  867.0 89.8 %copy-start.95 = (f32[512]{0:T(512)S(1)}, f32[512]{0:T(512)}, u32[]{:S(2)}) copy-start(f32[512]{0:T(512)} %copy-done.94) | copy-start | bytes 6148
  867.0 89.8 %copy-start.96 = (f32[512]{0:T(512)S(1)}, f32[512]{0:T(512)}, u32[]{:S(2)}) copy-start(f32[512]{0:T(512)} %get-tuple-element.516) | copy-start | bytes 6148
  (95 other events, 494.2 us)
Sparse Core Ops, SparseCore 0:
  10.4 53.4 all-gather.5
  109.2 50.3 all-gather.7
  217.1 58.6 all-reduce.6
  278.4 63.8 all-gather.9
  344.9 61.1 all-gather.11
  408.6 61.1 all-gather.13
  503.2 56.3 all-reduce.8
  858.9 95.6 all-reduce.12
  963.3 182.4 all-reduce.10
where the time goes:
time: 1180 us; the launch traced here: 1170 us
  waiting for transfers between devices  559 us (47%)
  matrix products  232 us (20%)
  local copies, waits for them, and re-layouts  128 us (11%)
  other arithmetic  126 us (11%)
  blocking collectives  52.1 us (4%)
  starting transfers between devices  33.4 us (3%)
  loops' own time  21.6 us (2%)
  between operations  16.4 us (1%)
    psum x1, waiting for transfers between devices, shards(): lax.psum((padded[0], padded[1], padded[2], padded[3], padded[4], padded[5...  184 us
    psum x1, waiting for transfers between devices, shards(): lax.psum(ffn_partial.astype(jnp.bfloat16), 'tensor').astype(jnp.float32)  87.6 us
    all_gather x1, waiting for transfers between devices, shards(): lax.all_gather(gate_projection_weight, 'fsdp', axis=0, tiled=True)  61.5 us
    dot_general x28, matrix products, precise_product(): lax.dot_general(left_side, right_side, (contract, ((), ())), precision=hi...  60.1 us
    dot_general x28, matrix products, default_product(): lax.dot_general(left_side, right_side, (contract, ((), ())), preferred_el...  55.7 us
    all_gather x1, waiting for transfers between devices, shards(): lax.all_gather(down_projection_weight, 'fsdp', axis=0, tiled=True)  52.3 us
    all_gather x1, waiting for transfers between devices, shards(): lax.all_gather(up_projection_weight, 'fsdp', axis=0, tiled=True)  52.2 us
    another operation x9, other arithmetic  47.2 us
  transfers between devices with their start and end apart: 17, of which 13 were waited for; matrix products, arithmetic and copies ran while one was open for 16% of the time, Pallas kernels for 0%

commit v1 on v0

v1 whole, which is shorter than its diff:
```python
import jax
import jax.numpy as jnp
from jax import lax
from jax.experimental import pallas as pl
from jax.experimental.pallas import tpu as pltpu
from jax.sharding import Mesh
from jax.sharding import PartitionSpec as P

F32 = jnp.float32
BF16 = jnp.bfloat16
EPS = 1e-05
ROPE_BASE = 10000.0
RS = 1.4 / 52.0**0.5
MASKED = -1e30
TOK = 512
D = 1536
HQ = 768
HK = 256
HDIM = 64
SPAN = 1280
RT = 256
HALO = 1024
CHUNKS = (512, 512, 512, 384)
CHUNK_PATH = ("yx", "xy", "yx", "xy")
VMEM_LIMIT = 56 * 1024 * 1024


def nn(a, b):
    return lax.dot_general(a, b, (((1,), (0,)), ((), ())), preferred_element_type=F32)


def nt(a, b):
    return lax.dot_general(a, b, (((1,), (1,)), ((), ())), preferred_element_type=F32)


def tn(a, b):
    return lax.dot_general(a, b, (((0,), (0,)), ((), ())), preferred_element_type=F32)


VM = pl.BlockSpec(memory_space=pltpu.VMEM)
SM = pl.BlockSpec(memory_space=pltpu.SMEM)
HB = pl.BlockSpec(memory_space=pl.ANY)


def params():
    return pltpu.CompilerParams(vmem_limit_bytes=VMEM_LIMIT)


def sds(shape, dtype):
    return jax.ShapeDtypeStruct(shape, dtype)


def piece_copies(offs, refs, dst, sems):
    copies = []
    for ref in refs:
        for k in range(ref.shape[0]):
            row = pl.multiple_of(offs[len(copies)] * 96, 96)
            copies.append(
                pltpu.make_async_copy(ref.at[k], dst.at[pl.ds(row, 96)], sems.at[len(copies)])
            )
    return copies


def half_swap(v, sign=1):
    lane = lax.broadcasted_iota(jnp.int32, v.shape, 1)
    width = v.shape[1]
    from_low = pltpu.roll(v, 32, 1)
    from_high = pltpu.roll(v, width - 32, 1)
    return jnp.where((lane % 64) < 32, from_high, from_low)


def qkv_kernel(
    offs_a, offs_b, tok, gain, a1, b2, cos, sin, q0, q1, q2, q3, q4, k0, k1, k2, k3, k4,
    normed_o, q_o, kv_o, mid_o, wq, wkv, sem_a, sem_b,
):
    cq = piece_copies(offs_a, (q0, q1, q2, q3, q4), wq, sem_a)
    ck = piece_copies(offs_b, (k0, k1, k2, k3, k4), wkv, sem_b)
    for c in cq + ck:
        c.start()
    for r in range(4):
        rows = pl.ds(r * 128, 128)
        x = tok[rows, :].astype(F32)
        inv = lax.rsqrt(jnp.mean(x * x, axis=-1, keepdims=True) + EPS)
        normed_o[rows, :] = (x * inv * gain[...]).astype(BF16)
    normed = normed_o[...]
    mid = nt(normed, a1[...]).astype(BF16)
    mid_o[...] = mid
    for c in cq + ck:
        c.wait()
    cw = jnp.concatenate([cos[...], cos[...]], axis=1)
    sw = jnp.concatenate([sin[...], sin[...]], axis=1)
    for n in range(5):
        if n < 3:
            w = wq[:, n * 256 : (n + 1) * 256]
        else:
            w = wkv[:, (n - 3) * 256 : (n - 2) * 256]
        acc = nn(normed, w) + nn(mid, b2[:, n * 256 : (n + 1) * 256])
        if n < 4:
            acc = acc * cw + half_swap(acc) * sw
        if n < 3:
            q_o[:, n * 256 : (n + 1) * 256] = (acc.astype(BF16).astype(F32) * 0.125).astype(BF16)
        else:
            kv_o[n - 3] = acc.astype(BF16)


def qkv_call(offs_a, offs_b, tok, gain, a1, b2, cos, sin, wq, wkv):
    return pl.pallas_call(
        qkv_kernel,
        out_shape=(
            sds((TOK, D), BF16),
            sds((TOK, HQ), BF16),
            sds((2, TOK, HK), BF16),
            sds((TOK, 128), BF16),
        ),
        in_specs=[SM, SM] + [VM] * 6 + [HB] * 10,
        out_specs=(VM,) * 4,
        scratch_shapes=[
            pltpu.VMEM((D, HQ), BF16),
            pltpu.VMEM((D, 2 * HK), BF16),
            pltpu.SemaphoreType.DMA((16,)),
            pltpu.SemaphoreType.DMA((16,)),
        ],
        compiler_params=params(),
        cost_estimate=pl.CostEstimate(
            flops=2 * TOK * D * 1280, bytes_accessed=9_000_000, transcendentals=0
        ),
        name="norm_qkv",
    )(offs_a, offs_b, tok, gain, a1, b2, cos, sin, *wq, *wkv)


HEADS_OF_PAIR = ((0, 0, 0), (0, 1, 0), (1, 0, 0), (1, 1, 1), (2, 0, 1), (2, 1, 1))


def bias_of(lo, r):
    key = lax.broadcasted_iota(jnp.int32, (SPAN, RT), 0) + r * RT
    row = lax.broadcasted_iota(jnp.int32, (SPAN, RT), 1) + r * RT + HALO
    return jnp.where((key >= lo) & (key <= row), 0.0, MASKED)


def variants(dst, src):
    lane = lax.broadcasted_iota(jnp.int32, src.shape, 1)
    srcf = src.astype(F32)
    rolled = pltpu.roll(srcf, 64, 1)
    low = lane < 64
    dst[0] = jnp.where(low, srcf, 0.0).astype(BF16)
    dst[1] = jnp.where(low, 0.0, rolled).astype(BF16)
    dst[2] = jnp.where(low, rolled, 0.0).astype(BF16)
    dst[3] = jnp.where(low, 0.0, srcf).astype(BF16)


def attend_kernel(q, lo, kv2, kv1, kv0, out, lse, kvar, vt, bias, ot):
    r = pl.program_id(1)

    @pl.when(r == 0)
    def _():
        kcat = jnp.concatenate([kv2[0], kv1[0], kv0[0]], axis=0)
        variants(kvar, kcat)
        vcat = jnp.concatenate([kv2[1], kv1[1], kv0[1]], axis=0)
        vt[...] = vcat.astype(F32).T.astype(BF16)

    bias[...] = bias_of(lo[...], r)
    keys = pl.ds(pl.multiple_of(r * RT, RT), SPAN)
    for i, (tile, half, kv) in enumerate(HEADS_OF_PAIR):
        qt = q[:, tile * 128 : (tile + 1) * 128]
        s = nt(kvar[2 * kv + half, keys, :], qt) + bias[...]
        m = jnp.max(s, axis=0, keepdims=True)
        e = jnp.exp(s - m)
        total = jnp.sum(e, axis=0, keepdims=True)
        o = nn(vt[kv * 64 : (kv + 1) * 64, keys], e.astype(BF16))
        ot[i * 64 : (i + 1) * 64, :] = o * (1.0 / total)
        lse[i : i + 1, :] = m + jnp.log(total)
    out[...] = ot[...].T.astype(BF16)


def attend_call(q, lo, kv2, kv1, kv0):
    kvspec = pl.BlockSpec((2, TOK, 128), lambda p, r: (0, 0, p))
    return pl.pallas_call(
        attend_kernel,
        grid=(2, 2),
        out_shape=(sds((TOK, HQ), BF16), sds((16, TOK), F32)),
        in_specs=[
            pl.BlockSpec((RT, 384), lambda p, r: (r, p)),
            pl.BlockSpec((1, RT), lambda p, r: (0, r)),
            kvspec,
            kvspec,
            kvspec,
        ],
        out_specs=(
            pl.BlockSpec((RT, 384), lambda p, r: (r, p)),
            pl.BlockSpec((8, RT), lambda p, r: (p, r)),
        ),
        scratch_shapes=[
            pltpu.VMEM((4, HALO + TOK, 128), BF16),
            pltpu.VMEM((128, HALO + TOK), BF16),
            pltpu.VMEM((SPAN, RT), F32),
            pltpu.VMEM((384, RT), F32),
        ],
        compiler_params=params(),
        cost_estimate=pl.CostEstimate(
            flops=4 * 12 * 2 * RT * SPAN * 128, bytes_accessed=4_000_000, transcendentals=0
        ),
        name="attend",
    )(q, lo, kv2, kv1, kv0)


def attend_back_kernel(
    q, do, lse, delta, lo, kv2, kv1, kv0, dq, d2, d1, d0,
    kvar, vvar, kt, bias, dqt, dk_same, dk_cross, dv_same, dv_cross,
):
    r = pl.program_id(1)

    @pl.when(r == 0)
    def _():
        kcat = jnp.concatenate([kv2[0], kv1[0], kv0[0]], axis=0)
        variants(kvar, kcat)
        kt[...] = kcat.astype(F32).T.astype(BF16)
        vcat = jnp.concatenate([kv2[1], kv1[1], kv0[1]], axis=0)
        variants(vvar, vcat)
        for ref in (dk_same, dk_cross, dv_same, dv_cross):
            ref[...] = jnp.zeros_like(ref)

    bias[...] = bias_of(lo[...], r)
    keys = pl.ds(pl.multiple_of(r * RT, RT), SPAN)
    lane = lax.broadcasted_iota(jnp.int32, (RT, 128), 1)
    for i, (tile, half, kv) in enumerate(HEADS_OF_PAIR):
        cols = slice(tile * 128, (tile + 1) * 128)
        qt = q[:, cols]
        dt = do[:, cols]
        keep = (lane < 64) if half == 0 else (lane >= 64)
        qm = jnp.where(keep, qt, jnp.zeros_like(qt))
        dm = jnp.where(keep, dt, jnp.zeros_like(dt))
        s = nt(kvar[2 * kv + half, keys, :], qt) + bias[...]
        p = jnp.exp(s - lse[i : i + 1, :])
        dp = nt(vvar[2 * kv + half, keys, :], dt)
        ds = (p * (dp - delta[i : i + 1, :])).astype(BF16)
        dk_acc, dv_acc = (dk_same, dv_same) if half == kv else (dk_cross, dv_cross)
        dv_acc[keys, :] += nn(p.astype(BF16), dm)
        dk_acc[keys, :] += nn(ds, qm)
        dqt[i * 64 : (i + 1) * 64, :] = nn(kt[kv * 64 : (kv + 1) * 64, keys], ds)
    dq[...] = dqt[...].T * 0.125

    @pl.when(r == 1)
    def _():
        dk = dk_same[...] + pltpu.roll(dk_cross[...], 64, 1)
        dv = dv_same[...] + pltpu.roll(dv_cross[...], 64, 1)
        d2[0] = dk[0:512].astype(BF16)
        d2[1] = dv[0:512].astype(BF16)
        d1[0] = dk[512:1024].astype(BF16)
        d1[1] = dv[512:1024].astype(BF16)
        d0[0] = dk[1024:1536]
        d0[1] = dv[1024:1536]


def attend_back_call(q, do, lse, delta, lo, kv2, kv1, kv0):
    kvspec = pl.BlockSpec((2, TOK, 128), lambda p, r: (0, 0, p))
    rowspec = pl.BlockSpec((RT, 384), lambda p, r: (r, p))
    statspec = pl.BlockSpec((8, RT), lambda p, r: (p, r))
    acc = pltpu.VMEM((HALO + TOK, 128), F32)
    return pl.pallas_call(
        attend_back_kernel,
        grid=(2, 2),
        out_shape=(
            sds((TOK, HQ), F32),
            sds((2, TOK, HK), BF16),
            sds((2, TOK, HK), BF16),
            sds((2, TOK, HK), F32),
        ),
        in_specs=[
            rowspec,
            rowspec,
            statspec,
            statspec,
            pl.BlockSpec((1, RT), lambda p, r: (0, r)),
            kvspec,
            kvspec,
            kvspec,
        ],
        out_specs=(rowspec, kvspec, kvspec, kvspec),
        scratch_shapes=[
            pltpu.VMEM((4, HALO + TOK, 128), BF16),
            pltpu.VMEM((4, HALO + TOK, 128), BF16),
            pltpu.VMEM((128, HALO + TOK), BF16),
            pltpu.VMEM((SPAN, RT), F32),
            pltpu.VMEM((384, RT), F32),
            acc,
            acc,
            acc,
            acc,
        ],
        compiler_params=params(),
        cost_estimate=pl.CostEstimate(
            flops=10 * 12 * 2 * RT * SPAN * 128, bytes_accessed=6_000_000, transcendentals=0
        ),
        name="attend_back",
    )(q, do, lse, delta, lo, kv2, kv1, kv0)


def out_proj_kernel(offs, att, oi, oo2, w0, w1, w2, w3, w4, part, mid_o, w, sem):
    cs = piece_copies(offs, (w0, w1, w2, w3, w4), w, sem)
    for c in cs:
        c.start()
    a = att[...]
    mid = nt(a, oi[...]).astype(BF16)
    mid_o[...] = mid
    for c in cs:
        c.wait()
    for n in range(6):
        cols = slice(n * 256, (n + 1) * 256)
        part[:, cols] = (nt(a, w[cols, :]) + nn(mid, oo2[:, cols])).astype(BF16)


def out_proj_call(offs, att, oi, oo2, wo):
    return pl.pallas_call(
        out_proj_kernel,
        out_shape=(sds((TOK, D), BF16), sds((TOK, 128), BF16)),
        in_specs=[SM] + [VM] * 3 + [HB] * 5,
        out_specs=(VM, VM),
        scratch_shapes=[pltpu.VMEM((D, HQ), BF16), pltpu.SemaphoreType.DMA((16,))],
        compiler_params=params(),
        cost_estimate=pl.CostEstimate(
            flops=2 * TOK * D * HQ, bytes_accessed=5_000_000, transcendentals=0
        ),
        name="out_proj",
    )(offs, att, oi, oo2, *wo)


def ffn_in_kernel(tok, own, other, gain, a_gu, resid_o, nf_o, mid_o):
    for r in range(4):
        rows = pl.ds(r * 128, 128)
        branch = own[rows, :].astype(F32) + other[rows, :].astype(F32)
        x = tok[rows, :].astype(F32) + RS * branch
        resid_o[rows, :] = x
        inv = lax.rsqrt(jnp.mean(x * x, axis=-1, keepdims=True) + EPS)
        nf_o[rows, :] = (x * inv * gain[...]).astype(BF16)
    mid_o[...] = nt(nf_o[...], a_gu[...]).astype(BF16)


def ffn_in_call(tok, own, other, gain, a_gu):
    return pl.pallas_call(
        ffn_in_kernel,
        out_shape=(sds((TOK, D), F32), sds((TOK, D), BF16), sds((TOK, 128), BF16)),
        in_specs=[VM] * 5,
        out_specs=(VM,) * 3,
        compiler_params=params(),
        cost_estimate=pl.CostEstimate(
            flops=2 * TOK * D * 256, bytes_accessed=10_000_000, transcendentals=0
        ),
        name="ffn_norm",
    )(tok, own, other, gain, a_gu)


def cot_kernel(og, do2, fg_o, mid_o):
    fg_o[...] = (RS * og[...].astype(F32)).astype(BF16)
    mid_o[...] = nt(fg_o[...], do2[...]).astype(BF16)


def cot_call(og, do2):
    return pl.pallas_call(
        cot_kernel,
        out_shape=(sds((TOK, D), BF16), sds((TOK, 128), BF16)),
        in_specs=[VM] * 2,
        out_specs=(VM,) * 2,
        compiler_params=params(),
        cost_estimate=pl.CostEstimate(
            flops=2 * TOK * D * 256, bytes_accessed=4_000_000, transcendentals=0
        ),
        name="branch_cotangent",
    )(og, do2)


def ffn_kernel(width, first, last, *refs):
    offs, nf, fg, mid_gu, mid_dg, bg, bu, di = refs[:8]
    refs = refs[8:]
    w0, w1, w2, w3, w4 = refs[:5]
    refs = refs[5:]
    if last:
        a_gu, do2 = refs[:2]
        refs = refs[2:]
    if not first:
        accf_i, accn_i, midd_i, midg_i = refs[:4]
        refs = refs[4:]
    if last:
        part_f, part_n, gu_in, d_out, gout, uout, din = refs[:7]
        refs = refs[7:]
    else:
        accf_o, accn_o, midd_o, midg_o, gout, uout, din = refs[:7]
        refs = refs[7:]
    w, accf, accn, midd, midg, sem, sem_acc = refs
    cs = piece_copies(offs, (w0, w1, w2, w3, w4), w, sem)
    for c in cs:
        c.start()
    if not first:
        ca = [
            pltpu.make_async_copy(accf_i, accf, sem_acc.at[0]),
            pltpu.make_async_copy(accn_i, accn, sem_acc.at[1]),
        ]
        for c in ca:
            c.start()
        midd[...] = midd_i[...]
        midg[...] = midg_i[...]
    else:
        midd[...] = jnp.zeros_like(midd)
        midg[...] = jnp.zeros_like(midg)
    mid_t = mid_gu[...].astype(F32).T.astype(BF16)
    dg_t = mid_dg[...].astype(F32).T.astype(BF16)
    for c in cs:
        c.wait()
    if not first:
        for c in ca:
            c.wait()
    start = 0
    while start < width:
        n = min(256, width - start)
        blk = slice(start, start + n)
        wg = w[:, start : start + n]
        wu = w[:, width + start : width + start + n]
        wd = w[:, 2 * width + start : 2 * width + start + n]
        g = nn(nf[...], wg) + nn(mid_gu[...], bg[:, blk])
        u = nn(nf[...], wu) + nn(mid_gu[...], bu[:, blk])
        hg = nn(fg[...], wd) + nn(mid_dg[...], di[:, blk])
        sig = 1.0 / (1.0 + jnp.exp(-g))
        si = g * sig
        hid = (si * u).astype(BF16)
        gg = (hg * u * (sig * (1.0 + g * (1.0 - sig)))).astype(BF16)
        ug = (hg * si).astype(BF16)
        gout[:, blk] = 2.0 * nn(mid_t[0:16], gg)
        uout[:, blk] = 2.0 * nn(mid_t[16:32], ug)
        din[:, blk] = nn(dg_t[0:16], hid)
        midd[...] += nt(hid, di[:, blk])
        midg[...] += nt(gg, bg[:, blk]) + nt(ug, bu[:, blk])
        for c0 in range(0, D, 512):
            cols = slice(c0, c0 + 512)
            f = nt(hid, wd[cols, :])
            d = nt(gg, wg[cols, :]) + nt(ug, wu[cols, :])
            if first and start == 0:
                accf[:, cols] = f
                accn[:, cols] = d
            else:
                accf[:, cols] += f
                accn[:, cols] += d
        start += n
    if last:
        midd_b = midd[...].astype(BF16)
        midg_b = midg[...].astype(BF16)
        for c0 in range(0, D, 512):
            cols = slice(c0, c0 + 512)
            part_f[:, cols] = (accf[:, cols] + nn(midd_b, do2[:, cols])).astype(BF16)
            part_n[:, cols] = (accn[:, cols] + nn(midg_b, a_gu[:, cols])).astype(BF16)
        d_out[...] = 2.0 * nn(midd[...].T.astype(BF16)[0:16], fg[...])
        gu_in[...] = nn(midg[...].T.astype(BF16)[0:32], nf[...])
    else:
        co = [
            pltpu.make_async_copy(accf, accf_o, sem_acc.at[0]),
            pltpu.make_async_copy(accn, accn_o, sem_acc.at[1]),
        ]
        for c in co:
            c.start()
        midd_o[...] = midd[...]
        midg_o[...] = midg[...]
        for c in co:
            c.wait()


def ffn_call(width, first, last, offs, nf, fg, mid_gu, mid_dg, bg, bu, di, wp, tail, prev):
    args = [offs, nf, fg, mid_gu, mid_dg, bg, bu, di, *wp]
    specs = [SM] + [VM] * 7 + [HB] * 5
    if last:
        args += list(tail)
        specs += [VM] * 2
    if not first:
        args += list(prev)
        specs += [HB, HB, VM, VM]
    small = [sds((16, width), F32)] * 3
    if last:
        shapes = [sds((TOK, D), BF16)] * 2 + [sds((32, D), F32), sds((16, D), F32)] + small
        ospecs = [VM] * 7
    else:
        shapes = [sds((TOK, D), F32)] * 2 + [sds((TOK, 128), F32)] * 2 + small
        ospecs = [HB, HB] + [VM] * 5

    def body(*refs):
        ffn_kernel(width, first, last, *refs)

    return pl.pallas_call(
        body,
        out_shape=tuple(shapes),
        in_specs=specs,
        out_specs=tuple(ospecs),
        scratch_shapes=[
            pltpu.VMEM((D, 3 * width), BF16),
            pltpu.VMEM((TOK, D), F32),
            pltpu.VMEM((TOK, D), F32),
            pltpu.VMEM((TOK, 128), F32),
            pltpu.VMEM((TOK, 128), F32),
            pltpu.SemaphoreType.DMA((16,)),
            pltpu.SemaphoreType.DMA((2,)),
        ],
        compiler_params=params(),
        cost_estimate=pl.CostEstimate(
            flops=12 * TOK * D * width, bytes_accessed=20_000_000, transcendentals=0
        ),
        name="ffn_chunk",
    )(*args)


def out_back_kernel(
    offs, og, resid, own, other, gain, oi, oo2, mid_att, att, hsel, w0, w1, w2, w3, w4,
    rg_o, do_o, delta_o, oout_o, oin_o, w, abg, sem,
):
    cs = piece_copies(offs, (w0, w1, w2, w3, w4), w, sem)
    for c in cs:
        c.start()
    for r in range(4):
        rows = pl.ds(r * 128, 128)
        x = resid[rows, :]
        inv = lax.rsqrt(jnp.mean(x * x, axis=-1, keepdims=True) + EPS)
        wv = (own[rows, :].astype(F32) + other[rows, :].astype(F32)) * gain[...]
        dot = jnp.mean(wv * x, axis=-1, keepdims=True)
        rg = og[rows, :].astype(F32) + inv * wv - x * (inv * inv * inv * dot)
        rg_o[rows, :] = rg
        abg[rows, :] = (RS * rg).astype(BF16)
    g = abg[...]
    mid_g = nt(g, oo2[...]).astype(BF16)
    oout_o[...] = 2.0 * nn(mid_att[...].astype(F32).T.astype(BF16)[0:16], g)
    oin_o[...] = nn(mid_g.astype(F32).T.astype(BF16)[0:16], att[...])
    for c in cs:
        c.wait()
    delta = jnp.zeros((16, TOK), F32)
    for n in range(3):
        cols = slice(n * 256, (n + 1) * 256)
        dd = (nn(g, w[:, cols]) + nn(mid_g, oi[:, cols])).astype(BF16)
        do_o[:, cols] = dd
        prod = dd.astype(F32) * att[:, cols].astype(F32)
        high = prod.astype(BF16)
        low = (prod - high.astype(F32)).astype(BF16)
        delta = delta + nt(hsel[:, cols], high) + nt(hsel[:, cols], low)
    delta_o[...] = delta


def out_back_call(offs, og, resid, own, other, gain, oi, oo2, mid_att, att, hsel, wo):
    return pl.pallas_call(
        out_back_kernel,
        out_shape=(
            sds((TOK, D), F32),
            sds((TOK, HQ), BF16),
            sds((16, TOK), F32),
            sds((16, D), F32),
            sds((16, HQ), F32),
        ),
        in_specs=[SM] + [VM] * 10 + [HB] * 5,
        out_specs=(VM,) * 5,
        scratch_shapes=[
            pltpu.VMEM((D, HQ), BF16),
            pltpu.VMEM((TOK, D), BF16),
            pltpu.SemaphoreType.DMA((16,)),
        ],
        compiler_params=params(),
        cost_estimate=pl.CostEstimate(
            flops=2 * TOK * D * HQ, bytes_accessed=14_000_000, transcendentals=0
        ),
        name="out_proj_back",
    )(offs, og, resid, own, other, gain, oi, oo2, mid_att, att, hsel, *wo)


def qkv_back_kernel(
    offs_a, offs_b, dq, d0, d1, d2, cos, sin, b2, a1, mid, normed,
    q0, q1, q2, q3, q4, k0, k1, k2, k3, k4,
    part, in_o, out_o, wq, wkv, dall, sem_a, sem_b,
):
    cq = piece_copies(offs_a, (q0, q1, q2, q3, q4), wq, sem_a)
    ck = piece_copies(offs_b, (k0, k1, k2, k3, k4), wkv, sem_b)
    for c in cq + ck:
        c.start()
    cw = jnp.concatenate([cos[...], cos[...]], axis=1)
    sw = jnp.concatenate([sin[...], sin[...]], axis=1)
    for n in range(3):
        g = dq[:, n * 256 : (n + 1) * 256]
        dall[:, n * 256 : (n + 1) * 256] = (g * cw - half_swap(g) * sw).astype(BF16)
    g = d0[0] + d1[0].astype(F32) + d2[0].astype(F32)
    dall[:, 768:1024] = (g * cw - half_swap(g) * sw).astype(BF16)
    dall[:, 1024:1280] = (d0[1] + d1[1].astype(F32) + d2[1].astype(F32)).astype(BF16)
    d = dall[...]
    mid_g = nt(d, b2[...]).astype(BF16)
    mid_t = mid[...].astype(F32).T.astype(BF16)
    out_o[:, 0:768] = 2.0 * nn(mid_t[0:16], dall[:, 0:768])
    out_o[:, 768:1024] = 2.0 * nn(mid_t[16:32], dall[:, 768:1024])
    out_o[:, 1024:1280] = 2.0 * nn(mid_t[32:48], dall[:, 1024:1280])
    in_o[...] = nn(mid_g.astype(F32).T.astype(BF16)[0:48], normed[...])
    for c in cq + ck:
        c.wait()
    for n in range(6):
        cols = slice(n * 256, (n + 1) * 256)
        acc = nt(dall[:, 0:768], wq[cols, :]) + nt(dall[:, 768:1280], wkv[cols, :])
        part[:, cols] = (acc + nn(mid_g, a1[:, cols])).astype(BF16)


def qkv_back_call(offs_a, offs_b, dq, d0, d1, d2, cos, sin, b2, a1, mid, normed, wq, wkv):
    return pl.pallas_call(
        qkv_back_kernel,
        out_shape=(sds((TOK, D), BF16), sds((48, D), F32), sds((16, 1280), F32)),
        in_specs=[SM, SM] + [VM] * 10 + [HB] * 10,
        out_specs=(VM,) * 3,
        scratch_shapes=[
            pltpu.VMEM((D, HQ), BF16),
            pltpu.VMEM((D, 2 * HK), BF16),
            pltpu.VMEM((TOK, 1280), BF16),
            pltpu.SemaphoreType.DMA((16,)),
            pltpu.SemaphoreType.DMA((16,)),
        ],
        compiler_params=params(),
        cost_estimate=pl.CostEstimate(
            flops=2 * TOK * D * 1280, bytes_accessed=12_000_000, transcendentals=0
        ),
        name="qkv_back",
    )(offs_a, offs_b, dq, d0, d1, d2, cos, sin, b2, a1, mid, normed, *wq, *wkv)


def token_grad_kernel(tok, rg, own, other, gain, out):
    for r in range(4):
        rows = pl.ds(r * 128, 128)
        x = tok[rows, :].astype(F32)
        inv = lax.rsqrt(jnp.mean(x * x, axis=-1, keepdims=True) + EPS)
        wv = (own[rows, :].astype(F32) + other[rows, :].astype(F32)) * gain[...]
        dot = jnp.mean(wv * x, axis=-1, keepdims=True)
        out[rows, :] = (rg[rows, :] + inv * wv - x * (inv * inv * inv * dot)).astype(BF16)


def token_grad_call(tok, rg, own, other, gain):
    return pl.pallas_call(
        token_grad_kernel,
        out_shape=sds((TOK, D), BF16),
        in_specs=[VM] * 5,
        out_specs=VM,
        compiler_params=params(),
        cost_estimate=pl.CostEstimate(
            flops=TOK * D * 10, bytes_accessed=9_000_000, transcendentals=0
        ),
        name="token_grad",
    )(tok, rg, own, other, gain)


YLIN = (0, 2, 1, 3)


def go_x(v, step):
    return lax.ppermute(v, "x", [(i, (i + step) % 4) for i in range(4)])


def go_y(v, step):
    return lax.ppermute(
        v, ("tensor", "yh"), [(YLIN[i], YLIN[(i + step) % 4]) for i in range(4)]
    )


def go_z(v, step):
    return lax.ppermute(v, "seq", [(i, (i + step) % 4) for i in range(4)])


def go_core(v):
    return lax.ppermute(v, "core", [(0, 1), (1, 0)])


def to_role(v):
    return lax.ppermute(v, ("tensor", "core"), [(0, 0), (1, 2), (2, 1), (3, 3)])


REL = (0, -1, 1, 2)


def ring_gather(shard, near, far):
    line = jnp.stack([shard, near(shard, 1), near(shard, -1), near(shard, 2)])
    below, above = far(line, 1), far(line, -1)
    return (line, below, above, far(below[:2], 1), far(above[2:], -1))


def offsets(x, y, path):
    out = []
    for far_rel, near_rel in ((0, REL), (-1, REL), (1, REL), (2, REL[:2]), (2, REL[2:])):
        for nr in near_rel:
            if path == "yx":
                out.append(((x + far_rel) % 4) * 4 + (y + nr) % 4)
            else:
                out.append(((x + nr) % 4) * 4 + (y + far_rel) % 4)
    return jnp.stack(out).astype(jnp.int32)


def finish_grads(packed, z, core, index):
    m = packed.shape[1] // 4
    parts = packed.reshape(16, 4, m)
    pick = lambda k: lax.dynamic_index_in_dim(parts, (z + k) % 4, 1, keepdims=False)
    total = pick(0).astype(F32)
    for k in (1, 2, 3):
        total = total + go_z(pick(k), k).astype(F32)
    mine = jnp.concatenate(
        [total.astype(BF16), jnp.full((16, 128), index.astype(BF16), BF16)], axis=1
    )
    line = jnp.stack([mine, go_y(mine, 1), go_y(mine, -1), go_y(mine, 2)])
    plane = jnp.concatenate([line, go_x(line, 1), go_x(line, -1), go_x(line, 2)], axis=0)
    which = plane[:, 0, m].astype(F32)
    onehot = (which[None, :] == jnp.arange(8, dtype=F32)[:, None]).astype(BF16)
    dense = lax.dot_general(
        onehot, plane[:, :, :m], (((1,), (0,)), ((), ())), preferred_element_type=F32
    ).astype(BF16)
    whole = jnp.zeros((4, 8, 16, m), BF16)
    for rel, piece in (
        (0, dense),
        (-1, go_z(dense, 1)),
        (1, go_z(dense, -1)),
        (2, go_z(dense, 2)),
    ):
        whole = lax.dynamic_update_index_in_dim(whole, piece, (z + rel) % 4, 0)
    other = go_core(whole)
    first = jnp.where(core == 0, whole, other)
    second = jnp.where(core == 0, other, whole)
    flat = lambda v: v.transpose(1, 2, 0, 3).reshape(8, 16, 4 * m).astype(F32)
    return flat(first), flat(second)


def core_sum(rep, core):
    low, high = rep[:, :768].astype(BF16), rep[:, 768:].astype(BF16)
    send = jnp.where(core == 0, high, low)
    keep = jnp.where(core == 0, low, high)
    return (keep.astype(F32) + go_core(send).astype(F32)).astype(BF16)


def pad_rows(v, rows=128, at=0):
    return jnp.pad(v, ((at, rows - at - v.shape[0]), (0, 0)))


def shards(
    tokens,
    output_gradient,
    document_length_table,
    sequence_adapter_index,
    sequence_window_length,
    attention_norm_gain,
    feedforward_norm_gain,
    query_projection_weight,
    key_projection_weight,
    value_projection_weight,
    output_projection_weight,
    gate_projection_weight,
    up_projection_weight,
    down_projection_weight,
    query_adapter_first,
    query_adapter_second,
    key_adapter_first,
    key_adapter_second,
    value_adapter_first,
    value_adapter_second,
    output_adapter_first,
    output_adapter_second,
    gate_adapter_first,
    gate_adapter_second,
    up_adapter_first,
    up_adapter_second,
    down_adapter_first,
    down_adapter_second,
):
    z = lax.axis_index("seq")
    yl = lax.axis_index("tensor")
    x = lax.axis_index("x")
    y = lax.axis_index("yh") * 2 + yl
    core = lax.axis_index("core")
    same = core == yl

    w_q = to_role(query_projection_weight)
    w_kv = to_role(jnp.concatenate([key_projection_weight, value_projection_weight], axis=1))
    starts = [sum(CHUNKS[:i]) for i in range(len(CHUNKS))]
    three = (gate_projection_weight, up_projection_weight, down_projection_weight)
    chunk_cols = [
        jnp.concatenate([w[:, s : s + n] for w in three], axis=1)
        for s, n in zip(starts, CHUNKS, strict=True)
    ]
    yx_cols = to_role(
        jnp.concatenate([c for c, p in zip(chunk_cols, CHUNK_PATH) if p == "yx"], axis=1)
    )
    xy_cols = to_role(
        jnp.concatenate(
            [output_projection_weight]
            + [c for c, p in zip(chunk_cols, CHUNK_PATH) if p == "xy"],
            axis=1,
        )
    )
    offs = {"yx": offsets(x, y, "yx"), "xy": offsets(x, y, "xy")}
    full_q = ring_gather(w_q, go_y, go_x)
    full_kv = ring_gather(w_kv, go_x, go_y)
    full_o = ring_gather(xy_cols[:, :HQ], go_x, go_y)
    full_ffn = []
    at = {"yx": 0, "xy": HQ}
    for n, path in zip(CHUNKS, CHUNK_PATH, strict=True):
        src = yx_cols if path == "yx" else xy_cols
        cols = src[:, at[path] : at[path] + 3 * n]
        at[path] += 3 * n
        full_ffn.append(ring_gather(cols, *((go_y, go_x) if path == "yx" else (go_x, go_y))))

    tok_other = go_core(tokens[0])
    tok = jnp.where(same, tokens[0], tok_other)
    og_other = go_core(output_gradient[0])
    og = jnp.where(same, output_gradient[0], og_other)
    meta = jnp.concatenate(
        [document_length_table[0], sequence_adapter_index, sequence_window_length]
    )
    meta = jnp.where(same, meta, go_core(meta))
    lengths, index, window = meta[:4], meta[4], meta[5]
    own_index = sequence_adapter_index[0]
    pick_own = lambda v: lax.dynamic_index_in_dim(v, own_index, 0, keepdims=False)
    pick = lambda v: lax.dynamic_index_in_dim(v, index, 0, keepdims=False)
    halves = to_role(
        jnp.concatenate(
            [
                pick_own(v)
                for v in (
                    query_adapter_second,
                    key_adapter_second,
                    value_adapter_second,
                    output_adapter_first,
                    gate_adapter_second,
                    up_adapter_second,
                    down_adapter_first,
                )
            ],
            axis=1,
        )
    )
    b_q, b_k, b_v, o_i = halves[:, :768], halves[:, 768:1024], halves[:, 1024:1280], halves[:, 1280:2048]
    b_g, b_u, d_i = halves[:, 2048:3968], halves[:, 3968:5888], halves[:, 5888:7808]
    a_q, a_k, a_v, a_g, a_u = (
        pick(v.swapaxes(1, 2))
        for v in (
            query_adapter_first,
            key_adapter_first,
            value_adapter_first,
            gate_adapter_first,
            up_adapter_first,
        )
    )
    o_o, d_o = pick(output_adapter_second), pick(down_adapter_second)
    a_qkv = pad_rows(jnp.concatenate([a_q, a_k, a_v], axis=0))
    b_qkv = 2 * jnp.concatenate(
        [pad_rows(b_q), pad_rows(b_k, at=16), pad_rows(b_v, at=32)], axis=1
    )
    a_gu = pad_rows(jnp.concatenate([a_g, a_u], axis=0))
    bg2, bu2 = pad_rows(2 * b_g), pad_rows(2 * b_u, at=16)
    di_p, oi_p = pad_rows(d_i), pad_rows(o_i)
    oo2, do2 = pad_rows(2 * o_o), pad_rows(2 * d_o)

    ends = jnp.cumsum(lengths, dtype=jnp.int32)
    begins = ends - lengths
    place = z * TOK + jnp.arange(TOK, dtype=jnp.int32)
    begin = jnp.max(jnp.where(place[:, None] >= begins[None, :], begins[None, :], 0), axis=1)
    lo = (jnp.maximum(begin, place - window + 1) - (z * TOK - HALO))[None, :]
    lane = jnp.arange(128, dtype=jnp.int32) % HDIM
    frequency = ROPE_BASE ** (-((lane % 32).astype(F32) * (2.0 / HDIM)))
    angles = (place - begin).astype(F32)[:, None] * frequency[None, :]
    cos = jnp.cos(angles)
    sin = jnp.sin(angles) * jnp.where(lane < 32, -1.0, 1.0)[None, :]

    gain1 = attention_norm_gain[None, :]
    gain2 = feedforward_norm_gain[None, :]

    normed, q, kv0, mid_qkv = qkv_call(
        offs["yx"], offs["xy"], tok, gain1, a_qkv, b_qkv, cos, sin, full_q, full_kv
    )
    kv1 = lax.ppermute(kv0, "seq", [(0, 1), (1, 2), (2, 3)])
    kv2 = lax.ppermute(kv0, "seq", [(0, 2), (1, 3)])
    att, lse = attend_call(q, lo, kv2, kv1, kv0)
    attn_part, mid_att = out_proj_call(offs["xy"], att, oi_p, oo2, full_o)
    attn_other = go_core(attn_part)
    resid, nf, mid_gu = ffn_in_call(tok, attn_part, attn_other, gain2, a_gu)
    fg, mid_dg = cot_call(og, do2)
    prev = None
    couts = []
    for i, (s, n) in enumerate(zip(starts, CHUNKS, strict=True)):
        first, last = i == 0, i == len(CHUNKS) - 1
        res = ffn_call(
            n, first, last, offs[CHUNK_PATH[i]], nf, fg, mid_gu, mid_dg,
            bg2[:, s : s + n], bu2[:, s : s + n], di_p[:, s : s + n], full_ffn[i], (a_gu, do2), prev,
        )
        prev = res[:4]
        couts.append(res[4:])
    ffn_part, nfg_part, gu_in, d_out = prev
    g_out, u_out, d_in = (jnp.concatenate([c[k] for c in couts], axis=1) for k in range(3))
    nfg_other = go_core(nfg_part)
    ffn_other = go_core(ffn_part)
    out = (resid + RS * (ffn_part.astype(F32) + ffn_other.astype(F32))).astype(BF16)
    output = to_role(out)

    hsel = jnp.stack(
        [
            (jnp.arange(HQ) // HDIM == (6 * (r // 8) + r % 8)) & (r % 8 < 6)
            for r in range(16)
        ]
    ).astype(BF16)
    rg, do, delta, o_out, o_in = out_back_call(
        offs["xy"], og, resid, nfg_part, nfg_other, gain2, oi_p, oo2, mid_att, att, hsel, full_o
    )
    dq, d2, d1, d0 = attend_back_call(q, do, lse, delta, lo, kv2, kv1, kv0)
    r1 = lax.ppermute(d1, "seq", [(1, 0), (2, 1), (3, 2)])
    r2 = lax.ppermute(d2, "seq", [(2, 0), (3, 1)])
    na_part, qkv_in, qkv_out = qkv_back_call(
        offs["yx"], offs["xy"], dq, d0, r1, r2, cos, sin, b_qkv, a_qkv, mid_qkv, normed,
        full_q, full_kv,
    )
    na_other = go_core(na_part)
    token_grad = to_role(token_grad_call(tok, rg, na_part, na_other, gain1))

    rep = core_sum(jnp.concatenate([gu_in, d_out, o_out], axis=0), core)
    early = jnp.concatenate(
        [rep[0:16], rep[16:32], rep[32:48], rep[48:64]]
        + [v.astype(BF16) for v in (g_out, u_out, d_in, o_in)]
        + [jnp.zeros((16, 128), BF16)],
        axis=1,
    )
    e0, e1 = finish_grads(early, z, core, index)
    rep = core_sum(qkv_in, core)
    late = jnp.concatenate([rep[0:16], rep[16:32], rep[32:48], qkv_out.astype(BF16)], axis=1)
    l0, l1 = finish_grads(late, z, core, index)

    def join(pair, start, width):
        return jnp.concatenate([v[:, :, start : start + width] for v in pair], axis=2)

    e, l = (e0, e1), (l0, l1)
    g_in_f, u_in_f, d_out_f, o_out_f = (join(e, k * 768, 768) for k in range(4))
    g_out_f = join(e, 3072, 1920)
    u_out_f = join(e, 4992, 1920)
    d_in_f = join(e, 6912, 1920)
    o_in_f = join(e, 8832, 768)
    q_in_f, k_in_f, v_in_f = (join(l, k * 768, 768) for k in range(3))
    q_out_f = join(l, 2304, 768)
    k_out_f = join(l, 3072, 256)
    v_out_f = join(l, 3328, 256)
    t = lambda v: v.swapaxes(1, 2)
    return (
        output[None],
        token_grad[None],
        t(q_in_f),
        q_out_f,
        t(k_in_f),
        k_out_f,
        t(v_in_f),
        v_out_f,
        o_in_f,
        o_out_f,
        t(g_in_f),
        g_out_f,
        t(u_in_f),
        u_out_f,
        d_in_f,
        d_out_f,
    )


def solution(mesh):
    fine = Mesh(mesh.devices.reshape(4, 2, 4, 2, 2), ("seq", "tensor", "x", "yh", "core"))
    fsdp = ("x", "yh", "core")
    weight = P(fsdp, "tensor")
    half = P(None, None, "tensor")
    return jax.shard_map(
        shards,
        mesh=fine,
        in_specs=(
            P(fsdp, "seq", None),
            P(fsdp, "seq", None),
            P(fsdp, None),
            P(fsdp),
            P(fsdp),
            P(),
            P(),
        )
        + (weight,) * 7
        + (P(), half, P(), half, P(), half, half, P(), P(), half, P(), half, half, P()),
        out_specs=(P(fsdp, "seq", None), P(fsdp, "seq", None)) + (P(),) * 14,
        check_vma=False,
    )
```

time: 1180 us -> 708 us (0.60)
  waiting for transfers between devices: 559 us -> 168 us
  matrix products: 232 us -> 4.03 us
  Pallas kernels: 0 us -> 166 us
  starting transfers between devices: 33.4 us -> 179 us
  other arithmetic: 126 us -> 49.9 us
  blocking collectives: 52.1 us -> 0 us
  loops' own time: 21.6 us -> 0 us
    psum x4 -> x0, waiting for transfers between devices: 356 us -> none  [the longest x1 184 us: shards(): lax.psum((padded[0], padded[1], padded[2], padded[3], padded[4], padded[5...]
    dot_general x98 -> x2, matrix products: 232 us -> 4.03 us  [finish_grads(): lax.dot_general(onehot, plane[:, :, :m], (((1,), (0,)), ((), ())), prefer...]
    ppermute x0 -> x95, starting transfers between devices: none -> 179 us  [the longest x12 39.6 us: go_z(): return lax.ppermute(v, 'seq', [(i, (i + step) % 4) for i in range(4)])]
    ppermute x0 -> x95, waiting for transfers between devices: none -> 168 us  [the longest x30 68.4 us: go_x(): return lax.ppermute(v, 'x', [(i, (i + step) % 4) for i in range(4)])]
    pallas_call x0 -> x13, Pallas kernels: none -> 166 us  [the longest x4 68.2 us: ffn_call(): pl.pallas_call(body, out_shape=tuple(shapes), in_specs=specs, out_specs=t...]
    all_gather x5 -> x0, waiting for transfers between devices: 166 us -> none  [the longest x1 61.5 us: shards(): lax.all_gather(gate_projection_weight, 'fsdp', axis=0, tiled=True)]
    all_gather x2 -> x0, blocking collectives: 52.1 us -> none  [the longest x1 29.8 us: shards(): lax.all_gather(value_projection_weight, 'fsdp', axis=0, tiled=True)]
    another operation x9 -> x12, other arithmetic: 47.2 us -> 7.24 us  [the longest x7 3.99 us: ring_gather(): line = jnp.stack([shard, near(shard, 1), near(shard, -1), near(shard, 2)])]
  transfers between devices with their start and end apart: 17 -> 95, of which waited for: 13 -> 28; matrix products, arithmetic and copies ran while one was open for 16% -> 18% of each run, Pallas kernels for 0% -> 20%
where the time goes in v1:
time: 708 us; the launch traced here: 695 us
  starting transfers between devices  179 us (25%)
  waiting for transfers between devices  168 us (24%)
  Pallas kernels  166 us (23%)
  local copies, waits for them, and re-layouts  120 us (17%)
  other arithmetic  49.9 us (7%)
  between operations  7.18 us (1%)
    ppermute x30, waiting for transfers between devices, go_x(): return lax.ppermute(v, 'x', [(i, (i + step) % 4) for i in range(4)])  68.4 us
    pallas_call x4, Pallas kernels, ffn_call(): pl.pallas_call(body, out_shape=tuple(shapes), in_specs=specs, out_specs=t...  68.2 us
    ppermute x31, waiting for transfers between devices, go_y(): lax.ppermute(v, ('tensor', 'yh'), [(YLIN[i], YLIN[(i + step) % 4]) for i...  43.2 us
    ppermute x12, starting transfers between devices, go_z(): return lax.ppermute(v, 'seq', [(i, (i + step) % 4) for i in range(4)])  39.6 us
    ppermute x11, starting transfers between devices, go_core(): return lax.ppermute(v, 'core', [(0, 1), (1, 0)])  38.1 us
    dynamic_update_slice x8, local copies, waits for them, and re-layouts, finish_grads(): whole = lax.dynamic_update_index_in_dim(whole, piece, (z + rel) % 4, 0)  34.5 us
    ppermute x31, starting transfers between devices, go_y(): lax.ppermute(v, ('tensor', 'yh'), [(YLIN[i], YLIN[(i + step) % 4]) for i...  32.2 us
    ppermute x30, starting transfers between devices, go_x(): return lax.ppermute(v, 'x', [(i, (i + step) % 4) for i in range(4)])  31.9 us
  transfers between devices with their start and end apart: 95, of which 28 were waited for; matrix products, arithmetic and copies ran while one was open for 18% of the time, Pallas kernels for 20%

profile of v1, /device:TPU:1, one launch (start us, length us, event | category | flops | bytes accessed | tf_op | source)
XLA Modules:
  0.0 694.8 jit_solution(11605977305830744587)
XLA Ops:
  60.4 10.4 %collective-permute-done.6 = bf16[96,768]{1,0:T(8,128)(2,1)S(1)} collective-permute-done((bf16[96,768]{1,0:T(8,128)(2,1)S(1)}, bf16[96,768]{1,0:T(8,128)(2,1)S(1)}, u32[]{:S(2)}, u32[]{:S(2)}) %collective-permute-start.6) | collective-permute-done | bytes 147488 | tf_op jit(solution)/shard_map/ppermute | solution.py:650
  70.8 7.1 %collective-permute-start.2 = (bf16[16,7808]{1,0:T(8,128)(2,1)S(1)}, bf16[16,7808]{1,0:T(8,128)(2,1)S(1)}, u32[]{:S(2)}, u32[]{:S(2)}) collective-permute-start(bf16[16,7808]{1,0:T(8,128)(2,1)S(1)} %constant_dynamic-update-slice_fusion), channel_id=1, source_target_pairs={{0,0},{1,16},{16,1},{17,17},{2,2},{3,18},{18,3},{19,19},{4,4},{5,2... | collective-permute-start | bytes 749576 | tf_op jit(solution)/shard_map/ppermute | solution.py:664
  87.6 15.7 %collective-permute-done.22 = bf16[96,768]{1,0:T(8,128)(2,1)S(1)} collective-permute-done((bf16[96,768]{1,0:T(8,128)(2,1)S(1)}, bf16[96,768]{1,0:T(8,128)(2,1)S(1)}, u32[]{:S(2)}, u32[]{:S(2)}) %collective-permute-start.22) | collective-permute-done | bytes 147488 | tf_op jit(solution)/shard_map/ppermute | solution.py:646
  108.5 10.0 %collective-permute-done.53 = bf16[96,1536]{1,0:T(8,128)(2,1)S(1)} collective-permute-done((bf16[96,1536]{1,0:T(8,128)(2,1)S(1)}, bf16[96,1536]{1,0:T(8,128)(2,1)S(1)}, u32[]{:S(2)}, u32[]{:S(2)}) %collective-permute-start.53) | collective-permute-done | bytes 294944 | tf_op jit(solution)/shard_map/ppermute | solution.py:650
  119.2 12.6 %collective-permute-done.39 = bf16[96,1536]{1,0:T(8,128)(2,1)S(1)} collective-permute-done((bf16[96,1536]{1,0:T(8,128)(2,1)S(1)}, bf16[96,1536]{1,0:T(8,128)(2,1)S(1)}, u32[]{:S(2)}, u32[]{:S(2)}) %collective-permute-start.39) | collective-permute-done | bytes 294944 | tf_op jit(solution)/shard_map/ppermute | solution.py:650
  135.0 9.9 %collective-permute-done.32 = bf16[96,1152]{1,0:T(8,128)(2,1)S(1)} collective-permute-done((bf16[96,1152]{1,0:T(8,128)(2,1)S(1)}, bf16[96,1152]{1,0:T(8,128)(2,1)S(1)}, u32[]{:S(2)}, u32[]{:S(2)}) %collective-permute-start.32) | collective-permute-done | bytes 221216 | tf_op jit(solution)/shard_map/ppermute | solution.py:646
  149.8 6.2 collective-permute-done.48
  164.8 25.4 %collective-permute-done.33 = bf16[96,1152]{1,0:T(8,128)(2,1)S(1)} collective-permute-done((bf16[96,1152]{1,0:T(8,128)(2,1)S(1)}, bf16[96,1152]{1,0:T(8,128)(2,1)S(1)}, u32[]{:S(2)}, u32[]{:S(2)}) %collective-permute-start.33) | collective-permute-done | bytes 221216 | tf_op jit(solution)/shard_map/ppermute | solution.py:646
  200.2 8.0 %norm_qkv.1 = (bf16[512,1536]{1,0:T(8,128)(2,1)}, bf16[512,768]{1,0:T(8,128)(2,1)}, bf16[2,512,256]{2,1,0:T(8,128)(2,1)}, bf16[512,128]{1,0:T(8,128)(2,1)}) custom-call(s32[16]{0:T(128)} %stack.237.offs_a.refs_0_, s32[16]{0:T(128)} %stack.236.offs_b.offs.refs_0_, bf16[512,1536]{1,0:T(8,128)(2,1)} %broadcast_select_fusion.1.tok, ...), custom_call_target="tpu_custom_call" | custom-call | flops 2013265920 | bytes 9000000 | tf_op jit(solution)/shard_map/norm_qkv/pallas_call | solution.py:107
  222.7 10.1 %collective-permute-done.20.kv1 = bf16[2,512,256]{2,1,0:T(8,128)(2,1)S(1)} collective-permute-done((bf16[2,512,256]{2,1,0:T(8,128)(2,1)}, bf16[2,512,256]{2,1,0:T(8,128)(2,1)S(1)}, u32[]{:S(2)}, u32[]{:S(2)}) %collective-permute-start.20) | collective-permute-done | bytes 524320 | tf_op jit(solution)/shard_map/ppermute | solution.py:865
  233.7 23.6 %attend.1 = (bf16[512,768]{1,0:T(8,128)(2,1)}, f32[16,512]{1,0:T(8,128)}) custom-call(bf16[512,768]{1,0:T(8,128)(2,1)} %get-tuple-element.69.q, s32[1,512]{1,0:T(1,128)} %maximum_subtract_fusion.lo, bf16[2,512,256]{2,1,0:T(8,128)(2,1)} %copy-done.70, bf16[2,512,256]{2,1,0:T(8,128)(2,1)} %copy-done.71, bf16[2,512,256]{2,1,0:T(8,128)(2,1)} %get-tuple-element.70.kv0), custom_call_target="tpu_custom_call" | custom-call | flops 4026531840 | bytes 4000000 | tf_op jit(solution)/shard_map/attend/pallas_call | solution.py:177
  257.3 6.1 out_proj.1
  302.0 15.9 %ffn_chunk.4 = (f32[512,1536]{1,0:T(8,128)}, f32[512,1536]{1,0:T(8,128)}, f32[512,128]{1,0:T(8,128)}, f32[512,128]{1,0:T(8,128)}, f32[16,512]{1,0:T(8,128)}, /*index=5*/f32[16,512]{1,0:T(8,128)}, f32[16,512]{1,0:T(8,128)}) custom-call(s32[16]{0:T(128)} %stack.237.offs_a.refs_0_, bf16[512,1536]{1,0:T(8,128)(2,1)} %get-tuple-element.74.refs_1_, ...), custom_call_target="tpu_custom_call" | custom-call | flops 4831838208 | bytes 20000000 | tf_op jit(solution)/shard_map/ffn_chunk/pallas_call | solution.py:484
  320.8 17.9 %ffn_chunk.5 = (f32[512,1536]{1,0:T(8,128)}, f32[512,1536]{1,0:T(8,128)}, f32[512,128]{1,0:T(8,128)}, f32[512,128]{1,0:T(8,128)}, f32[16,512]{1,0:T(8,128)}, /*index=5*/f32[16,512]{1,0:T(8,128)}, f32[16,512]{1,0:T(8,128)}) custom-call(s32[16]{0:T(128)} %stack.236.offs_b.offs.refs_0_, bf16[512,1536]{1,0:T(8,128)(2,1)} %get-tuple-element.74.refs_1_, ...), custom_call_target="tpu_custom_call" | custom-call | flops 4831838208 | bytes 20000000 | tf_op jit(solution)/shard_map/ffn_chunk/pallas_call | solution.py:484
  339.7 18.0 %ffn_chunk.6 = (f32[512,1536]{1,0:T(8,128)}, f32[512,1536]{1,0:T(8,128)}, f32[512,128]{1,0:T(8,128)}, f32[512,128]{1,0:T(8,128)}, f32[16,512]{1,0:T(8,128)}, /*index=5*/f32[16,512]{1,0:T(8,128)}, f32[16,512]{1,0:T(8,128)}) custom-call(s32[16]{0:T(128)} %stack.237.offs_a.refs_0_, bf16[512,1536]{1,0:T(8,128)(2,1)} %get-tuple-element.74.refs_1_, ...), custom_call_target="tpu_custom_call" | custom-call | flops 4831838208 | bytes 20000000 | tf_op jit(solution)/shard_map/ffn_chunk/pallas_call | solution.py:484
  358.6 16.5 %ffn_chunk.7 = (bf16[512,1536]{1,0:T(8,128)(2,1)}, bf16[512,1536]{1,0:T(8,128)(2,1)}, f32[32,1536]{1,0:T(8,128)}, f32[16,1536]{1,0:T(8,128)}, f32[16,384]{1,0:T(...) custom-call(s32[16]{0:T(128)} %stack.236.offs_b.offs.refs_0_, bf16[512,1536]{1,0:T(8,128)(2,1)} %get-tuple-element.74.refs_1_, ...), custom_call_target="tpu_custom_call" | custom-call | flops 3623878656 | bytes 20000000 | tf_op jit(solution)/shard_map/ffn_chunk/pallas_call | solution.py:484
  375.1 7.8 %collective-permute-start.62 = (bf16[512,1536]{1,0:T(8,128)(2,1)}, bf16[512,1536]{1,0:T(8,128)(2,1)S(1)}, u32[]{:S(2)}, u32[]{:S(2)}) collective-permute-start(bf16[512,1536]{1,0:T(8,128)(2,1)} %get-tuple-element.91.own), channel_id=1, source_target_pairs={{0,1},{1,0},{2,3},{3,2},{4,5},{5,4},{6,7},{7,6},{8,9},{9,8},{10,11... | collective-permute-start | bytes 4718600 | tf_op jit(solution)/shard_map/ppermute | solution.py:660
  387.3 9.6 %out_proj_back.1 = (f32[512,1536]{1,0:T(8,128)}, bf16[512,768]{1,0:T(8,128)(2,1)}, f32[16,512]{1,0:T(8,128)}, f32[16,1536]{1,0:T(8,128)}, f32[16,768]{1,0:T(8,128)}) custom-call(s32[16]{0:T(128)} %stack.236.offs_b.offs.refs_0_, bf16[512,1536]{1,0:T(8,128)(2,1)} %broadcast_select_fusion.og, f32[512,1536]{1,0:T(8,128)} %get-tuple-element.73.resid, ...), custom_call_target="tpu_custom_call" | custom-call | flops 1207959552 | bytes 14000000 | tf_op jit(solution)/shard_map/out_proj_back/pallas_call | solution.py:541
  411.6 25.7 %attend_back.1 = (f32[512,768]{1,0:T(8,128)}, bf16[2,512,256]{2,1,0:T(8,128)(2,1)}, bf16[2,512,256]{2,1,0:T(8,128)(2,1)}, f32[2,512,256]{2,1,0:T(8,128)}) custom-call(bf16[512,768]{1,0:T(8,128)(2,1)} %get-tuple-element.69.q, bf16[512,768]{1,0:T(8,128)(2,1)} %get-tuple-element.94.do, f32[16,512]{1,0:T(8,128)} %get-tuple-element.95.lse, ...), custom_call_target="tpu_custom_call" | custom-call | flops 10066329600 | bytes 6000000 | tf_op jit(solution)/shard_map/attend_back/pallas_call | solution.py:259
  455.3 10.2 %qkv_back.1 = (bf16[512,1536]{1,0:T(8,128)(2,1)}, f32[48,1536]{1,0:T(8,128)}, f32[16,1280]{1,0:T(8,128)}) custom-call(s32[16]{0:T(128)} %stack.237.offs_a.refs_0_, s32[16]{0:T(128)} %stack.236.offs_b.offs.refs_0_, f32[512,768]{1,0:T(8,128)} %get-tuple-element.97.dq, f32[2,512,256]{2,1,0:T(8,128)} %get-tuple-element.98.d0, bf16[2,512,256]{2,1,0:T(8,128)(2,1)} %copy-done.27, ...), custom_call_target="tpu_custom_call" | custom-call | flops 2013265920 | bytes 12000000 | tf_op jit(solution)/shard_map/qkv_back/pallas_call | solution.py:598
  472.7 8.1 %collective-permute-start.68 = (bf16[16,896]{1,0:T(8,128)(2,1)S(1)}, bf16[16,896]{1,0:T(8,128)(2,1)S(1)}, u32[]{:S(2)}, u32[]{:S(2)}) collective-permute-start(bf16[16,896]{1,0:T(8,128)(2,1)S(1)} %bitcast.222), channel_id=1, source_target_pairs={{0,32},{32,64},{64,96},{96,0},{1,33},{33,65},{65,97},{97,1},{2,34}... | collective-permute-start | bytes 86024 | tf_op jit(solution)/shard_map/ppermute | solution.py:656
  480.8 6.4 collective-permute-done.88
  487.1 7.7 %collective-permute-start.69 = (bf16[16,896]{1,0:T(8,128)(2,1)S(1)}, bf16[16,896]{1,0:T(8,128)(2,1)S(1)}, u32[]{:S(2)}, u32[]{:S(2)}) collective-permute-start(bf16[16,896]{1,0:T(8,128)(2,1)S(1)} %bitcast.224), channel_id=1, source_target_pairs={{0,64},{32,96},{64,0},{96,32},{1,65},{33,97},{65,1},{97,33},{2,66}... | collective-permute-start | bytes 86024 | tf_op jit(solution)/shard_map/ppermute | solution.py:656
  530.0 13.0 %collective-permute-start.65 = (bf16[512,1536]{1,0:T(8,128)(2,1)}, bf16[512,1536]{1,0:T(8,128)(2,1)}, u32[]{:S(2)}, u32[]{:S(2)}) collective-permute-start(bf16[512,1536]{1,0:T(8,128)(2,1)} %get-tuple-element.103.own), channel_id=1, source_target_pairs={{0,1},{1,0},{2,3},{3,2},{4,5},{5,4},{6,7},{7,6},{8,9},{9,8},{10,11... | collective-permute-start | bytes 4718600 | tf_op jit(solution)/shard_map/ppermute | solution.py:660
  546.8 16.9 %collective-permute-done.78 = bf16[8,16,896]{2,0,1:T(8,128)(2,1)S(1)} collective-permute-done((bf16[8,16,896]{2,0,1:T(8,128)(2,1)S(1)}, bf16[8,16,896]{2,0,1:T(8,128)(2,1)S(1)}, u32[]{:S(2)}, u32[]{:S(2)}) %collective-permute-start.78) | collective-permute-done | bytes 229408 | tf_op jit(solution)/shard_map/ppermute | solution.py:656
  575.5 10.2 %dynamic_update_slice.29 = bf16[4,8,16,896]{3,0,2,1:T(4,128)(2,1)} dynamic-update-slice(bf16[4,8,16,896]{3,0,2,1:T(4,128)(2,1)} %copy.174, bf16[1,8,16,896]{3,0,2,1:T(2,128)(2,1)S(1)} %copy.175, s32[]{:T(128)S(6)} %select_n.462, s32[]{:T(128)} %constant.403.clone.1, s32[]{:T(128)} %constant.403.clone.1, s32[]{:T(128)} %constant.403.clone.1) | dynamic-update-slice | bytes 458756 | tf_op jit(solution)/shard_map/jit(dynamic_update_index_in_dim)/dynamic_update_slice | solution.py:711
  596.1 16.2 %dynamic_update_slice.33 = bf16[4,8,16,2432]{3,0,2,1:T(4,128)(2,1)S(1)} dynamic-update-slice(bf16[4,8,16,2432]{3,0,2,1:T(4,128)(2,1)S(1)} %copy.188, bf16[1,8,16,2432]{3,0,2,1:T(2,128)(2,1)} %copy.189, s32[]{:T(128)S(6)} %select_n.462, s32[]{:T(128)} %constant.403.clone.1, s32[]{:T(128)} %constant.403.clone.1, s32[]{:T(128)} %constant.403.clone.1) | dynamic-update-slice | bytes 1245188 | tf_op jit(solution)/shard_map/jit(dynamic_update_index_in_dim)/dynamic_update_slice | solution.py:711
  624.9 6.0 token_grad.1
  639.4 13.5 %collective-permute-done.66 = bf16[512,1536]{1,0:T(8,128)(2,1)S(1)} collective-permute-done((bf16[512,1536]{1,0:T(8,128)(2,1)}, bf16[512,1536]{1,0:T(8,128)(2,1)S(1)}, u32[]{:S(2)}, u32[]{:S(2)}) %collective-permute-start.66) | collective-permute-done | bytes 1572896 | tf_op jit(solution)/shard_map/ppermute | solution.py:664
  652.9 7.6 %convert_bitcast_fusion.1 = (f32[8,16,4,2432]{3,2,1,0:T(4,128)}, f32[8,16,4,2432]{3,2,1,0:T(4,128)}) fusion(bf16[4,8,16,2432]{3,0,2,1:T(4,128)(2,1)S(1)} %dynamic_update_slice.33, bf16[4,8,16,2432]{3,0,2,1:T(4,128)(2,1)} %collective-permute-done.94, pred[]{:T(512)S(6)} %eq.295), kind=kLoop, calls=%fused_computation.1 | loop fusion | flops 4980736 | bytes 14942209 | tf_op jit(solution)/shard_map/convert_element_type | solution.py:715
  660.4 6.2 reshape.251
  671.3 6.3 reshape.252
  (503 shorter events, 302.8 us)
Async XLA Ops:
  2.8 31.0 %collective-permute-start.1 = (s32[6]{0:T(128)S(1)}, s32[6]{0:T(128)S(1)}, u32[]{:S(2)}, u32[]{:S(2)}) collective-permute-start(s32[6]{0:T(128)S(1)} %pad_add_fusion), channel_id=1, source_target_pairs={{0,1},{1,0},{2,3},{3,2},{4,5},{5,4},{6,7},{7,6},{8,9},{9,8},{10,11... | collective-permute-start | bytes 80 | tf_op jit(solution)/shard_map/ppermute | solution.py:660
  4.2 42.0 %collective-permute-start.3 = (bf16[96,768]{1,0:T(8,128)(2,1)}, bf16[96,768]{1,0:T(8,128)(2,1)S(1)}, u32[]{:S(2)}, u32[]{:S(2)}) collective-permute-start(bf16[96,768]{1,0:T(8,128)(2,1)} %param.35), channel_id=1, source_target_pairs={{0,0},{1,16},{16,1},{17,17},{2,2},{3,18},{18,3},{19,19},{4,4},{5,2... | collective-permute-start | bytes 442376 | tf_op jit(solution)/shard_map/ppermute | solution.py:664
  8.2 33.8 %collective-permute-start.11 = (bf16[96,512]{1,0:T(8,128)(2,1)S(1)}, bf16[96,512]{1,0:T(8,128)(2,1)S(1)}, u32[]{:S(2)}, u32[]{:S(2)}) collective-permute-start(bf16[96,512]{1,0:T(8,128)(2,1)S(1)} %pad_maximum_fusion.19), channel_id=1, source_target_pairs={{0,0},{1,16},{16,1},{17,17},{2,2},{3,18},{18,3},{19,19},{4,4},{5,2... | collective-permute-start | bytes 294920 | tf_op jit(solution)/shard_map/ppermute | solution.py:664
  22.7 56.6 %collective-permute-start.21 = (bf16[96,3456]{1,0:T(8,128)(2,1)}, bf16[96,3456]{1,0:T(8,128)(2,1)S(1)}, u32[]{:S(2)}, u32[]{:S(2)}) collective-permute-start(bf16[96,3456]{1,0:T(8,128)(2,1)} %constant_dynamic-update-slice_fusion.7), channel_id=1, source_target_pairs={{0,0},{1,16},{16,1},{17,17},{2,2},{3,18},{18,3},{19,19},{4,4},{5,2... | collective-permute-start | bytes 1990664 | tf_op jit(solution)/shard_map/ppermute | solution.py:664
  47.1 35.5 %collective-permute-start.38 = (bf16[96,3072]{1,0:T(8,128)(2,1)}, bf16[96,3072]{1,0:T(8,128)(2,1)S(1)}, u32[]{:S(2)}, u32[]{:S(2)}) collective-permute-start(bf16[96,3072]{1,0:T(8,128)(2,1)} %get-tuple-element.164), channel_id=1, source_target_pairs={{0,0},{1,16},{16,1},{17,17},{2,2},{3,18},{18,3},{19,19},{4,4},{5,2... | collective-permute-start | bytes 1769480 | tf_op jit(solution)/shard_map/ppermute | solution.py:664
  78.0 28.5 %collective-permute-start.8 = (bf16[4,96,768]{2,1,0:T(8,128)(2,1)S(1)}, bf16[4,96,768]{2,1,0:T(8,128)(2,1)S(1)}, u32[]{:S(2)}, u32[]{:S(2)}) collective-permute-start(bf16[4,96,768]{2,1,0:T(8,128)(2,1)S(1)} %pad_maximum_fusion.11.q0), channel_id=1, source_target_pairs={{0,12},{4,0},{8,4},{12,8},{1,13},{5,1},{9,5},{13,9},{2,14},{6,2},{... | collective-permute-start | bytes 1769480 | tf_op jit(solution)/shard_map/ppermute | solution.py:646
  106.6 83.8 %collective-permute-start = (bf16[512,1536]{1,0:T(8,128)(2,1)S(1)}, bf16[512,1536]{1,0:T(8,128)(2,1)S(1)}, u32[]{:S(2)}, u32[]{:S(2)}) collective-permute-start(bf16[512,1536]{1,0:T(8,128)(2,1)S(1)} %bitcast.185), channel_id=1, source_target_pairs={{0,1},{1,0},{2,3},{3,2},{4,5},{5,4},{6,7},{7,6},{8,9},{9,8},{10,11... | collective-permute-start | bytes 4718600 | tf_op jit(solution)/shard_map/ppermute | solution.py:660
  144.9 52.5 %collective-permute-start.30 = (bf16[512,1536]{1,0:T(8,128)(2,1)S(1)}, bf16[512,1536]{1,0:T(8,128)(2,1)S(1)}, u32[]{:S(2)}, u32[]{:S(2)}) collective-permute-start(bf16[512,1536]{1,0:T(8,128)(2,1)S(1)} %bitcast.186), channel_id=1, source_target_pairs={{0,1},{1,0},{2,3},{3,2},{4,5},{5,4},{6,7},{7,6},{8,9},{9,8},{10,11... | collective-permute-start | bytes 4718600 | tf_op jit(solution)/shard_map/ppermute | solution.py:660
  156.1 34.2 %collective-permute-start.10 = (bf16[2,96,768]{2,1,0:T(8,128)(2,1)S(1)}, bf16[2,96,768]{2,1,0:T(8,128)(2,1)S(1)}, u32[]{:S(2)}, u32[]{:S(2)}) collective-permute-start(bf16[2,96,768]{2,1,0:T(8,128)(2,1)S(1)} %slice.392), channel_id=1, source_target_pairs={{0,12},{4,0},{8,4},{12,8},{1,13},{5,1},{9,5},{13,9},{2,14},{6,2},{... | collective-permute-start | bytes 884744 | tf_op jit(solution)/shard_map/ppermute | solution.py:646
  159.5 54.5 %collective-permute-start.56 = (bf16[4,96,1536]{2,1,0:T(8,128)(2,1)}, bf16[4,96,1536]{2,1,0:T(8,128)(2,1)}, u32[]{:S(2)}, u32[]{:S(2)}) collective-permute-start(bf16[4,96,1536]{2,1,0:T(8,128)(2,1)} %pad_maximum_fusion.5.refs_8_), channel_id=1, source_target_pairs={{0,4},{4,8},{8,12},{12,0},{1,5},{5,9},{9,13},{13,1},{2,6},{6,10},{... | collective-permute-start | bytes 3538952 | tf_op jit(solution)/shard_map/ppermute | solution.py:646
  162.5 27.7 %collective-permute-start.33 = (bf16[96,1152]{1,0:T(8,128)(2,1)S(1)}, bf16[96,1152]{1,0:T(8,128)(2,1)S(1)}, u32[]{:S(2)}, u32[]{:S(2)}) collective-permute-start(bf16[96,1152]{1,0:T(8,128)(2,1)S(1)} %get-tuple-element.157), channel_id=1, source_target_pairs={{0,8},{4,12},{8,0},{12,4},{1,9},{5,13},{9,1},{13,5},{2,10},{6,14},... | collective-permute-start | bytes 663560 | tf_op jit(solution)/shard_map/ppermute | solution.py:646
  197.5 66.0 %collective-permute-start.57 = (bf16[4,96,1536]{2,1,0:T(8,128)(2,1)}, bf16[4,96,1536]{2,1,0:T(8,128)(2,1)}, u32[]{:S(2)}, u32[]{:S(2)}) collective-permute-start(bf16[4,96,1536]{2,1,0:T(8,128)(2,1)} %pad_maximum_fusion.5.refs_8_), channel_id=1, source_target_pairs={{0,12},{4,0},{8,4},{12,8},{1,13},{5,1},{9,5},{13,9},{2,14},{6,2},{... | collective-permute-start | bytes 3538952 | tf_op jit(solution)/shard_map/ppermute | solution.py:646
  197.5 66.0 %collective-permute-start.49 = (bf16[4,96,1536]{2,1,0:T(8,128)(2,1)}, bf16[4,96,1536]{2,1,0:T(8,128)(2,1)}, u32[]{:S(2)}, u32[]{:S(2)}) collective-permute-start(bf16[4,96,1536]{2,1,0:T(8,128)(2,1)} %pad_maximum_fusion.4.refs_8_), channel_id=1, source_target_pairs={{0,16},{16,2},{2,18},{18,0},{1,17},{17,3},{3,19},{19,1},{4,20},{20... | collective-permute-start | bytes 3538952 | tf_op jit(solution)/shard_map/ppermute | solution.py:650
  197.6 68.6 %collective-permute-start.50 = (bf16[4,96,1536]{2,1,0:T(8,128)(2,1)}, bf16[4,96,1536]{2,1,0:T(8,128)(2,1)}, u32[]{:S(2)}, u32[]{:S(2)}) collective-permute-start(bf16[4,96,1536]{2,1,0:T(8,128)(2,1)} %pad_maximum_fusion.4.refs_8_), channel_id=1, source_target_pairs={{0,18},{16,0},{2,16},{18,2},{1,19},{17,1},{3,17},{19,3},{4,22},{20... | collective-permute-start | bytes 3538952 | tf_op jit(solution)/shard_map/ppermute | solution.py:650
  221.6 62.4 %collective-permute-start.42 = (bf16[4,96,1536]{2,1,0:T(8,128)(2,1)}, bf16[4,96,1536]{2,1,0:T(8,128)(2,1)}, u32[]{:S(2)}, u32[]{:S(2)}) collective-permute-start(bf16[4,96,1536]{2,1,0:T(8,128)(2,1)} %pad_maximum_fusion.3.refs_8_), channel_id=1, source_target_pairs={{0,4},{4,8},{8,12},{12,0},{1,5},{5,9},{9,13},{13,1},{2,6},{6,10},{... | collective-permute-start | bytes 3538952 | tf_op jit(solution)/shard_map/ppermute | solution.py:646
  232.8 51.1 %collective-permute-start.43 = (bf16[4,96,1536]{2,1,0:T(8,128)(2,1)}, bf16[4,96,1536]{2,1,0:T(8,128)(2,1)}, u32[]{:S(2)}, u32[]{:S(2)}) collective-permute-start(bf16[4,96,1536]{2,1,0:T(8,128)(2,1)} %pad_maximum_fusion.3.refs_8_), channel_id=1, source_target_pairs={{0,12},{4,0},{8,4},{12,8},{1,13},{5,1},{9,5},{13,9},{2,14},{6,2},{... | collective-permute-start | bytes 3538952 | tf_op jit(solution)/shard_map/ppermute | solution.py:646
  266.2 27.1 %collective-permute-start.29 = (bf16[512,1536]{1,0:T(8,128)(2,1)}, bf16[512,1536]{1,0:T(8,128)(2,1)}, u32[]{:S(2)}, u32[]{:S(2)}) collective-permute-start(bf16[512,1536]{1,0:T(8,128)(2,1)} %get-tuple-element.72.own), channel_id=1, source_target_pairs={{0,1},{1,0},{2,3},{3,2},{4,5},{5,4},{6,7},{7,6},{8,9},{9,8},{10,11... | collective-permute-start | bytes 4718600 | tf_op jit(solution)/shard_map/ppermute | solution.py:660
  284.0 33.9 %collective-permute-start.51 = (bf16[2,96,1536]{2,1,0:T(8,128)(2,1)S(1)}, bf16[2,96,1536]{2,1,0:T(8,128)(2,1)}, u32[]{:S(2)}, u32[]{:S(2)}) collective-permute-start(bf16[2,96,1536]{2,1,0:T(8,128)(2,1)S(1)} %slice.409), channel_id=1, source_target_pairs={{0,16},{16,2},{2,18},{18,0},{1,17},{17,3},{3,19},{19,1},{4,20},{20... | collective-permute-start | bytes 1769480 | tf_op jit(solution)/shard_map/ppermute | solution.py:650
  284.0 36.8 %collective-permute-start.52 = (bf16[2,96,1536]{2,1,0:T(8,128)(2,1)S(1)}, bf16[2,96,1536]{2,1,0:T(8,128)(2,1)}, u32[]{:S(2)}, u32[]{:S(2)}) collective-permute-start(bf16[2,96,1536]{2,1,0:T(8,128)(2,1)S(1)} %slice.410), channel_id=1, source_target_pairs={{0,18},{16,0},{2,16},{18,2},{1,19},{17,1},{3,17},{19,3},{4,22},{20... | collective-permute-start | bytes 1769480 | tf_op jit(solution)/shard_map/ppermute | solution.py:650
  293.3 64.3 %collective-permute-start.36 = (bf16[2,96,1152]{2,1,0:T(8,128)(2,1)S(1)}, bf16[2,96,1152]{2,1,0:T(8,128)(2,1)S(1)}, u32[]{:S(2)}, u32[]{:S(2)}) collective-permute-start(bf16[2,96,1152]{2,1,0:T(8,128)(2,1)S(1)} %slice.403), channel_id=1, source_target_pairs={{0,16},{16,2},{2,18},{18,0},{1,17},{17,3},{3,19},{19,1},{4,20},{20... | collective-permute-start | bytes 1327112 | tf_op jit(solution)/shard_map/ppermute | solution.py:650
  298.9 39.8 %collective-permute-start.44 = (bf16[2,96,1536]{2,1,0:T(8,128)(2,1)S(1)}, bf16[2,96,1536]{2,1,0:T(8,128)(2,1)S(1)}, u32[]{:S(2)}, u32[]{:S(2)}) collective-permute-start(bf16[2,96,1536]{2,1,0:T(8,128)(2,1)S(1)} %slice.406), channel_id=1, source_target_pairs={{0,4},{4,8},{8,12},{12,0},{1,5},{5,9},{9,13},{13,1},{2,6},{6,10},{... | collective-permute-start | bytes 1769480 | tf_op jit(solution)/shard_map/ppermute | solution.py:646
  299.3 39.4 %collective-permute-start.45 = (bf16[2,96,1536]{2,1,0:T(8,128)(2,1)S(1)}, bf16[2,96,1536]{2,1,0:T(8,128)(2,1)S(1)}, u32[]{:S(2)}, u32[]{:S(2)}) collective-permute-start(bf16[2,96,1536]{2,1,0:T(8,128)(2,1)S(1)} %slice.407), channel_id=1, source_target_pairs={{0,12},{4,0},{8,4},{12,8},{1,13},{5,1},{9,5},{13,9},{2,14},{6,2},{... | collective-permute-start | bytes 1769480 | tf_op jit(solution)/shard_map/ppermute | solution.py:646
  317.9 39.8 %collective-permute-start.37 = (bf16[2,96,1152]{2,1,0:T(8,128)(2,1)S(1)}, bf16[2,96,1152]{2,1,0:T(8,128)(2,1)S(1)}, u32[]{:S(2)}, u32[]{:S(2)}) collective-permute-start(bf16[2,96,1152]{2,1,0:T(8,128)(2,1)S(1)} %slice.404), channel_id=1, source_target_pairs={{0,18},{16,0},{2,16},{18,2},{1,19},{17,1},{3,17},{19,3},{4,22},{20... | collective-permute-start | bytes 1327112 | tf_op jit(solution)/shard_map/ppermute | solution.py:650
  401.1 38.9 %collective-permute-start.82 = (bf16[16,2432]{1,0:T(8,128)(2,1)S(1)}, bf16[16,2432]{1,0:T(8,128)(2,1)S(1)}, u32[]{:S(2)}, u32[]{:S(2)}) collective-permute-start(bf16[16,2432]{1,0:T(8,128)(2,1)S(1)} %bitcast.216), channel_id=1, source_target_pairs={{0,32},{32,64},{64,96},{96,0},{1,33},{33,65},{65,97},{97,1},{2,34}... | collective-permute-start | bytes 233480 | tf_op jit(solution)/shard_map/ppermute | solution.py:656
  406.8 33.1 %collective-permute-start.83 = (bf16[16,2432]{1,0:T(8,128)(2,1)S(1)}, bf16[16,2432]{1,0:T(8,128)(2,1)S(1)}, u32[]{:S(2)}, u32[]{:S(2)}) collective-permute-start(bf16[16,2432]{1,0:T(8,128)(2,1)S(1)} %bitcast.217), channel_id=1, source_target_pairs={{0,64},{32,96},{64,0},{96,32},{1,65},{33,97},{65,1},{97,33},{2,66}... | collective-permute-start | bytes 233480 | tf_op jit(solution)/shard_map/ppermute | solution.py:656
  409.5 30.5 %collective-permute-start.84 = (bf16[16,2432]{1,0:T(8,128)(2,1)S(1)}, bf16[16,2432]{1,0:T(8,128)(2,1)S(1)}, u32[]{:S(2)}, u32[]{:S(2)}) collective-permute-start(bf16[16,2432]{1,0:T(8,128)(2,1)S(1)} %bitcast.218), channel_id=1, source_target_pairs={{0,96},{32,0},{64,32},{96,64},{1,97},{33,1},{65,33},{97,65},{2,98}... | collective-permute-start | bytes 233480 | tf_op jit(solution)/shard_map/ppermute | solution.py:656
  444.6 76.4 %collective-permute-start.60 = (bf16[512,1536]{1,0:T(8,128)(2,1)}, bf16[512,1536]{1,0:T(8,128)(2,1)}, u32[]{:S(2)}, u32[]{:S(2)}) collective-permute-start(bf16[512,1536]{1,0:T(8,128)(2,1)} %get-tuple-element.90), channel_id=1, source_target_pairs={{0,1},{1,0},{2,3},{3,2},{4,5},{5,4},{6,7},{7,6},{8,9},{9,8},{10,11... | collective-permute-start | bytes 4718600 | tf_op jit(solution)/shard_map/ppermute | solution.py:660
  514.0 71.7 %collective-permute-start.91 = (bf16[8,16,2432]{2,0,1:T(8,128)(2,1)}, bf16[8,16,2432]{2,0,1:T(8,128)(2,1)}, u32[]{:S(2)}, u32[]{:S(2)}) collective-permute-start(bf16[8,16,2432]{2,0,1:T(8,128)(2,1)} %get-tuple-element.208), channel_id=1, source_target_pairs={{0,32},{32,64},{64,96},{96,0},{1,33},{33,65},{65,97},{97,1},{2,34}... | collective-permute-start | bytes 1867784 | tf_op jit(solution)/shard_map/ppermute | solution.py:656
  524.7 87.7 %collective-permute-start.61 = (bf16[512,1536]{1,0:T(8,128)(2,1)}, bf16[512,1536]{1,0:T(8,128)(2,1)}, u32[]{:S(2)}, u32[]{:S(2)}) collective-permute-start(bf16[512,1536]{1,0:T(8,128)(2,1)} %add_convert_fusion), channel_id=1, source_target_pairs={{0,0},{1,16},{16,1},{17,17},{2,2},{3,18},{18,3},{19,19},{4,4},{5,2... | collective-permute-start | bytes 4718600 | tf_op jit(solution)/shard_map/ppermute | solution.py:664
  530.0 94.9 %collective-permute-start.65 = (bf16[512,1536]{1,0:T(8,128)(2,1)}, bf16[512,1536]{1,0:T(8,128)(2,1)}, u32[]{:S(2)}, u32[]{:S(2)}) collective-permute-start(bf16[512,1536]{1,0:T(8,128)(2,1)} %get-tuple-element.103.own), channel_id=1, source_target_pairs={{0,1},{1,0},{2,3},{3,2},{4,5},{5,4},{6,7},{7,6},{8,9},{9,8},{10,11... | collective-permute-start | bytes 4718600 | tf_op jit(solution)/shard_map/ppermute | solution.py:660
  542.9 46.7 %collective-permute-start.92 = (bf16[8,16,2432]{2,0,1:T(8,128)(2,1)}, bf16[8,16,2432]{2,0,1:T(8,128)(2,1)S(1)}, u32[]{:S(2)}, u32[]{:S(2)}) collective-permute-start(bf16[8,16,2432]{2,0,1:T(8,128)(2,1)} %get-tuple-element.208), channel_id=1, source_target_pairs={{0,96},{32,0},{64,32},{96,64},{1,97},{33,1},{65,33},{97,65},{2,98}... | collective-permute-start | bytes 1867784 | tf_op jit(solution)/shard_map/ppermute | solution.py:656
  612.3 40.6 %collective-permute-start.94 = (bf16[4,8,16,2432]{3,0,2,1:T(4,128)(2,1)S(1)}, bf16[4,8,16,2432]{3,0,2,1:T(4,128)(2,1)}, u32[]{:S(2)}, u32[]{:S(2)}) collective-permute-start(bf16[4,8,16,2432]{3,0,2,1:T(4,128)(2,1)S(1)} %dynamic_update_slice.33), channel_id=1, source_target_pairs={{0,1},{1,0},{2,3},{3,2},{4,5},{5,4},{6,7},{7,6},{8,9},{9,8},{10,11... | collective-permute-start | bytes 7471112 | tf_op jit(solution)/shard_map/ppermute | solution.py:660
  (135 other events, 1777.3 us)

commit v2 on v1

v2 whole, which is shorter than its diff:
```python
import jax
import jax.numpy as jnp
import numpy as np
from jax import lax
from jax.experimental import pallas as pl
from jax.experimental.pallas import tpu as pltpu
from jax.sharding import Mesh
from jax.sharding import PartitionSpec as P

F32 = jnp.float32
BF16 = jnp.bfloat16
EPS = 1e-05
ROPE_BASE = 10000.0
RS = 1.4 / 52.0**0.5
MASKED = -1e30
TOK = 512
D = 1536
DX = D + 128
HQ = 768
HK = 256
HDIM = 64
SPAN = 1280
RT = 256
HALO = 1024
FH = 1920
FA, FB, FC = 640, 640, 640
EARLY = 2048
LATE = 1280


def nn(a, b):
    return lax.dot_general(a, b, (((1,), (0,)), ((), ())), preferred_element_type=F32)


def nt(a, b):
    return lax.dot_general(a, b, (((1,), (1,)), ((), ())), preferred_element_type=F32)


def tn(a, b):
    return lax.dot_general(a, b, (((0,), (0,)), ((), ())), preferred_element_type=F32)


VM = pl.BlockSpec(memory_space=pltpu.VMEM)
SM = pl.BlockSpec(memory_space=pltpu.SMEM)
HB = pl.BlockSpec(memory_space=pl.ANY)


def row_block(width):
    return pl.BlockSpec((128, width), lambda i: (i, 0))


def all_block(rows, width):
    return pl.BlockSpec((rows, width), lambda i: (0, 0))


def params():
    return pltpu.CompilerParams(vmem_limit_bytes=58 * 1024 * 1024)


def cost():
    return pl.CostEstimate(flops=1, bytes_accessed=1, transcendentals=0)


def sds(shape, dtype):
    return jax.ShapeDtypeStruct(shape, dtype)


def piece_copies(offs, refs, dst, sems):
    copies = []
    for ref in refs:
        for k in range(ref.shape[0]):
            row = pl.multiple_of(offs[len(copies)] * 96, 96)
            copies.append(
                pltpu.make_async_copy(ref.at[k], dst.at[pl.ds(row, 96)], sems.at[len(copies)])
            )
    return copies


def half_swap(v, sign=1):
    lane = lax.broadcasted_iota(jnp.int32, v.shape, 1)
    width = v.shape[1]
    from_low = pltpu.roll(v, 32, 1)
    from_high = pltpu.roll(v, width - 32, 1)
    return jnp.where((lane % 64) < 32, from_high, from_low)


def qkv_kernel(offs, tok, gain, a1, b2, cos, sin, *refs):
    pieces, (normed_o, q_o, kv_o, mid_o, w, sem) = refs[:5], refs[5:]
    cs = piece_copies(offs, pieces, w, sem)
    for c in cs:
        c.start()
    for r in range(4):
        rows = pl.ds(r * 128, 128)
        x = tok[rows, :].astype(F32)
        inv = lax.rsqrt(jnp.mean(x * x, axis=-1, keepdims=True) + EPS)
        normed_o[rows, :] = (x * inv * gain[...]).astype(BF16)
    normed = normed_o[...]
    mid = nt(normed, a1[...]).astype(BF16)
    mid_o[...] = mid
    for c in cs:
        c.wait()
    cw = jnp.concatenate([cos[...], cos[...]], axis=1)
    sw = jnp.concatenate([sin[...], sin[...]], axis=1)
    for n in (3, 4, 0, 1, 2):
        cols = slice(n * 256, (n + 1) * 256)
        acc = nn(normed, w[:, cols]) + nn(mid, b2[:, cols])
        if n < 4:
            acc = acc * cw + half_swap(acc) * sw
        if n < 3:
            q_o[:, cols] = (acc.astype(BF16).astype(F32) * 0.125).astype(BF16)
        else:
            kv_o[n - 3] = acc.astype(BF16)


def qkv_call(offs, tok, gain, a1, b2, cos, sin, w):
    return pl.pallas_call(
        qkv_kernel,
        out_shape=(
            sds((TOK, D), BF16),
            sds((TOK, HQ), BF16),
            sds((2, TOK, HK), BF16),
            sds((TOK, 128), BF16),
        ),
        in_specs=[SM] + [VM] * 6 + [HB] * 5,
        out_specs=(VM,) * 4,
        scratch_shapes=[pltpu.VMEM((D, 1280), BF16), pltpu.SemaphoreType.DMA((16,))],
        compiler_params=params(),
        cost_estimate=cost(),
        name="norm_qkv",
    )(offs, tok, gain, a1, b2, cos, sin, *w)


HEADS_OF_PAIR = ((0, 0, 0), (0, 1, 0), (1, 0, 0), (1, 1, 1), (2, 0, 1), (2, 1, 1))


def bias_of(lo, r):
    key = lax.broadcasted_iota(jnp.int32, (SPAN, RT), 0) + r * RT
    row = lax.broadcasted_iota(jnp.int32, (SPAN, RT), 1) + r * RT + HALO
    return jnp.where((key >= lo) & (key <= row), 0.0, MASKED)


def variants(dst, src):
    lane = lax.broadcasted_iota(jnp.int32, src.shape, 1)
    srcf = src.astype(F32)
    rolled = pltpu.roll(srcf, 64, 1)
    low = lane < 64
    dst[0] = jnp.where(low, srcf, 0.0).astype(BF16)
    dst[1] = jnp.where(low, 0.0, rolled).astype(BF16)
    dst[2] = jnp.where(low, rolled, 0.0).astype(BF16)
    dst[3] = jnp.where(low, 0.0, srcf).astype(BF16)


def attend_kernel(q, lo, kv2, kv1, kv0, out, lse, kvar, vt, bias, ot):
    r = pl.program_id(1)

    @pl.when(r == 0)
    def _():
        kcat = jnp.concatenate([kv2[0], kv1[0], kv0[0]], axis=0)
        variants(kvar, kcat)
        vcat = jnp.concatenate([kv2[1], kv1[1], kv0[1]], axis=0)
        vt[...] = vcat.astype(F32).T.astype(BF16)

    bias[...] = bias_of(lo[...], r)
    keys = pl.ds(pl.multiple_of(r * RT, RT), SPAN)
    for i, (tile, half, kv) in enumerate(HEADS_OF_PAIR):
        qt = q[:, tile * 128 : (tile + 1) * 128]
        s = nt(kvar[2 * kv + half, keys, :], qt) + bias[...]
        m = jnp.max(s, axis=0, keepdims=True)
        e = jnp.exp(s - m)
        total = jnp.sum(e, axis=0, keepdims=True)
        o = nn(vt[kv * 64 : (kv + 1) * 64, keys], e.astype(BF16))
        ot[i * 64 : (i + 1) * 64, :] = o * (1.0 / total)
        lse[i : i + 1, :] = m + jnp.log(total)
    out[...] = ot[...].T.astype(BF16)


def attend_call(q, lo, kv2, kv1, kv0):
    kvspec = pl.BlockSpec((2, TOK, 128), lambda p, r: (0, 0, p))
    return pl.pallas_call(
        attend_kernel,
        grid=(2, 2),
        out_shape=(sds((TOK, HQ), BF16), sds((16, TOK), F32)),
        in_specs=[
            pl.BlockSpec((RT, 384), lambda p, r: (r, p)),
            pl.BlockSpec((1, RT), lambda p, r: (0, r)),
            kvspec,
            kvspec,
            kvspec,
        ],
        out_specs=(
            pl.BlockSpec((RT, 384), lambda p, r: (r, p)),
            pl.BlockSpec((8, RT), lambda p, r: (p, r)),
        ),
        scratch_shapes=[
            pltpu.VMEM((4, HALO + TOK, 128), BF16),
            pltpu.VMEM((128, HALO + TOK), BF16),
            pltpu.VMEM((SPAN, RT), F32),
            pltpu.VMEM((384, RT), F32),
        ],
        compiler_params=params(),
        cost_estimate=cost(),
        name="attend",
    )(q, lo, kv2, kv1, kv0)


def attend_back_kernel(
    q, do, lse, delta, lo, kv2, kv1, kv0, dq, d2, d1, d0,
    kvar, vvar, kt, bias, dqt, dk_same, dk_cross, dv_same, dv_cross,
):
    r = pl.program_id(1)

    @pl.when(r == 0)
    def _():
        kcat = jnp.concatenate([kv2[0], kv1[0], kv0[0]], axis=0)
        variants(kvar, kcat)
        kt[...] = kcat.astype(F32).T.astype(BF16)
        vcat = jnp.concatenate([kv2[1], kv1[1], kv0[1]], axis=0)
        variants(vvar, vcat)
        for ref in (dk_same, dk_cross, dv_same, dv_cross):
            ref[...] = jnp.zeros_like(ref)

    bias[...] = bias_of(lo[...], r)
    keys = pl.ds(pl.multiple_of(r * RT, RT), SPAN)
    lane = lax.broadcasted_iota(jnp.int32, (RT, 128), 1)
    for i, (tile, half, kv) in enumerate(HEADS_OF_PAIR):
        cols = slice(tile * 128, (tile + 1) * 128)
        qt = q[:, cols]
        dt = do[:, cols]
        keep = (lane < 64) if half == 0 else (lane >= 64)
        qm = jnp.where(keep, qt, jnp.zeros_like(qt))
        dm = jnp.where(keep, dt, jnp.zeros_like(dt))
        s = nt(kvar[2 * kv + half, keys, :], qt) + bias[...]
        p = jnp.exp(s - lse[i : i + 1, :])
        dp = nt(vvar[2 * kv + half, keys, :], dt)
        ds = (p * (dp - delta[i : i + 1, :])).astype(BF16)
        dk_acc, dv_acc = (dk_same, dv_same) if half == kv else (dk_cross, dv_cross)
        dv_acc[keys, :] += nn(p.astype(BF16), dm)
        dk_acc[keys, :] += nn(ds, qm)
        dqt[i * 64 : (i + 1) * 64, :] = nn(kt[kv * 64 : (kv + 1) * 64, keys], ds)
    dq[...] = dqt[...].T * 0.125

    @pl.when(r == 1)
    def _():
        dk = dk_same[...] + pltpu.roll(dk_cross[...], 64, 1)
        dv = dv_same[...] + pltpu.roll(dv_cross[...], 64, 1)
        d2[0] = dk[0:512].astype(BF16)
        d2[1] = dv[0:512].astype(BF16)
        d1[0] = dk[512:1024].astype(BF16)
        d1[1] = dv[512:1024].astype(BF16)
        d0[0] = dk[1024:1536]
        d0[1] = dv[1024:1536]


def attend_back_call(p, q, do, lse, delta, lo, kv2, kv1, kv0):
    kvspec = pl.BlockSpec((2, TOK, 128), lambda i, r: (0, 0, p))
    rowspec = pl.BlockSpec((RT, 384), lambda i, r: (r, p))
    statspec = pl.BlockSpec((8, RT), lambda i, r: (p, r))
    kvout = pl.BlockSpec((2, TOK, 128), lambda i, r: (0, 0, 0))
    acc = pltpu.VMEM((HALO + TOK, 128), F32)
    return pl.pallas_call(
        attend_back_kernel,
        grid=(1, 2),
        out_shape=(
            sds((TOK, 384), F32),
            sds((2, TOK, 128), BF16),
            sds((2, TOK, 128), BF16),
            sds((2, TOK, 128), F32),
        ),
        in_specs=[
            rowspec,
            rowspec,
            statspec,
            statspec,
            pl.BlockSpec((1, RT), lambda i, r: (0, r)),
            kvspec,
            kvspec,
            kvspec,
        ],
        out_specs=(pl.BlockSpec((RT, 384), lambda i, r: (r, 0)), kvout, kvout, kvout),
        scratch_shapes=[
            pltpu.VMEM((4, HALO + TOK, 128), BF16),
            pltpu.VMEM((4, HALO + TOK, 128), BF16),
            pltpu.VMEM((128, HALO + TOK), BF16),
            pltpu.VMEM((SPAN, RT), F32),
            pltpu.VMEM((384, RT), F32),
            acc,
            acc,
            acc,
            acc,
        ],
        compiler_params=params(),
        cost_estimate=cost(),
        name="attend_back",
    )(q, do, lse, delta, lo, kv2, kv1, kv0)


def out_proj_kernel(offs, att, oi, oo2, wo, part, mid_o, w, sem):
    cs = piece_copies(offs, (wo,), w, sem)
    for c in cs:
        c.start()
    a = att[...]
    mid = nt(a, oi[...]).astype(BF16)
    mid_o[...] = mid
    for c in cs:
        c.wait()
    for n in range(3):
        cols = slice(n * 512, (n + 1) * 512)
        part[:, cols] = (nt(a, w[cols, :]) + nn(mid, oo2[:, cols])).astype(BF16)


def out_proj_call(offs, att, oi, oo2, wo):
    return pl.pallas_call(
        out_proj_kernel,
        out_shape=(sds((TOK, D), BF16), sds((TOK, 128), BF16)),
        in_specs=[SM] + [VM] * 3 + [HB],
        out_specs=(VM, VM),
        scratch_shapes=[pltpu.VMEM((D, HQ), BF16), pltpu.SemaphoreType.DMA((16,))],
        compiler_params=params(),
        cost_estimate=cost(),
        name="out_proj",
    )(offs, att, oi, oo2, wo)


def ffn_in_kernel(tok, own, other, gain, a_gu, resid_o, nf_o, mid_o):
    branch = own[...].astype(F32) + other[...].astype(F32)
    x = tok[...].astype(F32) + RS * branch
    resid_o[...] = x
    inv = lax.rsqrt(jnp.mean(x * x, axis=-1, keepdims=True) + EPS)
    nf_o[...] = (x * inv * gain[...]).astype(BF16)
    mid_o[...] = nt(nf_o[...], a_gu[...]).astype(BF16)


def ffn_in_call(tok, own, other, gain, a_gu):
    return pl.pallas_call(
        ffn_in_kernel,
        grid=(4,),
        out_shape=(sds((TOK, D), F32), sds((TOK, D), BF16), sds((TOK, 128), BF16)),
        in_specs=[row_block(D)] * 3 + [all_block(1, D), all_block(128, D)],
        out_specs=(row_block(D), row_block(D), row_block(128)),
        compiler_params=params(),
        cost_estimate=cost(),
        name="ffn_norm",
    )(tok, own, other, gain, a_gu)


def cot_kernel(og, do2, fg_o, mid_o):
    fg_o[...] = (RS * og[...].astype(F32)).astype(BF16)
    mid_o[...] = nt(fg_o[...], do2[...]).astype(BF16)


def cot_call(og, do2):
    return pl.pallas_call(
        cot_kernel,
        out_shape=(sds((TOK, D), BF16), sds((TOK, 128), BF16)),
        in_specs=[VM] * 2,
        out_specs=(VM,) * 2,
        compiler_params=params(),
        cost_estimate=cost(),
        name="branch_cotangent",
    )(og, do2)


def ffn_kernel(offs_a, offs_b, nf, fg, mid_gu, mid_dg, bg, bu, di, a_gu, do2, *refs):
    pb, pa, pc = refs[:5], refs[5:10], refs[10:15]
    part_f, part_n, rep_o, gout, uout, din = refs[15:21]
    wb, wa, wc, xn, xf, accf, accn, sem_b, sem_a, sem_c = refs[21:]
    cb = piece_copies(offs_b, pb, wb, sem_b)
    ca = piece_copies(offs_a, pa, wa, sem_a)
    cc = piece_copies(offs_b, pc, wc, sem_c)
    for c in cb + ca + cc:
        c.start()
    xn[:, 0:D] = nf[...]
    xn[:, D:DX] = mid_gu[...]
    xf[:, 0:D] = fg[...]
    xf[:, D:DX] = mid_dg[...]
    mid_t = mid_gu[...].astype(F32).T.astype(BF16)[0:32]
    dg_t = mid_dg[...].astype(F32).T.astype(BF16)[0:16]
    for w, copies, start, n in ((wb, cb, FA, FB), (wa, ca, 0, FA), (wc, cc, FA + FB, FC)):
        blk = slice(start, start + n)
        w[D:DX, 0:n] = bg[:, blk]
        w[D:DX, n : 2 * n] = bu[:, blk]
        w[D:DX, 2 * n : 3 * n] = di[:, blk]
        for c in copies:
            c.wait()
        gu = nn(xn[...], w[:, 0 : 2 * n])
        hg = nn(xf[...], w[:, 2 * n : 3 * n])
        g, u = gu[:, 0:n], gu[:, n : 2 * n]
        sig = 1.0 / (1.0 + jnp.exp(-g))
        si = g * sig
        hid = (si * u).astype(BF16)
        gg = (hg * u * (sig * (1.0 + g * (1.0 - sig)))).astype(BF16)
        ug = (hg * si).astype(BF16)
        both = jnp.concatenate([gg, ug], axis=1)
        terms = 2.0 * nn(mid_t, both)
        gout[:, blk] = terms[0:16, 0:n].astype(BF16)
        uout[:, blk] = terms[16:32, n : 2 * n].astype(BF16)
        din[:, blk] = nn(dg_t, hid).astype(BF16)
        for c0, c1 in ((0, 512), (512, 1024), (1024, DX)):
            cols = slice(c0, c1)
            f = nt(hid, w[cols, 2 * n : 3 * n])
            d = nt(both, w[cols, 0 : 2 * n])
            if w is wb:
                accf[:, cols] = f
                accn[:, cols] = d
            else:
                accf[:, cols] += f
                accn[:, cols] += d
    midd, midg = accf[:, D:DX], accn[:, D:DX]
    midd_b = midd.astype(BF16)
    midg_b = midg.astype(BF16)
    for c0 in range(0, D, 512):
        cols = slice(c0, c0 + 512)
        part_n[:, cols] = (accn[:, cols] + nn(midg_b, a_gu[:, cols])).astype(BF16)
        part_f[:, cols] = (accf[:, cols] + nn(midd_b, do2[:, cols])).astype(BF16)
    gu_in = nn(midg.T.astype(BF16)[0:32], nf[...])
    d_out = 2.0 * nn(midd.T.astype(BF16)[0:16], fg[...])
    for c in range(2):
        half = slice(c * 768, (c + 1) * 768)
        rep_o[c, 0:32] = gu_in[:, half].astype(BF16)
        rep_o[c, 32:48] = d_out[:, half].astype(BF16)


def ffn_call(offs_a, offs_b, nf, fg, mid_gu, mid_dg, bg, bu, di, a_gu, do2, wb, wa, wc):
    return pl.pallas_call(
        ffn_kernel,
        out_shape=(sds((TOK, D), BF16), sds((TOK, D), BF16), sds((2, 48, 768), BF16))
        + (sds((16, FH), BF16),) * 3,
        in_specs=[SM, SM] + [VM] * 9 + [HB] * 15,
        out_specs=(VM,) * 6,
        scratch_shapes=[
            pltpu.VMEM((DX, 3 * FB), BF16),
            pltpu.VMEM((DX, 3 * FA), BF16),
            pltpu.VMEM((DX, 3 * FC), BF16),
            pltpu.VMEM((TOK, DX), BF16),
            pltpu.VMEM((TOK, DX), BF16),
            pltpu.VMEM((TOK, DX), F32),
            pltpu.VMEM((TOK, DX), F32),
            pltpu.SemaphoreType.DMA((16,)),
            pltpu.SemaphoreType.DMA((16,)),
            pltpu.SemaphoreType.DMA((16,)),
        ],
        compiler_params=params(),
        cost_estimate=cost(),
        name="ffn_both",
    )(offs_a, offs_b, nf, fg, mid_gu, mid_dg, bg, bu, di, a_gu, do2, *wb, *wa, *wc)


def out_back_kernel(
    offs, og, resid, own, other, gain, oi, oo2, mid_att, att, hsel, wo,
    rg_o, do_o, delta_o, rep_o, oin_o, w, abg, sem,
):
    cs = piece_copies(offs, (wo,), w, sem)
    for c in cs:
        c.start()
    for r in range(4):
        rows = pl.ds(r * 128, 128)
        x = resid[rows, :]
        inv = lax.rsqrt(jnp.mean(x * x, axis=-1, keepdims=True) + EPS)
        wv = (own[rows, :].astype(F32) + other[rows, :].astype(F32)) * gain[...]
        dot = jnp.mean(wv * x, axis=-1, keepdims=True)
        rg = og[rows, :].astype(F32) + inv * wv - x * (inv * inv * inv * dot)
        rg_o[rows, :] = rg
        abg[rows, :] = (RS * rg).astype(BF16)
    g = abg[...]
    mid_g = nt(g, oo2[...]).astype(BF16)
    for c in cs:
        c.wait()
    delta = jnp.zeros((16, TOK), F32)
    for n in range(3):
        cols = slice(n * 256, (n + 1) * 256)
        dd = (nn(g, w[:, cols]) + nn(mid_g, oi[:, cols])).astype(BF16)
        do_o[:, cols] = dd
        prod = dd.astype(F32) * att[:, cols].astype(F32)
        high = prod.astype(BF16)
        low = (prod - high.astype(F32)).astype(BF16)
        delta = delta + nt(hsel[:, cols], high) + nt(hsel[:, cols], low)
    delta_o[...] = delta
    o_out = 2.0 * nn(mid_att[...].astype(F32).T.astype(BF16)[0:16], g)
    for c in range(2):
        rep_o[c] = o_out[:, c * 768 : (c + 1) * 768].astype(BF16)
    oin_o[...] = nn(mid_g.astype(F32).T.astype(BF16)[0:16], att[...]).astype(BF16)


def out_back_call(offs, og, resid, own, other, gain, oi, oo2, mid_att, att, hsel, wo):
    return pl.pallas_call(
        out_back_kernel,
        out_shape=(
            sds((TOK, D), F32),
            sds((TOK, HQ), BF16),
            sds((16, TOK), F32),
            sds((2, 16, 768), BF16),
            sds((16, HQ), BF16),
        ),
        in_specs=[SM] + [VM] * 10 + [HB],
        out_specs=(VM,) * 5,
        scratch_shapes=[
            pltpu.VMEM((D, HQ), BF16),
            pltpu.VMEM((TOK, D), BF16),
            pltpu.SemaphoreType.DMA((16,)),
        ],
        compiler_params=params(),
        cost_estimate=cost(),
        name="out_proj_back",
    )(offs, og, resid, own, other, gain, oi, oo2, mid_att, att, hsel, wo)


def q_back_kernel(offs, dq0, dq1, cos, sin, b2, a1, mid, normed, *refs):
    pieces, (part, in_o, out_o, w, dall, sem) = refs[:5], refs[5:]
    cs = piece_copies(offs, [p.at[:, :, pl.ds(0, HQ)] for p in pieces], w, sem)
    for c in cs:
        c.start()
    cw = jnp.concatenate([cos[...], cos[...]], axis=1)
    sw = jnp.concatenate([sin[...], sin[...]], axis=1)
    dq = jnp.concatenate([dq0[...], dq1[...]], axis=1)
    for n in range(3):
        g = dq[:, n * 256 : (n + 1) * 256]
        dall[:, n * 256 : (n + 1) * 256] = (g * cw - half_swap(g) * sw).astype(BF16)
    d = dall[...]
    mid_g = nt(d, b2[:, 0:HQ]).astype(BF16)
    mid_t = mid[...].astype(F32).T.astype(BF16)
    out_o[...] = (2.0 * nn(mid_t[0:16], d)).astype(BF16)
    in_o[...] = nn(mid_g.astype(F32).T.astype(BF16)[0:16], normed[...]).astype(BF16)
    for c in cs:
        c.wait()
    for n in range(3):
        cols = slice(n * 512, (n + 1) * 512)
        part[:, cols] = nt(d, w[cols, :]) + nn(mid_g, a1[:, cols])


def q_back_call(offs, dq0, dq1, cos, sin, b2, a1, mid, normed, w):
    return pl.pallas_call(
        q_back_kernel,
        out_shape=(sds((TOK, D), F32), sds((16, D), BF16), sds((16, HQ), BF16)),
        in_specs=[SM] + [VM] * 8 + [HB] * 5,
        out_specs=(VM,) * 3,
        scratch_shapes=[
            pltpu.VMEM((D, HQ), BF16),
            pltpu.VMEM((TOK, HQ), BF16),
            pltpu.SemaphoreType.DMA((16,)),
        ],
        compiler_params=params(),
        cost_estimate=cost(),
        name="q_back",
    )(offs, dq0, dq1, cos, sin, b2, a1, mid, normed, *w)


def kv_back_kernel(offs, qpart, q_in, da0, da1, da2, db0, db1, db2, cos, sin, b2, a1, mid, normed, orep, *refs):
    pieces, (part, rep_o, out_o, w, dall, sem) = refs[:5], refs[5:]
    cs = piece_copies(offs, [p.at[:, :, pl.ds(HQ, 512)] for p in pieces], w, sem)
    for c in cs:
        c.start()
    cw = jnp.concatenate([cos[...], cos[...]], axis=1)
    sw = jnp.concatenate([sin[...], sin[...]], axis=1)
    both = []
    for i in range(2):
        own = jnp.concatenate([da0[i], db0[i]], axis=1)
        one = jnp.concatenate([da1[i], db1[i]], axis=1)
        two = jnp.concatenate([da2[i], db2[i]], axis=1)
        both.append(own + one.astype(F32) + two.astype(F32))
    dall[:, 0:256] = (both[0] * cw - half_swap(both[0]) * sw).astype(BF16)
    dall[:, 256:512] = both[1].astype(BF16)
    d = dall[...]
    mid_g = nt(d, b2[:, HQ:1280]).astype(BF16)
    mid_t = mid[...].astype(F32).T.astype(BF16)
    out_o[:, 0:256] = (2.0 * nn(mid_t[16:32], dall[:, 0:256])).astype(BF16)
    out_o[:, 256:512] = (2.0 * nn(mid_t[32:48], dall[:, 256:512])).astype(BF16)
    in_grads = nn(mid_g.astype(F32).T.astype(BF16)[16:48], normed[...]).astype(BF16)
    for c in range(2):
        cols = slice(c * 768, (c + 1) * 768)
        rep_o[c, 0:16] = q_in[:, cols]
        rep_o[c, 16:48] = in_grads[:, cols]
        rep_o[c, 48:64] = orep[c]
    for c in cs:
        c.wait()
    for n in range(3):
        cols = slice(n * 512, (n + 1) * 512)
        part[:, cols] = (qpart[:, cols] + nt(d, w[cols, :]) + nn(mid_g, a1[:, cols])).astype(BF16)


def kv_back_call(offs, qpart, q_in, da, db, cos, sin, b2, a1, mid, normed, orep, w):
    return pl.pallas_call(
        kv_back_kernel,
        out_shape=(sds((TOK, D), BF16), sds((2, 64, 768), BF16), sds((16, 512), BF16)),
        in_specs=[SM] + [VM] * 15 + [HB] * 5,
        out_specs=(VM,) * 3,
        scratch_shapes=[
            pltpu.VMEM((D, 512), BF16),
            pltpu.VMEM((TOK, 512), BF16),
            pltpu.SemaphoreType.DMA((16,)),
        ],
        compiler_params=params(),
        cost_estimate=cost(),
        name="kv_back",
    )(offs, qpart, q_in, *da, *db, cos, sin, b2, a1, mid, normed, orep, *w)


def token_grad_kernel(tok, rg, own, other, gain, out):
    x = tok[...].astype(F32)
    inv = lax.rsqrt(jnp.mean(x * x, axis=-1, keepdims=True) + EPS)
    wv = (own[...].astype(F32) + other[...].astype(F32)) * gain[...]
    dot = jnp.mean(wv * x, axis=-1, keepdims=True)
    out[...] = (rg[...] + inv * wv - x * (inv * inv * inv * dot)).astype(BF16)


def token_grad_call(tok, rg, own, other, gain):
    return pl.pallas_call(
        token_grad_kernel,
        grid=(4,),
        out_shape=sds((TOK, D), BF16),
        in_specs=[row_block(D)] * 4 + [all_block(1, D)],
        out_specs=row_block(D),
        compiler_params=params(),
        cost_estimate=cost(),
        name="token_grad",
    )(tok, rg, own, other, gain)


def pack_first_kernel(q, k, v, out):
    out[:, 0:768] = q[...]
    out[:, 768:1024] = k[...]
    out[:, 1024:1280] = v[...]


def pack_first_call(q, k, v):
    return pl.pallas_call(
        pack_first_kernel,
        out_shape=sds((96, 1280), BF16),
        in_specs=[VM] * 3,
        out_specs=VM,
        compiler_params=params(),
        cost_estimate=cost(),
        name="pack_qkv",
    )(q, k, v)


def pack_rest_kernel(o, g, u, d, yx, xy1, xy2):
    yx[:, 0:HQ] = o[...]
    for i, w in enumerate((g, u, d)):
        yx[:, HQ + i * FA : HQ + (i + 1) * FA] = w[:, 0:FA]
        xy1[:, i * FB : (i + 1) * FB] = w[:, FA : FA + FB]
        xy2[:, i * FC : (i + 1) * FC] = w[:, FA + FB : FH]


def pack_rest_call(o, g, u, d):
    return pl.pallas_call(
        pack_rest_kernel,
        out_shape=(
            sds((96, HQ + 3 * FA), BF16),
            sds((96, 3 * FB), BF16),
            sds((96, 3 * FC), BF16),
        ),
        in_specs=[VM] * 4,
        out_specs=(VM,) * 3,
        compiler_params=params(),
        cost_estimate=cost(),
        name="pack_rest",
    )(o, g, u, d)


def line_call(parts, head):
    n = parts[0].shape[1] - head

    def kernel(*refs):
        ins, outs = refs[:4], refs[4:]
        for i in range(4):
            if head:
                outs[0][i] = ins[i][:, 0:head]
            outs[-1][i] = ins[i][:, head:]

    shapes = (sds((4, 96, head), BF16),) * bool(head) + (sds((4, 96, n), BF16),)
    return pl.pallas_call(
        kernel,
        out_shape=shapes,
        in_specs=[VM] * 4,
        out_specs=(VM,) * len(shapes),
        compiler_params=params(),
        cost_estimate=cost(),
        name="line",
    )(*parts)


def own_half_kernel(idx, q, k, v, o, g, u, d, out):
    at = 0
    for ref in (q, k, v, o, g, u, d):
        n = ref.shape[2]
        out[:, at : at + n] = ref[0]
        at += n


def own_half_call(index, arrays):
    return pl.pallas_call(
        own_half_kernel,
        out_shape=sds((16, 7808), BF16),
        grid_spec=pltpu.PrefetchScalarGridSpec(
            num_scalar_prefetch=1,
            grid=(1,),
            in_specs=[
                pl.BlockSpec((1, 16, a.shape[2]), lambda i, idx: (idx[0], 0, 0)) for a in arrays
            ],
            out_specs=pl.BlockSpec((16, 7808), lambda i, idx: (0, 0)),
        ),
        compiler_params=params(),
        cost_estimate=cost(),
        name="pick_halves",
    )(index, *arrays)


def factors_kernel(
    idx, halves, aq, ak, av, ag, au, oo, do, a_qkv, b_qkv, a_gu, bg, bu, di, oi, oo2, do2
):
    for ref in (a_qkv, b_qkv, a_gu, bg, bu, di, oi, oo2, do2):
        ref[...] = jnp.zeros_like(ref)
    for i, ref in enumerate((aq, ak, av)):
        a_qkv[i * 16 : (i + 1) * 16] = ref[0]
    for i, ref in enumerate((ag, au)):
        a_gu[i * 16 : (i + 1) * 16] = ref[0]
    oo2[0:16] = 2 * oo[0]
    do2[0:16] = 2 * do[0]
    b_qkv[0:16, 0:768] = 2 * halves[:, 0:768]
    b_qkv[16:32, 768:1024] = 2 * halves[:, 768:1024]
    b_qkv[32:48, 1024:1280] = 2 * halves[:, 1024:1280]
    oi[0:16] = halves[:, 1280:2048]
    bg[0:16] = 2 * halves[:, 2048:3968]
    bu[16:32] = 2 * halves[:, 3968:5888]
    di[0:16] = halves[:, 5888:7808]


def factors_call(index, halves, arrays):
    widths = (D, 1280, D, FH, FH, FH, HQ, D, D)
    return pl.pallas_call(
        factors_kernel,
        out_shape=tuple(sds((128, w), BF16) for w in widths),
        grid_spec=pltpu.PrefetchScalarGridSpec(
            num_scalar_prefetch=1,
            grid=(1,),
            in_specs=[pl.BlockSpec((16, 7808), lambda i, idx: (0, 0))]
            + [pl.BlockSpec((1, 16, D), lambda i, idx: (idx[0], 0, 0))] * 7,
            out_specs=tuple(pl.BlockSpec((128, w), lambda i, idx: (0, 0)) for w in widths),
        ),
        compiler_params=params(),
        cost_estimate=cost(),
        name="factors",
    )(index, halves, *arrays)


def quarters_kernel(m, place, rep, got, *refs):
    parts, outs, buf = refs[:-5], refs[-5:-1], refs[-1]
    core, z = place[0], place[1]
    n_rep = rep.shape[1] // 16
    kept = (rep[core].astype(F32) + got[...].astype(F32)).astype(BF16)
    for i in range(n_rep):
        buf[:, i * 768 : (i + 1) * 768] = kept[i * 16 : (i + 1) * 16]
    at = n_rep * 768
    for p in parts:
        buf[:, at : at + p.shape[1]] = p[...]
        at += p.shape[1]
    if at < 4 * m:
        buf[:, at : 4 * m] = jnp.zeros((16, 4 * m - at), BF16)
    for k, out in enumerate(outs):
        quarter = lax.rem(z + k, 4)
        out[...] = buf[:, pl.ds(pl.multiple_of(quarter * m, 128), m)]


def quarters_call(m, place, rep, got, parts):
    def kernel(*refs):
        quarters_kernel(m, *refs)

    return pl.pallas_call(
        kernel,
        out_shape=(sds((16, m), BF16),) * 4,
        in_specs=[SM] + [VM] * (2 + len(parts)),
        out_specs=(VM,) * 4,
        scratch_shapes=[pltpu.VMEM((16, 4 * m), BF16)],
        compiler_params=params(),
        cost_estimate=cost(),
        name="quarters",
    )(place, rep, got, *parts)


def pack_early_kernel(place, rep, got, g, u, d, out):
    kept = (rep[place[0]].astype(F32) + got[...].astype(F32)).astype(BF16)
    for i in range(3):
        out[:, i * 768 : (i + 1) * 768] = kept[i * 16 : (i + 1) * 16]
    for i, ref in enumerate((g, u, d)):
        out[:, 2304 + i * FH : 2304 + (i + 1) * FH] = ref[...]
    out[:, 8064:8192] = jnp.zeros((16, 128), BF16)


def pack_early_call(place, rep, got, g, u, d):
    return pl.pallas_call(
        pack_early_kernel,
        out_shape=sds((16, 4 * EARLY), BF16),
        in_specs=[SM] + [VM] * 5,
        out_specs=VM,
        compiler_params=params(),
        cost_estimate=cost(),
        name="pack_early",
    )(place, rep, got, g, u, d)


def quarter_kernel(place, total, out):
    at = pl.multiple_of(place[1] * EARLY, 128)
    out[:, 0:EARLY] = total[:, pl.ds(at, EARLY)]
    out[:, EARLY : EARLY + 128] = (
        jnp.full((16, 128), place[2], jnp.int32).astype(F32).astype(BF16)
    )


def quarter_call(place, total):
    return pl.pallas_call(
        quarter_kernel,
        out_shape=sds((16, EARLY + 128), BF16),
        in_specs=[SM, VM],
        out_specs=VM,
        compiler_params=params(),
        cost_estimate=cost(),
        name="quarter",
    )(place, total)


def sum_kernel(place, a, b, c, d, out):
    m = a.shape[1]
    total = a[...].astype(F32) + b[...].astype(F32) + c[...].astype(F32) + d[...].astype(F32)
    out[:, 0:m] = total.astype(BF16)
    out[:, m : m + 128] = jnp.full((16, 128), place[2], jnp.int32).astype(F32).astype(BF16)


def sum_call(place, parts):
    m = parts[0].shape[1]
    return pl.pallas_call(
        sum_kernel,
        out_shape=sds((16, m + 128), BF16),
        in_specs=[SM] + [VM] * 4,
        out_specs=VM,
        compiler_params=params(),
        cost_estimate=cost(),
        name="sum_tokens",
    )(place, *parts)


def by_adapter_kernel(*refs):
    ins, out = refs[:-1], refs[-1]
    m = out.shape[2]
    rows = [(r, k) for r in ins for k in range(r.shape[0])]
    for a in range(8):
        total = jnp.zeros((16, m), F32)
        for r, k in rows:
            hit = r[k, :, m : m + 1].astype(F32) == float(a)
            total = total + jnp.where(hit, r[k, :, 0:m].astype(F32), 0.0)
        out[a] = total.astype(BF16)


def by_adapter_call(parts, m):
    return pl.pallas_call(
        by_adapter_kernel,
        out_shape=sds((8, 16, m), BF16),
        in_specs=[VM] * len(parts),
        out_specs=VM,
        compiler_params=params(),
        cost_estimate=cost(),
        name="by_adapter",
    )(*parts)


def spread(buf, outs, jobs, widths):
    at = 0
    for out, n in zip(outs, widths, strict=True):
        for c in range(2):
            out[:, :, c * n : (c + 1) * n] = buf[c, :, :, at : at + n].astype(F32)
        at += n


def unpack_early_kernel(src, *refs):
    outs, buf, sem = refs[:-2], refs[-2], refs[-1]
    copies = []
    for z in range(4):
        for c in range(2):
            copies.append(
                pltpu.make_async_copy(
                    src.at[2 * z + c], buf.at[c, :, :, pl.ds(z * EARLY, EARLY)], sem.at[2 * z + c]
                )
            )
    for c in copies:
        c.start()
    for c in copies:
        c.wait()
    spread(buf, outs, None, (768, 768, 768, FH, FH, FH))


def unpack_early_call(src):
    widths = (D, D, D, 2 * FH, 2 * FH, 2 * FH)
    return pl.pallas_call(
        unpack_early_kernel,
        out_shape=tuple(sds((8, 16, w), F32) for w in widths),
        in_specs=[HB],
        out_specs=(VM,) * 6,
        scratch_shapes=[pltpu.VMEM((2, 8, 16, 4 * EARLY), BF16), pltpu.SemaphoreType.DMA((8,))],
        compiler_params=params(),
        cost_estimate=cost(),
        name="unpack_early",
    )(src)


def unpack_late_kernel(place, *refs):
    srcs, outs, buf, sem = refs[:8], refs[8:-2], refs[-2], refs[-1]
    core, z = place[0], place[1]
    copies = []
    for i, src in enumerate(srcs):
        c = core if i < 4 else 1 - core
        at = lax.rem(z + REL[i % 4] + 4, 4) * LATE
        copies.append(
            pltpu.make_async_copy(
                src, buf.at[c, :, :, pl.ds(pl.multiple_of(at, 128), LATE)], sem.at[i]
            )
        )
    for c in copies:
        c.start()
    for c in copies:
        c.wait()
    spread(buf, outs, None, (768, 768, 768, 768, 768, 256, 256, 768))


def unpack_late_call(place, srcs):
    widths = (D, D, D, D, D, 512, 512, D)
    return pl.pallas_call(
        unpack_late_kernel,
        out_shape=tuple(sds((8, 16, w), F32) for w in widths),
        in_specs=[SM] + [HB] * 8,
        out_specs=(VM,) * 8,
        scratch_shapes=[pltpu.VMEM((2, 8, 16, 4 * LATE), BF16), pltpu.SemaphoreType.DMA((8,))],
        compiler_params=params(),
        cost_estimate=cost(),
        name="unpack_late",
    )(place, *srcs)


YLIN = (0, 2, 1, 3)


def go_x(v, step):
    return lax.ppermute(v, "x", [(i, (i + step) % 4) for i in range(4)])


def go_y(v, step):
    return lax.ppermute(
        v, ("tensor", "yh"), [(YLIN[i], YLIN[(i + step) % 4]) for i in range(4)]
    )


def go_z(v, step):
    return lax.ppermute(v, "seq", [(i, (i + step) % 4) for i in range(4)])


def go_core(v):
    return lax.ppermute(v, "core", [(0, 1), (1, 0)])


def to_role(v):
    return lax.ppermute(v, ("tensor", "core"), [(1, 2), (2, 1)])


REL = (0, -1, 1, 2)


def near_line(shard, near):
    return (shard, near(shard, 1), near(shard, -1), near(shard, 2))


def ring_start(line, far):
    return (line, far(line, 1), far(line, -1))


def ring_halves(below, above):
    return below[:2], above[2:]


class Order:
    def __init__(self):
        self.last = ()

    def gate(self, v):
        return lax.optimization_barrier((v, self.last))[0]

    def done(self, v):
        v = self.gate(v)
        self.last = jax.tree.leaves(v)[-1:]
        return v

    def run(self, step, *args):
        out = step(*self.gate(args))
        self.last = jax.tree.leaves(out)[-1:]
        return out


def offsets(x, y, path):
    near = np.tile(np.array(REL, np.int32), 4)
    far = np.repeat(np.array(REL, np.int32), 4)
    if path == "yx":
        return ((x + far + 4) % 4) * 4 + (y + near + 4) % 4
    if path == "xy":
        return np.tile(np.arange(4, dtype=np.int32), 4) * 4 + (y + far + 4) % 4
    return np.repeat(np.arange(4, dtype=np.int32), 4) * 4 + (y + near + 4) % 4


def halo_back(grads):
    two, one, own = grads
    one = lax.ppermute(one, "seq", [(1, 0), (2, 1), (3, 2)])
    return (own, one, lax.ppermute(two, "seq", [(2, 0), (3, 1)]))


def shards(
    tokens,
    output_gradient,
    document_length_table,
    sequence_adapter_index,
    sequence_window_length,
    attention_norm_gain,
    feedforward_norm_gain,
    query_projection_weight,
    key_projection_weight,
    value_projection_weight,
    output_projection_weight,
    gate_projection_weight,
    up_projection_weight,
    down_projection_weight,
    query_adapter_first,
    query_adapter_second,
    key_adapter_first,
    key_adapter_second,
    value_adapter_first,
    value_adapter_second,
    output_adapter_first,
    output_adapter_second,
    gate_adapter_first,
    gate_adapter_second,
    up_adapter_first,
    up_adapter_second,
    down_adapter_first,
    down_adapter_second,
):
    z = lax.axis_index("seq")
    yl = lax.axis_index("tensor")
    x = lax.axis_index("x")
    y = lax.axis_index("yh") * 2 + yl
    core = lax.axis_index("core")
    same = core == yl

    o = Order()
    t = lambda v: v.swapaxes(1, 2)
    mine = lambda own, got: jnp.where(same, own, got)
    offs_yx, offs_xy, offs_o = (offsets(x, y, p) for p in ("yx", "xy", "o"))
    gain1 = attention_norm_gain[None, :]
    gain2 = feedforward_norm_gain[None, :]

    own_qkv = o.run(
        pack_first_call, query_projection_weight, key_projection_weight, value_projection_weight
    )
    got_qkv = to_role(own_qkv)
    own_yx, own_b, own_c = o.run(
        pack_rest_call,
        output_projection_weight,
        gate_projection_weight,
        up_projection_weight,
        down_projection_weight,
    )
    got_b = to_role(own_b)
    meta = jnp.concatenate(
        [document_length_table[0], sequence_adapter_index, sequence_window_length]
    )
    meta_other = go_core(meta)
    tok_other = go_core(o.gate(tokens[0]))
    own_halves = o.run(
        own_half_call,
        sequence_adapter_index,
        (
            query_adapter_second,
            key_adapter_second,
            value_adapter_second,
            output_adapter_first,
            gate_adapter_second,
            up_adapter_second,
            down_adapter_first,
        ),
    )
    near_qkv = near_line(o.run(mine, own_qkv, o.done(got_qkv)), go_y)
    line_b = lax.all_gather(o.run(mine, own_b, o.done(got_b)), "x", axis=0)

    def tables(own, other):
        meta = mine(own, other)
        lengths, index, window = meta[:4], meta[4:5], meta[5]
        place = jnp.concatenate([jnp.stack([core, z]).astype(jnp.int32), index])
        ends = jnp.cumsum(lengths, dtype=jnp.int32)
        begins = ends - lengths
        row = z * TOK + jnp.arange(TOK, dtype=jnp.int32)
        begin = jnp.max(jnp.where(row[:, None] >= begins[None, :], begins[None, :], 0), axis=1)
        low_key = (jnp.maximum(begin, row - window + 1) - (z * TOK - HALO))[None, :]
        lane = jnp.arange(128, dtype=jnp.int32) % HDIM
        frequency = ROPE_BASE ** (-((lane % 32).astype(F32) * (2.0 / HDIM)))
        angles = (row - begin).astype(F32)[:, None] * frequency[None, :]
        cos = jnp.cos(angles)
        sin = jnp.sin(angles) * jnp.where(lane < 32, -1.0, 1.0)[None, :]
        return index, place, low_key, cos, sin

    index, place, low_key, cos, sin = o.run(tables, meta, o.done(meta_other))
    tok = o.run(mine, tokens[0], o.done(tok_other))
    line_qkv = o.run(lambda *v: line_call(v, 0)[0], *o.done(near_qkv))
    below_qkv, above_qkv = go_x(line_qkv, 1), go_x(line_qkv, -1)
    got_halves, got_yx, got_c = (to_role(o.gate(v)) for v in (own_halves, own_yx, own_c))
    og_other = go_core(o.gate(output_gradient[0]))
    halves = o.run(mine, own_halves, o.done(got_halves))
    a_qkv, b_qkv, a_gu, bg2, bu2, di_p, oi_p, oo2, do2 = o.run(
        factors_call,
        index,
        halves,
        (
            t(query_adapter_first),
            t(key_adapter_first),
            t(value_adapter_first),
            t(gate_adapter_first),
            t(up_adapter_first),
            output_adapter_second,
            down_adapter_second,
        ),
    )
    near_yx = near_line(o.run(mine, own_yx, o.done(got_yx)), go_y)
    line_c = lax.all_gather(o.run(mine, own_c, o.done(got_c)), "x", axis=0)
    og = o.run(mine, output_gradient[0], o.done(og_other))
    fg, mid_dg = o.run(cot_call, og, do2)
    line_b = o.done(line_b)
    below_b, above_b = go_y(line_b, 1), go_y(line_b, -1)
    low, high = o.run(ring_halves, *o.done((below_qkv, above_qkv)))
    far_qkv = (go_x(low, 1), go_x(high, -1))
    line_o, line_a = o.run(lambda *v: line_call(v, HQ), *o.done(near_yx))
    full_o = lax.all_gather(line_o, "x", axis=0, tiled=True)
    full_qkv = (line_qkv, below_qkv, above_qkv) + o.done(far_qkv)

    normed, q, kv0, mid_qkv = o.run(
        qkv_call, offs_yx, tok, gain1, a_qkv, b_qkv, cos, sin, full_qkv
    )
    kv1 = lax.ppermute(kv0, "seq", [(0, 1), (1, 2), (2, 3)])
    kv2 = lax.ppermute(kv0, "seq", [(0, 2), (1, 3)])
    line_a = o.gate(line_a)
    below_a, above_a = go_x(line_a, 1), go_x(line_a, -1)
    low, high = o.run(ring_halves, *o.done((below_b, above_b)))
    far_b = (go_y(low, 1), go_y(high, -1))
    line_c = o.done(line_c)
    below_c, above_c = go_y(line_c, 1), go_y(line_c, -1)
    kv1, kv2 = o.done((kv1, kv2))
    att, lse = o.run(attend_call, q, low_key, kv2, kv1, kv0)
    full_o = o.done(full_o)
    attn_part, mid_att = o.run(out_proj_call, offs_o, att, oi_p, oo2, full_o)
    attn_other = go_core(attn_part)
    low, high = o.run(ring_halves, *o.done((below_a, above_a)))
    far_a = (go_x(low, 1), go_x(high, -1))
    resid, nf, mid_gu = o.run(ffn_in_call, tok, attn_part, o.done(attn_other), gain2, a_gu)
    low, high = o.run(ring_halves, *o.done((below_c, above_c)))
    far_c = (go_y(low, 1), go_y(high, -1))
    full_b = (line_b, below_b, above_b) + o.done(far_b)
    full_a = (line_a, below_a, above_a) + o.done(far_a)
    full_c = (line_c, below_c, above_c) + o.done(far_c)
    ffn_part, nfg_part, rep_e, g_out, u_out, d_in = o.run(
        ffn_call,
        offs_yx, offs_xy, nf, fg, mid_gu, mid_dg, bg2, bu2, di_p, a_gu, do2, full_b, full_a, full_c,
    )

    def exchange(rep):
        return go_core(lax.dynamic_index_in_dim(rep, 1 - core, 0, keepdims=False))

    nfg_other = go_core(nfg_part)
    got_e = exchange(rep_e)
    quarters = o.run(
        lambda *v: quarters_call(EARLY, place, v[0], v[1], v[2:]),
        rep_e, o.done(got_e), g_out, u_out, d_in,
    )
    sent = [go_z(quarters[k], k) for k in (1, 2, 3)]
    head = np.arange(16)
    head = np.where(head % 8 < 6, 6 * (head // 8) + head % 8, -1)
    hsel = jnp.asarray((np.arange(HQ) // HDIM)[None, :] == head[:, None], BF16)
    rg, do, delta, rep_o, o_in = o.run(
        out_back_call,
        offs_o, og, resid, nfg_part, o.done(nfg_other), gain2, oi_p, oo2, mid_att, att, hsel, full_o,
    )
    ffn_other = go_core(o.gate(ffn_part))
    near = near_line(o.run(sum_call, place, [quarters[0]] + o.done(sent)), go_y)
    stats = (lse, delta, low_key, kv2, kv1, kv0)
    dqa, *da = o.run(lambda *v: attend_back_call(0, *v), q, do, *stats)
    ra = halo_back(da)
    plane = lax.all_gather(o.run(lambda *v: jnp.stack(v), *o.done(near)), "x", axis=0, tiled=True)
    dqb, *db = o.run(lambda *v: attend_back_call(1, *v), q, do, *stats)
    rb = halo_back(db)
    qpart, q_in, q_out = o.run(
        q_back_call, offs_yx, dqa, dqb, cos, sin, b_qkv, a_qkv, mid_qkv, normed, full_qkv
    )
    out = o.run(
        lambda r, a, b: (r + RS * (a.astype(F32) + b.astype(F32))).astype(BF16),
        resid, ffn_part, o.done(ffn_other),
    )
    out_other = to_role(out)
    dense = o.run(lambda v: by_adapter_call([v], EARLY), o.done(plane))
    ra, rb = o.done((ra, rb))
    early = lax.all_gather(o.gate(dense), ("seq", "core"), axis=0)
    na_part, rep_l, kv_out = o.run(
        kv_back_call,
        offs_yx, qpart, q_in, ra, rb, cos, sin, b_qkv, a_qkv, mid_qkv, normed, rep_o, full_qkv,
    )
    na_other = go_core(na_part)
    got_l = exchange(rep_l)

    quarters = o.run(
        lambda *v: quarters_call(LATE, place, v[0], v[1], v[2:]),
        rep_l, o.done(got_l), q_out, kv_out, o_in,
    )
    sent = [go_z(quarters[k], k) for k in (1, 2, 3)]
    token_grad = o.run(token_grad_call, tok, rg, na_part, o.done(na_other), gain1)
    tg_other = to_role(token_grad)
    near = near_line(o.run(sum_call, place, [quarters[0]] + o.done(sent)), go_y)
    line = o.run(lambda *v: jnp.stack(v), *o.done(near))
    lines = [go_x(line, 1), go_x(line, -1), go_x(line, 2)]
    output = o.run(mine, out, o.done(out_other))
    dense = o.run(lambda *v: by_adapter_call(v, LATE), line, *o.done(lines))
    zs = [go_z(dense, 1), go_z(dense, -1), go_z(dense, 2)]
    cores = [go_core(dense)]
    g_in, u_in, d_out, g_out, u_out, d_in = o.run(unpack_early_call, o.done(early))
    zs = o.done(zs)
    cores += [go_core(v) for v in zs]
    token_grad = o.run(mine, token_grad, o.done(tg_other))
    q_in, k_in, v_in, o_out, q_out, k_out, v_out, o_in = o.run(
        unpack_late_call, place, [dense] + zs + o.done(cores)
    )
    return (
        output[None],
        token_grad[None],
        t(q_in),
        q_out,
        t(k_in),
        k_out,
        t(v_in),
        v_out,
        o_in,
        o_out,
        t(g_in),
        g_out,
        t(u_in),
        u_out,
        d_in,
        d_out,
    )


def solution(mesh):
    fine = Mesh(mesh.devices.reshape(4, 2, 4, 2, 2), ("seq", "tensor", "x", "yh", "core"))
    fsdp = ("x", "yh", "core")
    weight = P(fsdp, "tensor")
    half = P(None, None, "tensor")
    return jax.shard_map(
        shards,
        mesh=fine,
        in_specs=(
            P(fsdp, "seq", None),
            P(fsdp, "seq", None),
            P(fsdp, None),
            P(fsdp),
            P(fsdp),
            P(),
            P(),
        )
        + (weight,) * 7
        + (P(), half, P(), half, P(), half, half, P(), P(), half, P(), half, half, P()),
        out_specs=(P(fsdp, "seq", None), P(fsdp, "seq", None)) + (P(),) * 14,
        check_vma=False,
    )
```

time: 708 us -> 491 us (0.69)
  local copies, waits for them, and re-layouts: 120 us -> 20.9 us
  starting transfers between devices: 179 us -> 98.6 us
  other arithmetic: 49.9 us -> 21.7 us
  waiting for transfers between devices: 168 us -> 144 us
  Pallas kernels: 166 us -> 182 us
  between operations: 7.18 us -> 16.1 us
    dynamic_update_slice x8 -> x0, local copies, waits for them, and re-layouts: 34.5 us -> none  [finish_grads(): whole = lax.dynamic_update_index_in_dim(whole, piece, (z + rel) % 4, 0)]
    ppermute x11 -> x13, starting transfers between devices: 38.1 us -> 11.1 us  [go_core(): return lax.ppermute(v, 'core', [(0, 1), (1, 0)])]
    ppermute x30 -> x11, starting transfers between devices: 31.9 us -> 11.8 us  [go_x(): return lax.ppermute(v, 'x', [(i, (i + step) % 4) for i in range(4)])]
    ppermute x12 -> x9, starting transfers between devices: 39.6 us -> 19.7 us  [go_z(): return lax.ppermute(v, 'seq', [(i, (i + step) % 4) for i in range(4)])]
    ppermute x31 -> x20, waiting for transfers between devices: 43.2 us -> 24.3 us  [go_y(): lax.ppermute(v, ('tensor', 'yh'), [(YLIN[i], YLIN[(i + step) % 4]) for i...]
    convert_element_type x4 -> x0, local copies, waits for them, and re-layouts: 18.4 us -> none  [finish_grads(): flat = lambda v: v.transpose(1, 2, 0, 3).reshape(8, 16, 4 * m).astype(F32)]
    slice x30 -> x9, local copies, waits for them, and re-layouts: 22.9 us -> 6.07 us  [the longest x8 5.46 us: ring_halves(): return (below[:2], above[2:])]
    ppermute x9 -> x11, waiting for transfers between devices: 20.1 us -> 4.83 us  [the longest x7 4.82 us: to_role(): return lax.ppermute(v, ('tensor', 'core'), [(1, 2), (2, 1)])]
  transfers between devices with their start and end apart: 95 -> 71, of which waited for: 28 -> 26; matrix products, arithmetic and copies ran while one was open for 18% -> 6% of each run, Pallas kernels for 20% -> 26%
where the time goes in v2:
time: 491 us; the launch traced here: 483 us
  Pallas kernels  182 us (37%)
  waiting for transfers between devices  144 us (29%)
  starting transfers between devices  98.6 us (20%)
  other arithmetic  21.7 us (4%)
  local copies, waits for them, and re-layouts  20.9 us (4%)
  between operations  16.1 us (3%)
    ppermute x11, waiting for transfers between devices, go_x(): return lax.ppermute(v, 'x', [(i, (i + step) % 4) for i in range(4)])  77.7 us
    pallas_call x1, Pallas kernels, ffn_call(): pl.pallas_call(ffn_kernel, out_shape=(sds((TOK, D), BF16), sds((TOK, D),...  36 us
    pallas_call x2, Pallas kernels, attend_back_call(): pl.pallas_call(attend_back_kernel, grid=(1, 2), out_shape=(sds((TOK, 384)...  28.2 us
    ppermute x20, waiting for transfers between devices, go_y(): lax.ppermute(v, ('tensor', 'yh'), [(YLIN[i], YLIN[(i + step) % 4]) for i...  24.3 us
    pallas_call x1, Pallas kernels, attend_call(): pl.pallas_call(attend_kernel, grid=(2, 2), out_shape=(sds((TOK, HQ), BF16...  23.6 us
    ppermute x20, starting transfers between devices, go_y(): lax.ppermute(v, ('tensor', 'yh'), [(YLIN[i], YLIN[(i + step) % 4]) for i...  22 us
    ppermute x7, starting transfers between devices, to_role(): return lax.ppermute(v, ('tensor', 'core'), [(1, 2), (2, 1)])  20.8 us
    ppermute x9, starting transfers between devices, go_z(): return lax.ppermute(v, 'seq', [(i, (i + step) % 4) for i in range(4)])  19.7 us
  transfers between devices with their start and end apart: 71, of which 26 were waited for; matrix products, arithmetic and copies ran while one was open for 6% of the time, Pallas kernels for 26%

profile of v2, /device:TPU:1, one launch (start us, length us, event | category | flops | bytes accessed | tf_op | source)
XLA Modules:
  0.0 482.8 jit_solution(9412217480012774633)
XLA Ops:
  9.0 4.6 collective-permute-start.3
  33.4 4.7 collective-permute-done.5.refs_2_
  55.0 4.7 collective-permute-done.12
  71.6 4.7 all-gather.13.cloned.1.call-done
  76.3 14.7 %collective-permute-done.9.refs_2_ = bf16[4,96,1280]{2,1,0:T(8,128)(2,1)S(1)} collective-permute-done((bf16[4,96,1280]{2,1,0:T(8,128)(2,1)S(1)}, bf16[4,96,1280]{2,1,0:T(8,128)(2,1)S(1)}, u32[]{:S(2)}, u32[]{:S(2)}) %collective-permute-start.9) | collective-permute-done | bytes 983072 | tf_op jit(solution)/shard_map/ppermute | solution.py:941
  102.2 14.1 %collective-permute-done.13.refs_3_ = bf16[2,96,1280]{2,1,0:T(8,128)(2,1)S(1)} collective-permute-done((bf16[2,96,1280]{2,1,0:T(8,128)(2,1)S(1)}, bf16[2,96,1280]{2,1,0:T(8,128)(2,1)S(1)}, u32[]{:S(2)}, u32[]{:S(2)}) %collective-permute-start.13) | collective-permute-done | bytes 491552 | tf_op jit(solution)/shard_map/ppermute | solution.py:941
  117.2 8.3 %norm_qkv.1 = (bf16[512,1536]{1,0:T(8,128)(2,1)}, bf16[512,768]{1,0:T(8,128)(2,1)}, bf16[2,512,256]{2,1,0:T(8,128)(2,1)}, bf16[512,128]{1,0:T(8,128)(2,1)}) custom-call(s32[16]{0:T(128)} %get-tuple-element.686.offs.offs_a, bf16[512,1536]{1,0:T(8,128)(2,1)} %broadcast_select_fusion.3.tok, f32[1,1536]{1,0:T(1,128)} %broadcast_in_dim.40.gain, ...), custom_call_target="tpu_custom_call" | custom-call | flops 1 | bytes 1 | tf_op jit(solution)/shard_map/norm_qkv/pallas_call | solution.py:116
  126.9 4.8 collective-permute-start.19
  137.0 5.0 %collective-permute-done.19.kv2 = bf16[2,512,256]{2,1,0:T(8,128)(2,1)S(1)} collective-permute-done((bf16[2,512,256]{2,1,0:T(8,128)(2,1)}, bf16[2,512,256]{2,1,0:T(8,128)(2,1)S(1)}, u32[]{:S(2)}, u32[]{:S(2)}) %collective-permute-start.19) | collective-permute-done | bytes 524320 | tf_op jit(solution)/shard_map/ppermute | solution.py:1141
  142.0 11.2 %collective-permute-done.18.kv1 = bf16[2,512,256]{2,1,0:T(8,128)(2,1)S(1)} collective-permute-done((bf16[2,512,256]{2,1,0:T(8,128)(2,1)}, bf16[2,512,256]{2,1,0:T(8,128)(2,1)S(1)}, u32[]{:S(2)}, u32[]{:S(2)}) %collective-permute-start.18) | collective-permute-done | bytes 524320 | tf_op jit(solution)/shard_map/ppermute | solution.py:1140
  154.0 23.6 %attend.1 = (bf16[512,768]{1,0:T(8,128)(2,1)}, f32[16,512]{1,0:T(8,128)}) custom-call(bf16[512,768]{1,0:T(8,128)(2,1)} %get-tuple-element.642.q, s32[1,512]{1,0:T(1,128)} %maximum_subtract_fusion.lo, bf16[2,512,256]{2,1,0:T(8,128)(2,1)} %copy-done.5, bf16[2,512,256]{2,1,0:T(8,128)(2,1)} %copy-done.6, bf16[2,512,256]{2,1,0:T(8,128)(2,1)} %get-tuple-element.649.kv0), custom_call_target="tpu_custom_call" | custom-call | flops 1 | bytes 1 | tf_op jit(solution)/shard_map/attend/pallas_call | solution.py:179
  177.6 6.3 %out_proj.1 = (bf16[512,1536]{1,0:T(8,128)(2,1)}, bf16[512,128]{1,0:T(8,128)(2,1)}) custom-call(s32[16]{0:T(128)} %add.145.offs, bf16[512,768]{1,0:T(8,128)(2,1)} %get-tuple-element.606.att, bf16[128,768]{1,0:T(8,128)(2,1)} %get-tuple-element.603.oi, bf16[128,1536]{1,0:T(8,128)(2,1)} %get-tuple-element.604.oo2, ...), custom_call_target="tpu_custom_call" | custom-call | flops 1 | bytes 1 | tf_op jit(solution)/shard_map/out_proj/pallas_call | solution.py:312
  190.9 30.6 %collective-permute-done.23.refs_6_ = bf16[4,96,1920]{2,1,0:T(8,128)(2,1)S(1)} collective-permute-done((bf16[4,96,1920]{2,1,0:T(8,128)(2,1)}, bf16[4,96,1920]{2,1,0:T(8,128)(2,1)S(1)}, u32[]{:S(2)}, u32[]{:S(2)}) %collective-permute-start.23) | collective-permute-done | bytes 1474592 | tf_op jit(solution)/shard_map/ppermute | solution.py:941
  225.7 5.6 %ffn_norm.1 = (f32[512,1536]{1,0:T(8,128)}, bf16[512,1536]{1,0:T(8,128)(2,1)}, bf16[512,128]{1,0:T(8,128)(2,1)}) custom-call(bf16[512,1536]{1,0:T(8,128)(2,1)} %broadcast_select_fusion.3.tok, bf16[512,1536]{1,0:T(8,128)(2,1)} %get-tuple-element.534.own, bf16[512,1536]{1,0:T(8,128)(2,1)} %collective-permute-done.22.other, f32[1,1536]{1,0:T(1,128)} %broadcast_in_dim.41.gain, ...), custom_call_target="tpu_custom_call" | custom-call | flops 1 | bytes 1 | tf_op jit(solution)/shard_map/ffn_norm/pallas_call | solution.py:334
  234.1 5.2 %collective-permute-done.25.refs_3_ = bf16[2,96,1920]{2,1,0:T(8,128)(2,1)} collective-permute-done((bf16[2,96,1920]{2,1,0:T(8,128)(2,1)S(1)}, bf16[2,96,1920]{2,1,0:T(8,128)(2,1)}, u32[]{:S(2)}, u32[]{:S(2)}) %collective-permute-start.25) | collective-permute-done | bytes 737312 | tf_op jit(solution)/shard_map/ppermute | solution.py:945
  239.7 9.9 %collective-permute-done.29.refs_8_ = bf16[2,96,1920]{2,1,0:T(8,128)(2,1)S(1)} collective-permute-done((bf16[2,96,1920]{2,1,0:T(8,128)(2,1)}, bf16[2,96,1920]{2,1,0:T(8,128)(2,1)S(1)}, u32[]{:S(2)}, u32[]{:S(2)}) %collective-permute-start.29) | collective-permute-done | bytes 737312 | tf_op jit(solution)/shard_map/ppermute | solution.py:941
  249.6 5.4 %collective-permute-done.31.refs_13_ = bf16[2,96,1920]{2,1,0:T(8,128)(2,1)S(1)} collective-permute-done((bf16[2,96,1920]{2,1,0:T(8,128)(2,1)S(1)}, bf16[2,96,1920]{2,1,0:T(8,128)(2,1)S(1)}, u32[]{:S(2)}, u32[]{:S(2)}) %collective-permute-start.31) | collective-permute-done | bytes 737312 | tf_op jit(solution)/shard_map/ppermute | solution.py:945
  256.1 36.0 %ffn_both.1 = (bf16[512,1536]{1,0:T(8,128)(2,1)}, bf16[512,1536]{1,0:T(8,128)(2,1)}, bf16[2,48,768]{2,1,0:T(8,128)(2,1)}, bf16[16,1920]{1,0:T(8,128)(2,1)}, bf16...) custom-call(s32[16]{0:T(128)} %get-tuple-element.686.offs.offs_a, s32[16]{0:T(128)} %get-tuple-element.558.offs_b, ...), custom_call_target="tpu_custom_call" | custom-call | flops 1 | bytes 1 | tf_op jit(solution)/shard_map/ffn_both/pallas_call | solution.py:424
  302.2 9.9 %out_proj_back.1 = (f32[512,1536]{1,0:T(8,128)}, bf16[512,768]{1,0:T(8,128)(2,1)}, f32[16,512]{1,0:T(8,128)}, bf16[2,16,768]{2,1,0:T(8,128)(2,1)}, bf16[16,768]{1,0:T(8,128)(2,1)}) custom-call(s32[16]{0:T(128)} %add.145.offs, bf16[512,1536]{1,0:T(8,128)(2,1)} %broadcast_select_fusion.2.og, f32[512,1536]{1,0:T(8,128)} %get-tuple-element.669.resid, ...), custom_call_target="tpu_custom_call" | custom-call | flops 1 | bytes 1 | tf_op jit(solution)/shard_map/out_proj_back/pallas_call | solution.py:485
  323.8 14.1 %attend_back.2 = (f32[512,384]{1,0:T(8,128)}, bf16[2,512,128]{2,1,0:T(8,128)(2,1)}, bf16[2,512,128]{2,1,0:T(8,128)(2,1)}, f32[2,512,128]{2,1,0:T(8,128)}) custom-call(bf16[512,768]{1,0:T(8,128)(2,1)} %get-tuple-element.642.q, bf16[512,768]{1,0:T(8,128)(2,1)} %get-tuple-element.643.do, f32[16,512]{1,0:T(8,128)} %get-tuple-element.644.lse, ...), custom_call_target="tpu_custom_call" | custom-call | flops 1 | bytes 1 | tf_op jit(solution)/shard_map/attend_back/pallas_call | solution.py:260
  341.8 14.1 %attend_back.3 = (f32[512,384]{1,0:T(8,128)}, bf16[2,512,128]{2,1,0:T(8,128)(2,1)}, bf16[2,512,128]{2,1,0:T(8,128)(2,1)}, f32[2,512,128]{2,1,0:T(8,128)}) custom-call(bf16[512,768]{1,0:T(8,128)(2,1)} %get-tuple-element.642.q, bf16[512,768]{1,0:T(8,128)(2,1)} %get-tuple-element.643.do, f32[16,512]{1,0:T(8,128)} %get-tuple-element.644.lse, ...), custom_call_target="tpu_custom_call" | custom-call | flops 1 | bytes 1 | tf_op jit(solution)/shard_map/attend_back/pallas_call | solution.py:260
  358.6 8.6 %q_back.1 = (f32[512,1536]{1,0:T(8,128)}, bf16[16,1536]{1,0:T(8,128)(2,1)}, bf16[16,768]{1,0:T(8,128)(2,1)}) custom-call(s32[16]{0:T(128)} %get-tuple-element.686.offs.offs_a, f32[512,384]{1,0:T(8,128)} %get-tuple-element.654.dq0, f32[512,384]{1,0:T(8,128)} %get-tuple-element.655.dq1, f32[512,128]{1,0:T(8,128)} %get-tuple-element.695.cos, ...), custom_call_target="tpu_custom_call" | custom-call | flops 1 | bytes 1 | tf_op jit(solution)/shard_map/q_back/pallas_call | solution.py:531
  369.9 3.8 by_adapter.2
  374.6 7.7 %kv_back.1 = (bf16[512,1536]{1,0:T(8,128)(2,1)}, bf16[2,64,768]{2,1,0:T(8,128)(2,1)}, bf16[16,512]{1,0:T(8,128)(2,1)}) custom-call(s32[16]{0:T(128)} %get-tuple-element.686.offs.offs_a, f32[512,1536]{1,0:T(8,128)} %get-tuple-element.687.qpart, bf16[16,1536]{1,0:T(8,128)(2,1)} %get-tuple-element.688.q_in, f32[2,512,128]{2,1,0:T(8,128)} %get-tuple-element.689.da0, ...), custom_call_target="tpu_custom_call" | custom-call | flops 1 | bytes 1 | tf_op jit(solution)/shard_map/kv_back/pallas_call | solution.py:581
  393.8 5.7 %token_grad.1 = bf16[512,1536]{1,0:T(8,128)(2,1)} custom-call(bf16[512,1536]{1,0:T(8,128)(2,1)} %broadcast_select_fusion.3.tok, f32[512,1536]{1,0:T(8,128)} %get-tuple-element.723.rg, bf16[512,1536]{1,0:T(8,128)(2,1)} %get-tuple-element.724.own, bf16[512,1536]{1,0:T(8,128)(2,1)} %copy-done.14, f32[1,1536]{1,0:T(1,128)} %broadcast_in_dim.40.gain), custom_call_target="tpu_custom_call" | custom-call | flops 1 | bytes 1 | tf_op jit(solution)/shard_map/token_grad/pallas_call | solution.py:606
  404.7 4.4 collective-permute-start.49
  419.0 7.4 %collective-permute-done.54 = bf16[16,1408]{1,0:T(8,128)(2,1)S(1)} collective-permute-done((bf16[16,1408]{1,0:T(8,128)(2,1)}, bf16[16,1408]{1,0:T(8,128)(2,1)S(1)}, u32[]{:S(2)}, u32[]{:S(2)}) %collective-permute-start.54) | collective-permute-done | bytes 45088 | tf_op jit(solution)/shard_map/ppermute | solution.py:945
  435.4 4.0 collective-permute-done.57.refs_2_
  443.8 4.7 collective-permute-start.61
  451.1 5.6 %unpack_early.1 = (f32[8,16,1536]{2,1,0:T(8,128)}, f32[8,16,1536]{2,1,0:T(8,128)}, f32[8,16,1536]{2,1,0:T(8,128)}, f32[8,16,3840]{2,1,0:T(8,128)}, f32[8,16,3840]{2,1,0:T(8,128)}, /*index=5*/f32[8,16,3840]{2,1,0:T(8,128)}) custom-call(bf16[8,8,16,2048]{3,2,1,0:T(8,128)(2,1)} %bitcast.38), custom_call_target="tpu_custom_call" | custom-call | flops 1 | bytes 1 | tf_op jit(solution)/shard_map/unpack_early/pallas_call | solution.py:892
  456.7 8.4 %collective-permute-done.60.refs_2_ = bf16[8,16,1280]{2,1,0:T(8,128)(2,1)S(1)} collective-permute-done((bf16[8,16,1280]{2,1,0:T(8,128)(2,1)}, bf16[8,16,1280]{2,1,0:T(8,128)(2,1)S(1)}, u32[]{:S(2)}, u32[]{:S(2)}) %collective-permute-start.60) | collective-permute-done | bytes 327712 | tf_op jit(solution)/shard_map/ppermute | solution.py:951
  471.2 4.8 unpack_late.1
  (300 shorter events, 164.1 us)
Async XLA Ops:
  7.2 69.1 %all-gather.13.cloned.1.call-start = ((), (), s32[]{:S(2)}) async-start(), calls=%async_computation.2 | async-start | bytes 1843200 | tf_op jit(solution)/shard_map/all_gather | solution.py:1086
  44.3 92.7 %all-gather.15.cloned.1.call-start = ((), (), s32[]{:S(2)}) async-start(), calls=%async_computation.3 | async-start | bytes 1843200 | tf_op jit(solution)/shard_map/all_gather | solution.py:1126
  60.7 116.9 %all-gather.9.cloned.1.call-start = ((), (), s32[]{:S(2)}) async-start(), calls=%async_computation | async-start | bytes 2949120 | tf_op jit(solution)/shard_map/all_gather | solution.py:1134
  60.9 30.2 %collective-permute-start.9 = (bf16[4,96,1280]{2,1,0:T(8,128)(2,1)S(1)}, bf16[4,96,1280]{2,1,0:T(8,128)(2,1)S(1)}, u32[]{:S(2)}, u32[]{:S(2)}) collective-permute-start(bf16[4,96,1280]{2,1,0:T(8,128)(2,1)S(1)} %copy-done), channel_id=1, source_target_pairs={{0,12},{4,0},{8,4},{12,8},{1,13},{5,1},{9,5},{13,9},{2,14},{6,2},{... | collective-permute-start | bytes 2949128 | tf_op jit(solution)/shard_map/ppermute | solution.py:941
  63.4 28.6 %collective-permute-start.8 = (bf16[4,96,1280]{2,1,0:T(8,128)(2,1)S(1)}, bf16[4,96,1280]{2,1,0:T(8,128)(2,1)S(1)}, u32[]{:S(2)}, u32[]{:S(2)}) collective-permute-start(bf16[4,96,1280]{2,1,0:T(8,128)(2,1)S(1)} %copy-done), channel_id=1, source_target_pairs={{0,4},{4,8},{8,12},{12,0},{1,5},{5,9},{9,13},{13,1},{2,6},{6,10},{... | collective-permute-start | bytes 2949128 | tf_op jit(solution)/shard_map/ppermute | solution.py:941
  63.4 28.7 %collective-permute-start.17 = (bf16[96,2688]{1,0:T(8,128)(2,1)S(1)}, bf16[96,2688]{1,0:T(8,128)(2,1)}, u32[]{:S(2)}, u32[]{:S(2)}) collective-permute-start(bf16[96,2688]{1,0:T(8,128)(2,1)S(1)} %broadcast_select_fusion.4.refs_0_), channel_id=1, source_target_pairs={{0,2},{16,18},{2,0},{18,16},{1,3},{17,19},{3,1},{19,17},{4,6},{20,... | collective-permute-start | bytes 1548296 | tf_op jit(solution)/shard_map/ppermute | solution.py:945
  65.7 26.3 %collective-permute-start.16 = (bf16[96,2688]{1,0:T(8,128)(2,1)S(1)}, bf16[96,2688]{1,0:T(8,128)(2,1)}, u32[]{:S(2)}, u32[]{:S(2)}) collective-permute-start(bf16[96,2688]{1,0:T(8,128)(2,1)S(1)} %broadcast_select_fusion.4.refs_0_), channel_id=1, source_target_pairs={{0,18},{16,0},{2,16},{18,2},{1,19},{17,1},{3,17},{19,3},{4,22},{20... | collective-permute-start | bytes 1548296 | tf_op jit(solution)/shard_map/ppermute | solution.py:945
  65.8 26.3 %collective-permute-start.15 = (bf16[96,2688]{1,0:T(8,128)(2,1)S(1)}, bf16[96,2688]{1,0:T(8,128)(2,1)}, u32[]{:S(2)}, u32[]{:S(2)}) collective-permute-start(bf16[96,2688]{1,0:T(8,128)(2,1)S(1)} %broadcast_select_fusion.4.refs_0_), channel_id=1, source_target_pairs={{0,16},{16,2},{2,18},{18,0},{1,17},{17,3},{3,19},{19,1},{4,20},{20... | collective-permute-start | bytes 1548296 | tf_op jit(solution)/shard_map/ppermute | solution.py:945
  95.4 274.5 %all-gather.11.cloned.1.call-start = ((), (), s32[]{:S(2)}) async-start(), calls=%async_computation.1 | async-start | bytes 1392640 | tf_op jit(solution)/shard_map/all_gather | solution.py:1188
  95.4 40.3 %collective-permute-start.21 = (bf16[4,96,1920]{2,1,0:T(8,128)(2,1)}, bf16[4,96,1920]{2,1,0:T(8,128)(2,1)}, u32[]{:S(2)}, u32[]{:S(2)}) collective-permute-start(bf16[4,96,1920]{2,1,0:T(8,128)(2,1)} %bitcast.45), channel_id=1, source_target_pairs={{0,18},{16,0},{2,16},{18,2},{1,19},{17,1},{3,17},{19,3},{4,22},{20... | collective-permute-start | bytes 4423688 | tf_op jit(solution)/shard_map/ppermute | solution.py:945
  98.1 37.7 %collective-permute-start.20 = (bf16[4,96,1920]{2,1,0:T(8,128)(2,1)}, bf16[4,96,1920]{2,1,0:T(8,128)(2,1)}, u32[]{:S(2)}, u32[]{:S(2)}) collective-permute-start(bf16[4,96,1920]{2,1,0:T(8,128)(2,1)} %bitcast.46), channel_id=1, source_target_pairs={{0,16},{16,2},{2,18},{18,0},{1,17},{17,3},{3,19},{19,1},{4,20},{20... | collective-permute-start | bytes 4423688 | tf_op jit(solution)/shard_map/ppermute | solution.py:945
  98.1 18.2 %collective-permute-start.13 = (bf16[2,96,1280]{2,1,0:T(8,128)(2,1)S(1)}, bf16[2,96,1280]{2,1,0:T(8,128)(2,1)S(1)}, u32[]{:S(2)}, u32[]{:S(2)}) collective-permute-start(bf16[2,96,1280]{2,1,0:T(8,128)(2,1)S(1)} %slice.35), channel_id=1, source_target_pairs={{0,4},{4,8},{8,12},{12,0},{1,5},{5,9},{9,13},{13,1},{2,6},{6,10},{... | collective-permute-start | bytes 1474568 | tf_op jit(solution)/shard_map/ppermute | solution.py:941
  98.8 17.5 %collective-permute-start.14 = (bf16[2,96,1280]{2,1,0:T(8,128)(2,1)S(1)}, bf16[2,96,1280]{2,1,0:T(8,128)(2,1)S(1)}, u32[]{:S(2)}, u32[]{:S(2)}) collective-permute-start(bf16[2,96,1280]{2,1,0:T(8,128)(2,1)S(1)} %slice.36), channel_id=1, source_target_pairs={{0,12},{4,0},{8,4},{12,8},{1,13},{5,1},{9,5},{13,9},{2,14},{6,2},{... | collective-permute-start | bytes 1474568 | tf_op jit(solution)/shard_map/ppermute | solution.py:941
  125.5 64.4 %collective-permute-start.24 = (bf16[4,96,1920]{2,1,0:T(8,128)(2,1)}, bf16[4,96,1920]{2,1,0:T(8,128)(2,1)S(1)}, u32[]{:S(2)}, u32[]{:S(2)}) collective-permute-start(bf16[4,96,1920]{2,1,0:T(8,128)(2,1)} %get-tuple-element.573.refs_5_), channel_id=1, source_target_pairs={{0,12},{4,0},{8,4},{12,8},{1,13},{5,1},{9,5},{13,9},{2,14},{6,2},{... | collective-permute-start | bytes 4423688 | tf_op jit(solution)/shard_map/ppermute | solution.py:941
  131.7 21.5 %collective-permute-start.18 = (bf16[2,512,256]{2,1,0:T(8,128)(2,1)}, bf16[2,512,256]{2,1,0:T(8,128)(2,1)S(1)}, u32[]{:S(2)}, u32[]{:S(2)}) collective-permute-start(bf16[2,512,256]{2,1,0:T(8,128)(2,1)} %get-tuple-element.649.kv0), channel_id=1, source_target_pairs={{0,32},{32,64},{64,96},{1,33},{33,65},{65,97},{2,34},{34,66},{66,9... | collective-permute-start | bytes 1572872 | tf_op jit(solution)/shard_map/ppermute | solution.py:1140
  183.9 41.7 %collective-permute-start.22 = (bf16[512,1536]{1,0:T(8,128)(2,1)}, bf16[512,1536]{1,0:T(8,128)(2,1)}, u32[]{:S(2)}, u32[]{:S(2)}) collective-permute-start(bf16[512,1536]{1,0:T(8,128)(2,1)} %get-tuple-element.534.own), channel_id=1, source_target_pairs={{0,1},{1,0},{2,3},{3,2},{4,5},{5,4},{6,7},{7,6},{8,9},{9,8},{10,11... | collective-permute-start | bytes 4718600 | tf_op jit(solution)/shard_map/ppermute | solution.py:955
  186.2 35.4 %collective-permute-start.23 = (bf16[4,96,1920]{2,1,0:T(8,128)(2,1)}, bf16[4,96,1920]{2,1,0:T(8,128)(2,1)S(1)}, u32[]{:S(2)}, u32[]{:S(2)}) collective-permute-start(bf16[4,96,1920]{2,1,0:T(8,128)(2,1)} %get-tuple-element.573.refs_5_), channel_id=1, source_target_pairs={{0,4},{4,8},{8,12},{12,0},{1,5},{5,9},{9,13},{13,1},{2,6},{6,10},{... | collective-permute-start | bytes 4423688 | tf_op jit(solution)/shard_map/ppermute | solution.py:941
  186.4 44.9 %collective-permute-start.28 = (bf16[4,96,1920]{2,1,0:T(8,128)(2,1)}, bf16[4,96,1920]{2,1,0:T(8,128)(2,1)S(1)}, u32[]{:S(2)}, u32[]{:S(2)}) collective-permute-start(bf16[4,96,1920]{2,1,0:T(8,128)(2,1)} %bitcast.48), channel_id=1, source_target_pairs={{0,18},{16,0},{2,16},{18,2},{1,19},{17,1},{3,17},{19,3},{4,22},{20... | collective-permute-start | bytes 4423688 | tf_op jit(solution)/shard_map/ppermute | solution.py:945
  188.8 44.0 %collective-permute-start.27 = (bf16[4,96,1920]{2,1,0:T(8,128)(2,1)}, bf16[4,96,1920]{2,1,0:T(8,128)(2,1)}, u32[]{:S(2)}, u32[]{:S(2)}) collective-permute-start(bf16[4,96,1920]{2,1,0:T(8,128)(2,1)} %bitcast.49), channel_id=1, source_target_pairs={{0,16},{16,2},{2,18},{18,0},{1,17},{17,3},{3,19},{19,1},{4,20},{20... | collective-permute-start | bytes 4423688 | tf_op jit(solution)/shard_map/ppermute | solution.py:945
  190.0 49.3 %collective-permute-start.25 = (bf16[2,96,1920]{2,1,0:T(8,128)(2,1)S(1)}, bf16[2,96,1920]{2,1,0:T(8,128)(2,1)}, u32[]{:S(2)}, u32[]{:S(2)}) collective-permute-start(bf16[2,96,1920]{2,1,0:T(8,128)(2,1)S(1)} %slice.40), channel_id=1, source_target_pairs={{0,16},{16,2},{2,18},{18,0},{1,17},{17,3},{3,19},{19,1},{4,20},{20... | collective-permute-start | bytes 2211848 | tf_op jit(solution)/shard_map/ppermute | solution.py:945
  221.5 18.2 %collective-permute-start.26 = (bf16[2,96,1920]{2,1,0:T(8,128)(2,1)S(1)}, bf16[2,96,1920]{2,1,0:T(8,128)(2,1)}, u32[]{:S(2)}, u32[]{:S(2)}) collective-permute-start(bf16[2,96,1920]{2,1,0:T(8,128)(2,1)S(1)} %slice.38), channel_id=1, source_target_pairs={{0,18},{16,0},{2,16},{18,2},{1,19},{17,1},{3,17},{19,3},{4,22},{20... | collective-permute-start | bytes 2211848 | tf_op jit(solution)/shard_map/ppermute | solution.py:945
  225.6 23.9 %collective-permute-start.30 = (bf16[2,96,1920]{2,1,0:T(8,128)(2,1)}, bf16[2,96,1920]{2,1,0:T(8,128)(2,1)}, u32[]{:S(2)}, u32[]{:S(2)}) collective-permute-start(bf16[2,96,1920]{2,1,0:T(8,128)(2,1)} %slice.39), channel_id=1, source_target_pairs={{0,12},{4,0},{8,4},{12,8},{1,13},{5,1},{9,5},{13,9},{2,14},{6,2},{... | collective-permute-start | bytes 2211848 | tf_op jit(solution)/shard_map/ppermute | solution.py:941
  231.3 18.3 %collective-permute-start.29 = (bf16[2,96,1920]{2,1,0:T(8,128)(2,1)}, bf16[2,96,1920]{2,1,0:T(8,128)(2,1)S(1)}, u32[]{:S(2)}, u32[]{:S(2)}) collective-permute-start(bf16[2,96,1920]{2,1,0:T(8,128)(2,1)} %slice.42), channel_id=1, source_target_pairs={{0,4},{4,8},{8,12},{12,0},{1,5},{5,9},{9,13},{13,1},{2,6},{6,10},{... | collective-permute-start | bytes 2211848 | tf_op jit(solution)/shard_map/ppermute | solution.py:941
  234.0 21.0 %collective-permute-start.31 = (bf16[2,96,1920]{2,1,0:T(8,128)(2,1)S(1)}, bf16[2,96,1920]{2,1,0:T(8,128)(2,1)S(1)}, u32[]{:S(2)}, u32[]{:S(2)}) collective-permute-start(bf16[2,96,1920]{2,1,0:T(8,128)(2,1)S(1)} %slice.43), channel_id=1, source_target_pairs={{0,16},{16,2},{2,18},{18,0},{1,17},{17,3},{3,19},{19,1},{4,20},{20... | collective-permute-start | bytes 2211848 | tf_op jit(solution)/shard_map/ppermute | solution.py:945
  312.1 55.1 %collective-permute-start.35 = (bf16[512,1536]{1,0:T(8,128)(2,1)S(1)}, bf16[512,1536]{1,0:T(8,128)(2,1)}, u32[]{:S(2)}, u32[]{:S(2)}) collective-permute-start(bf16[512,1536]{1,0:T(8,128)(2,1)S(1)} %copy-done.15), channel_id=1, source_target_pairs={{0,1},{1,0},{2,3},{3,2},{4,5},{5,4},{6,7},{7,6},{8,9},{9,8},{10,11... | collective-permute-start | bytes 4718600 | tf_op jit(solution)/shard_map/ppermute | solution.py:955
  338.7 111.6 %all-gather.17.cloned.1.call-start = ((), (), s32[]{:S(2)}) async-start(), calls=%async_computation.4 | async-start | bytes 4718592 | tf_op jit(solution)/shard_map/all_gather | solution.py:1201
  338.7 34.9 %collective-permute-start.43 = (bf16[2,512,128]{2,1,0:T(8,128)(2,1)}, bf16[2,512,128]{2,1,0:T(8,128)(2,1)S(1)}, u32[]{:S(2)}, u32[]{:S(2)}) collective-permute-start(bf16[2,512,128]{2,1,0:T(8,128)(2,1)} %get-tuple-element.674), channel_id=1, source_target_pairs={{32,0},{64,32},{96,64},{33,1},{65,33},{97,65},{34,2},{66,34},{98,6... | collective-permute-start | bytes 786440 | tf_op jit(solution)/shard_map/ppermute | solution.py:1007
  340.0 33.6 %collective-permute-start.44 = (bf16[2,512,128]{2,1,0:T(8,128)(2,1)}, bf16[2,512,128]{2,1,0:T(8,128)(2,1)S(1)}, u32[]{:S(2)}, u32[]{:S(2)}) collective-permute-start(bf16[2,512,128]{2,1,0:T(8,128)(2,1)} %get-tuple-element.675), channel_id=1, source_target_pairs={{64,0},{96,32},{65,1},{97,33},{66,2},{98,34},{67,3},{99,35},{68,4}... | collective-permute-start | bytes 786440 | tf_op jit(solution)/shard_map/ppermute | solution.py:1008
  355.8 17.9 %collective-permute-start.45 = (bf16[2,512,128]{2,1,0:T(8,128)(2,1)}, bf16[2,512,128]{2,1,0:T(8,128)(2,1)S(1)}, u32[]{:S(2)}, u32[]{:S(2)}) collective-permute-start(bf16[2,512,128]{2,1,0:T(8,128)(2,1)} %get-tuple-element.676), channel_id=1, source_target_pairs={{32,0},{64,32},{96,64},{33,1},{65,33},{97,65},{34,2},{66,34},{98,6... | collective-permute-start | bytes 786440 | tf_op jit(solution)/shard_map/ppermute | solution.py:1007
  384.5 46.1 %collective-permute-start.42 = (bf16[512,1536]{1,0:T(8,128)(2,1)S(1)}, bf16[512,1536]{1,0:T(8,128)(2,1)S(1)}, u32[]{:S(2)}, u32[]{:S(2)}) collective-permute-start(bf16[512,1536]{1,0:T(8,128)(2,1)S(1)} %add_convert_fusion), channel_id=1, source_target_pairs={{1,16},{16,1},{3,18},{18,3},{5,20},{20,5},{7,22},{22,7},{9,24},{24... | collective-permute-start | bytes 4718600 | tf_op jit(solution)/shard_map/ppermute | solution.py:959
  399.5 66.8 %collective-permute-start.55 = (bf16[512,1536]{1,0:T(8,128)(2,1)}, bf16[512,1536]{1,0:T(8,128)(2,1)}, u32[]{:S(2)}, u32[]{:S(2)}) collective-permute-start(bf16[512,1536]{1,0:T(8,128)(2,1)} %token_grad.1), channel_id=1, source_target_pairs={{1,16},{16,1},{3,18},{18,3},{5,20},{20,5},{7,22},{22,7},{9,24},{24... | collective-permute-start | bytes 4718600 | tf_op jit(solution)/shard_map/ppermute | solution.py:959
  450.3 19.3 %collective-permute-start.62 = (bf16[8,16,1280]{2,1,0:T(8,128)(2,1)}, bf16[8,16,1280]{2,1,0:T(8,128)(2,1)S(1)}, u32[]{:S(2)}, u32[]{:S(2)}) collective-permute-start(bf16[8,16,1280]{2,1,0:T(8,128)(2,1)} %by_adapter.3.refs_0_), channel_id=1, source_target_pairs={{0,1},{1,0},{2,3},{3,2},{4,5},{5,4},{6,7},{7,6},{8,9},{9,8},{10,11... | collective-permute-start | bytes 983048 | tf_op jit(solution)/shard_map/ppermute | solution.py:955
  (99 other events, 801.7 us)
Sparse Core Ops, SparseCore 0:
  44.4 31.8 all-gather.12
  78.6 30.9 all-gather.14
  111.8 50.4 all-gather.8
  338.8 26.2 all-gather.10
  373.9 39.5 all-gather.16
